TPU v7x, 256 devices: a whole 4x4x8 slice. The times are simulated.
256 devices in a mesh: band: 32 (over z_hi, y, core), grid: 8 (over x, z_lo).
Axes of the slice: x: 4, y: 4, z: 8 (z_hi: 4, z_lo: 2; z = z_hi * 2 + z_lo), core: 2. Of those that a mesh axis runs over, the one named last changes fastest.
Arguments:
- orbitals: float32 [32, 96, 9216], P('band', 'grid'), may hold values from -30 to 30
- energies: float32 [32], P('band'), may hold values from -2 to -0.5
- local_pot: float32 [96, 9216], P('grid', 'band'), may hold values from 0.5 to 2
- trial_pot: float32 [4, 96, 9216], P(None, 'grid', 'band'), may hold values from 0.2 to 1.5
Outputs:
- response: float32 [32, 4, 96, 9216], P('band', None, 'grid')
- residual: float32 [32, 4, 96, 9216], P('band', None, 'grid')
- direction: float32 [32, 4, 96, 9216], P('band', None, 'grid')
- density: float32 [4, 96, 9216], P(None, 'grid', 'band')
All inputs are finite; a program needn't handle non-finite values.
Results may differ from a plain program's by a relative error of at most 0.0003.
Values sent between devices are 32-bit elements; how exact they have to be, the bound alone decides.
No kernel may reach another device: no remote copies, remote signals or barrier semaphores. Data moves between devices by JAX's collectives and lax.ppermute only.
A program may use at most 192 MiB of HBM per device.

v0:
```python
import math

import jax
import jax.numpy as jnp
import numpy as np
from jax import lax
from jax.sharding import PartitionSpec as P

spacing = 0.49
highest = lax.Precision.HIGHEST


def signed_index(index, points):
    return jnp.where(index < points // 2, index, index - points)


def kinetic_weights(points, x_index, y_index, z_index):
    squares = (
        signed_index(x_index, points)[:, None, None] ** 2
        + signed_index(y_index, points)[None, :, None] ** 2
        + signed_index(z_index, points)[None, None, :] ** 2
    )
    prefactor = 0.5 * (2.0 * math.pi / (points * spacing)) ** 2
    return jnp.where(
        squares < (points // 4) ** 2, prefactor * squares.astype(jnp.float32), jnp.float32(0.0)
    )


def wave_tables(points, kept_waves):
    row_index = np.arange(points)[:, None]
    phases = row_index * kept_waves[None, :] % points
    angles = phases * (2.0 * np.pi / points)
    return (jnp.asarray(np.cos(angles), jnp.float32), jnp.asarray(np.sin(angles), jnp.float32))


def turn_pair(real_part, imag_part, cosine, sine, pattern, parity):
    real_c = jnp.einsum(pattern, real_part, cosine, precision=highest)
    real_s = jnp.einsum(pattern, real_part, sine, precision=highest)
    imag_c = jnp.einsum(pattern, imag_part, cosine, precision=highest)
    imag_s = jnp.einsum(pattern, imag_part, sine, precision=highest)
    return (real_c + parity * imag_s, imag_c - parity * real_s)


def kinetic_apply(field, points):
    kept_waves = np.arange(points)
    full_cos, full_sin = wave_tables(points, np.arange(points))
    kept_cos, kept_sin = wave_tables(points, kept_waves)
    fields = field.shape[0] * field.shape[1]
    volume = field.reshape(fields, field.shape[2], points, points)
    real_part = jnp.einsum("fxyz,zk->fxyk", volume, kept_cos, precision=highest)
    imag_part = -jnp.einsum("fxyz,zk->fxyk", volume, kept_sin, precision=highest)
    real_part, imag_part = turn_pair(real_part, imag_part, kept_cos, kept_sin, "fxyk,yj->fxjk", 1.0)
    stacked = jnp.stack([real_part, imag_part])
    slab_piece = lax.all_to_all(stacked, "grid", split_axis=3, concat_axis=2, tiled=True)
    columns = slab_piece.shape[3]
    offset = lax.axis_index("grid") * columns
    y_index = lax.dynamic_slice_in_dim(jnp.asarray(kept_waves, jnp.int32), offset, columns)
    z_index = jnp.asarray(kept_waves, jnp.int32)
    x_index = jnp.arange(points, dtype=jnp.int32)
    weights = kinetic_weights(points, x_index, y_index, z_index)
    wave_real, wave_imag = turn_pair(
        slab_piece[0], slab_piece[1], full_cos, full_sin, "fxjk,xi->fijk", 1.0
    )
    wave_real, wave_imag = turn_pair(
        wave_real * weights, wave_imag * weights, full_cos, full_sin, "fijk,xi->fxjk", -1.0
    )
    back = lax.all_to_all(
        jnp.stack([wave_real, wave_imag]), "grid", split_axis=2, concat_axis=3, tiled=True
    )
    real_part, imag_part = turn_pair(back[0], back[1], kept_cos, kept_sin, "fxjk,yj->fxyk", -1.0)
    spatial = jnp.einsum("fxyk,zk->fxyz", real_part, kept_cos, precision=highest) - jnp.einsum(
        "fxyk,zk->fxyz", imag_part, kept_sin, precision=highest
    )
    return (spatial / float(points**3)).reshape(field.shape)


def on_device(orbitals, energies, local_pot, trial_pot):
    points = orbitals.shape[1] * lax.axis_size("grid")
    portion = local_pot.shape[1]
    trial_all, local_all = (
        lax.all_gather(trial_pot, "band", axis=2, tiled=True),
        lax.all_gather(local_pot, "band", axis=1, tiled=True),
    )
    weighted = trial_all[None] * orbitals[:, None]
    correlation_part = jnp.sum(weighted * orbitals[:, None], axis=(2, 3))
    norm_part = jnp.sum(orbitals * orbitals, axis=(1, 2))
    correlation, norms = lax.psum((correlation_part, norm_part), "grid")
    source = -(weighted - orbitals[:, None] * (correlation / norms[:, None])[:, :, None, None])
    start_part = jnp.sum(source * source, axis=(2, 3))
    shifted = local_all[None, None] - energies[:, None, None, None]
    start_norm = lax.psum(start_part, "grid")
    image = kinetic_apply(source, points) + shifted * source
    curvature = lax.psum(jnp.sum(source * image, axis=(2, 3)), "grid")
    step_size = start_norm / curvature
    response = step_size[:, :, None, None] * source
    residual = source - step_size[:, :, None, None] * image
    new_norm = lax.psum(jnp.sum(residual * residual, axis=(2, 3)), "grid")
    direction = residual + (new_norm / start_norm)[:, :, None, None] * source
    prefactor = 4.0 / (orbitals.shape[0] * lax.axis_size("band"))
    partial_value = prefactor * jnp.sum(orbitals[:, None] * response, axis=0)
    summed = lax.psum(partial_value, "band")
    density = lax.dynamic_slice_in_dim(summed, lax.axis_index("band") * portion, portion, 2)
    return (response, residual, direction, density)


def solution(mesh):
    return jax.shard_map(
        on_device,
        mesh=mesh,
        in_specs=(P("band", "grid", None), P("band"), P("grid", "band"), P(None, "grid", "band")),
        out_specs=(
            P("band", None, "grid", None),
            P("band", None, "grid", None),
            P("band", None, "grid", None),
            P(None, "grid", "band"),
        ),
        check_vma=False,
    )
```

profile of v0, /device:TPU:1, one launch (start us, length us, event | category | flops | bytes accessed | tf_op | source)
XLA Modules:
  0.0 795.6 jit_solution(999367908625608091)
XLA Ops:
  7.2 0.0 all-gather.3.cloned.1.call-start
  7.2 2.0 copy.101
  9.2 1.1 copy.150
  10.4 1.5 multiply_reduce_fusion.4
  11.9 121.2 %all-gather.3.cloned.1.call-done = f32[4,12,9216]{1,0,2:T(4,128)} async-done(((f32[4,12,288]{1,0,2:T(4,128)}), f32[4,12,9216]{1,0,2:T(4,128)}) %all-gather.3.cloned.1.call-update) | async-done | bytes 1769488 | tf_op jit(solution)/shard_map/all_gather | solution.py:81
  133.1 14.0 %copy.102 = f32[4,12,9216]{2,0,1:T(4,128)S(1)} copy(f32[4,12,9216]{1,0,2:T(4,128)} %all-gather.3.cloned.1.call-done) | data formatting | bytes 3538944 | tf_op jit(solution)/shard_map/all_gather | solution.py:81
  147.1 1.0 multiply_reduce_fusion.3
  148.1 27.5 %all-reduce.1 = (f32[1,4]{1,0:T(1,128)S(1)}, f32[]{:T(128)}) all-reduce(f32[1,4]{1,0:T(1,128)S(1)} %bitcast.124, f32[]{:T(128)} %multiply_reduce_fusion.4), channel_id=1, replica_groups=mesh['band'=32,'grid'=8] {'grid'}, use_global_device_ids=true, to_apply=%region_1.0 | all-reduce | flops 5 | bytes 40 | tf_op jit(solution)/shard_map/psum | solution.py:87
  175.6 0.6 divide_bitcast_fusion
  176.3 2.2 multiply_reduce_fusion.2
  178.4 2.7 reshape.118
  181.2 7.1 fusion.10
  188.3 2.0 fusion.8
  190.3 2.0 fusion.34
  192.3 2.0 fusion.33
  194.4 4.4 subtract_bitcast_fusion.1
  198.7 3.9 add_bitcast_fusion.1
  202.6 2.8 pad_maximum_fusion
  205.4 6.9 copy.109
  212.3 4.6 all-to-all-start
  216.9 0.1 fusion.28
  217.0 0.1 broadcast_add_fusion
  217.1 0.2 fusion.26
  217.2 50.7 %all-to-all-done = f32[2,4,12,96,96]{4,1,2,0,3:T(4,128)} async-done(((f32[2,4,12,96,96]{4,1,2,0,3:T(4,128)}), f32[2,4,12,96,96]{4,1,2,0,3:T(4,128)}, u32[]{:S(2)}, u32[]{:S(2)}) %all-to-all-start) | async-done | bytes 3538976 | tf_op jit(solution)/shard_map/all_to_all | solution.py:54
  268.0 3.6 copy.110
  271.6 2.2 fusion.32
  273.9 1.6 copy.113
  275.5 4.4 copy.114
  279.9 5.2 fusion.37
  285.1 1.6 copy.111
  286.8 4.5 copy.112
  291.3 3.9 fusion.35
  295.2 2.1 bitcast_multiply_fusion
  297.4 2.0 fusion.38
  299.4 2.1 bitcast_multiply_fusion.1
  301.6 2.0 fusion.36
  303.6 2.3 subtract_bitcast_fusion
  306.0 2.1 add_bitcast_fusion
  308.1 2.6 pad_maximum_fusion.1
  310.7 6.9 copy.117
  317.6 6.9 all-to-all-start.1
  325.2 88.2 %all-gather = f32[32,288,12]{1,2,0:T(8,128)S(1)} all-gather(f32[1,288,12]{1,2,0:T(8,128)S(1)} %bitcast.120), channel_id=1, replica_groups=mesh['band'=32,'grid'=8] {'band'}, dimensions={0}, use_global_device_ids=true | all-gather | bytes 456192 | tf_op jit(solution)/shard_map/all_gather | solution.py:82
  413.4 0.2 copy_subtract_fusion
  413.6 0.3 reshape.124
  414.0 3.1 copy.118
  417.1 2.2 fusion.31
  419.4 1.7 copy.119
  421.0 4.3 copy.120
  425.3 5.2 fusion.42
  430.5 3.4 fusion.39
  434.0 1.6 copy.121
  435.6 4.6 copy.122
  440.2 3.9 fusion.41
  444.2 2.0 fusion.40
  446.2 4.0 fusion
  450.3 5.3 subtract_multiply_fusion
  455.5 3.8 reshape.127
  459.4 3.2 multiply_reduce_fusion.1
  462.6 19.0 %all-reduce = (f32[1,4]{1,0:T(1,128)S(1)}, f32[1,4]{1,0:T(1,128)S(1)}) all-reduce(f32[1,4]{1,0:T(1,128)S(1)} %bitcast.121, f32[1,4]{1,0:T(1,128)S(1)} %bitcast.123), channel_id=1, replica_groups=mesh['band'=32,'grid'=8] {'grid'}, use_global_device_ids=true, to_apply=%region_5.0 | all-reduce | flops 8 | bytes 64 | tf_op jit(solution)/shard_map/psum | solution.py:91
  481.5 5.3 multiply_reduce_fusion
  486.8 12.7 %psum.46 = f32[1,4]{1,0:T(1,128)S(1)} all-reduce(f32[1,4]{1,0:T(1,128)S(1)} %bitcast.122), channel_id=1, replica_groups=mesh['band'=32,'grid'=8] {'grid'}, use_global_device_ids=true, to_apply=%region_9.10 | all-reduce | flops 4 | bytes 32 | tf_op jit(solution)/shard_map/psum | solution.py:97
  499.6 1.7 add_bitcast_fusion.2
  501.3 285.7 %all-reduce.4.cloned.1.call-done = f32[4,12,9216]{2,0,1:T(4,128)} async-done(((f32[4,12,9216]{2,0,1:T(4,128)}), f32[4,12,9216]{2,0,1:T(4,128)}) %all-reduce.4.cloned.1.call-update) | async-done | bytes 1769488 | tf_op jit(solution)/shard_map/psum | solution.py:101
  787.0 1.6 constant_dynamic-slice_fusion
  (42 shorter events, 0.2 us)
Async XLA Ops:
  7.2 3.2 copy-start.15
  7.2 125.9 %all-gather.3.cloned.1.call-start = ((), (), s32[]{:S(2)}) async-start(), calls=%async_computation.2 | async-start | bytes 19464192 | tf_op jit(solution)/shard_map/all_gather | solution.py:81
  10.4 136.8 %copy-start.5 = (f32[1,12,9216]{2,1,0:T(8,128)}, f32[1,12,9216]{2,1,0:T(8,128)S(1)}, u32[]{:S(2)}) copy-start(f32[1,12,9216]{2,1,0:T(8,128)S(1)} %copy.150) | copy-start | bytes 1327108
  178.4 2.7 copy-start.13
  181.2 7.1 copy-start.4
  181.2 7.1 copy-start.14
  212.3 55.7 %all-to-all-start = ((f32[2,4,12,96,96]{4,1,2,0,3:T(4,128)}), f32[2,4,12,96,96]{4,1,2,0,3:T(4,128)}, u32[]{:S(2)}, u32[]{:S(2)}) async-start(f32[2,4,12,96,96]{4,1,2,0,3:T(4,128)} %copy.109), calls=%async_computation | async-start | bytes 9437184 | tf_op jit(solution)/shard_map/all_to_all | solution.py:54
  279.9 5.2 copy-start.10
  291.3 3.9 copy-start.3
  291.3 3.9 copy-start.11
  297.4 2.1 copy-start.2
  317.6 7.6 copy-start.16
  317.6 96.4 %all-to-all-start.1 = ((f32[2,4,96,12,96]{4,1,3,0,2:T(4,128)}), f32[2,4,96,12,96]{4,1,3,0,2:T(4,128)}, u32[]{:S(2)}, u32[]{:S(2)}) async-start(f32[2,4,96,12,96]{4,1,3,0,2:T(4,128)} %copy.117), calls=%async_computation.1 | async-start | bytes 9437184 | tf_op jit(solution)/shard_map/all_to_all | solution.py:67
  324.5 462.5 %all-reduce.4.cloned.1.call-start = ((), (), s32[]{:S(2)}) async-start(), calls=%async_computation.3 | async-start | bytes 3538944 | tf_op jit(solution)/shard_map/psum | solution.py:101
  425.3 5.2 copy-start
  430.5 3.4 copy-start.9
  440.2 3.9 copy-start.1
  444.1 2.1 copy-start.7
  446.2 4.0 copy-start.8
  459.4 22.2 %copy-start.6 = (f32[1,12,9216]{2,1,0:T(8,128)S(1)}, f32[1,12,9216]{2,1,0:T(8,128)}, u32[]{:S(2)}) copy-start(f32[1,12,9216]{2,1,0:T(8,128)} %copy-done.5) | copy-start | bytes 1327108
  486.8 12.7 %copy-start.12 = (f32[4,12,9216]{2,0,1:T(4,128)S(1)}, f32[4,12,9216]{2,0,1:T(4,128)}, u32[]{:S(2)}) copy-start(f32[4,12,9216]{2,0,1:T(4,128)} %get-tuple-element.9) | copy-start | bytes 5308420
Sparse Core Ops, SparseCore 0:
  11.1 121.9 all-gather.2
  499.7 287.2 all-reduce.3
where the time goes:
time: 809 us; the launch traced here: 796 us
  waiting for transfers between devices  458 us (57%)
  blocking collectives  147 us (18%)
  local copies, waits for them, and re-layouts  75.1 us (9%)
  matrix products  67.1 us (8%)
  other arithmetic  21.5 us (3%)
  between operations  15.3 us (2%)
  starting transfers between devices  11.6 us (1%)
    psum x1, waiting for transfers between devices, on_device(): summed = lax.psum(partial_value, 'band')  286 us
    all_gather x1, waiting for transfers between devices, on_device(): lax.all_gather(trial_pot, 'band', axis=2, tiled=True)  121 us
    all_gather x1, blocking collectives, on_device(): lax.all_gather(local_pot, 'band', axis=1, tiled=True)  88.2 us
    all_to_all x1, waiting for transfers between devices, kinetic_apply(): lax.all_to_all(stacked, 'grid', split_axis=3, concat_axis=2, tiled=True)  50.7 us
    psum x1, blocking collectives, on_device(): correlation, norms = lax.psum((correlation_part, norm_part), 'grid')  27.5 us
    psum x1, blocking collectives, on_device(): start_norm = lax.psum(start_part, 'grid')  19 us
  transfers between devices with their start and end apart: 4, of which 3 were waited for; matrix products, arithmetic and copies ran while one was open for 1% of the time, Pallas kernels for 0%

commit v1 on v0

v1 whole, which is shorter than its diff:
```python
import math

import jax
import jax.numpy as jnp
import ml_dtypes
import numpy as np
from jax import lax
from jax.experimental import pallas as pl
from jax.experimental.pallas import tpu as pltpu
from jax.sharding import PartitionSpec as P

points = 96
planes = 12
trials = 4
bands = 32
half = 24
groups = 8
rows = points * planes
chunk = rows // groups
spacing = 0.49
prefactor = 0.5 * (2.0 * math.pi / (points * spacing)) ** 2
f32 = jnp.float32
bf16 = jnp.bfloat16


def split_np(table):
    table = np.asarray(table, np.float32)
    high = table.astype(ml_dtypes.bfloat16)
    low = (table - high.astype(np.float32)).astype(ml_dtypes.bfloat16)
    return high, low


def angle(a, b):
    return (np.outer(a, b) % points) * (2.0 * np.pi / points)


def build_tables():
    grid = np.arange(points)
    signed = np.arange(2 * half) - half
    kz = np.arange(half)
    w1 = np.zeros((5 * 128, 256))
    az = angle(grid, kz)
    for p in range(5):
        w1[p * 128 : p * 128 + points, p * half : (p + 1) * half] = np.cos(az)
        w1[p * 128 : p * 128 + points, 128 + p * half : 128 + (p + 1) * half] = -np.sin(az)
    order = np.zeros(points, np.int64)
    part = np.zeros(points, np.int64)
    for jj in range(6):
        for c in range(2):
            for g in range(groups):
                order[(2 * jj + c) * 8 + g] = signed[6 * g + jj]
                part[(2 * jj + c) * 8 + g] = c
    ay = angle(order, grid)
    real = part[:, None] == 0
    g1 = np.concatenate(
        [np.where(real, np.cos(ay), -np.sin(ay)), np.where(real, np.sin(ay), np.cos(ay))], 1
    )
    g4 = np.concatenate(
        [np.where(real, np.cos(ay), -np.sin(ay)), np.where(real, np.sin(ay), np.cos(ay))], 1
    ).T
    ax = angle(signed, grid)
    cx, sx = np.cos(ax), np.sin(ax)
    g2 = np.block([[cx, sx], [-sx, cx]])
    g3 = np.block([[cx.T, -sx.T], [sx.T, cx.T]])
    w2 = np.zeros((256, 4 * 128))
    for p in range(4):
        w2[p * half : (p + 1) * half, p * 128 : p * 128 + points] = np.cos(az).T
        w2[128 + p * half : 128 + (p + 1) * half, p * 128 : p * 128 + points] = -np.sin(az).T
    return {"w1": split_np(w1), "g1": split_np(g1), "g2": split_np(g2), "g3": split_np(g3),
            "g4": split_np(g4), "w2": split_np(w2)}


def dot(a, b):
    return lax.dot_general(a, b, (((1,), (0,)), ((), ())), preferred_element_type=f32)


def split(value):
    high = value.astype(bf16)
    return high, (value - high.astype(f32)).astype(bf16)


def left_table(high, low, value):
    vh, vl = split(value)
    return dot(high, vh) + dot(high, vl) + dot(low, vh)


def right_table(vh, vl, high, low):
    return dot(vh, high) + dot(vl, high) + dot(vh, low)


def lane_of(shape):
    return lax.broadcasted_iota(jnp.int32, shape, 1)


def row_of(shape):
    return lax.broadcasted_iota(jnp.int32, shape, 0)


def total(value):
    return jnp.sum(jnp.sum(value, axis=0, keepdims=True), axis=1, keepdims=True)


def fold(value):
    return jnp.sum(value.reshape(value.shape[0] // 8, 8, 128), axis=0)


def tile_of(shape, entries):
    row, lane = row_of(shape), lane_of(shape)
    out = jnp.zeros(shape, f32)
    for r, l, value in entries:
        out = jnp.where((row == r) & (lane == l), value, out)
    return out


def spread(t0, t1, t2):
    lane = lane_of(t0.shape)
    c1 = pltpu.roll(jnp.where(lane >= 96, t0, t1), 32, 1)
    c2 = pltpu.roll(jnp.where(lane >= 64, t1, t2), 64, 1)
    return t0, c1, c2


def pack_kernel(trial_ref, local_ref, out_ref):
    lane = lane_of((planes, 128))
    fill = jnp.zeros((planes, 96), f32)

    def pieces(ref, *at):
        t2 = jnp.concatenate([ref[(*at, slice(None), slice(256, 288))], fill], axis=1)
        return spread(ref[(*at, slice(None), slice(0, 128))], ref[(*at, slice(None), slice(128, 256))], t2)

    last = pieces(trial_ref, 3)
    for q in range(3):
        mine = pieces(trial_ref, q)
        for i in range(3):
            tail = pltpu.roll(last[i], 96 - 32 * q, 1)
            out_ref[q * 36 + i * 12 : q * 36 + i * 12 + 12, :] = jnp.where(lane < 96, mine[i], tail)
    mine = pieces(local_ref)
    for i in range(3):
        out_ref[108 + i * 12 : 120 + i * 12, :] = jnp.where(lane < 96, mine[i], 0.0)


def unpack_last(b0, b1, b2):
    lane = lane_of(b0.shape)
    r0, r1, r2 = pltpu.roll(b0, 32, 1), pltpu.roll(b1, 64, 1), pltpu.roll(b2, 96, 1)
    return jnp.where(lane < 32, r0, jnp.where(lane < 64, r1, r2))


def orbital_kernel(o_ref, out_ref):
    lane = lane_of((planes, 128))
    for q in range(points // 4):
        t = [o_ref[0, :, 384 * q + 128 * i : 384 * q + 128 * i + 128] for i in range(3)]
        c = [*spread(*t), pltpu.roll(t[2], 96, 1)]
        for i in range(4):
            at = (4 * q + i) * planes
            out_ref[at : at + planes, :] = jnp.where(lane < 96, c[i], 0.0)


def forward_kernel(me_ref, t_ref, o_ref, w1h, w1l, g1h, g1l, field_ref, out_ref, stat_ref,
                   high, low, real, imag):
    me = me_ref[0]
    norm = jnp.zeros((36, 128), f32)
    corr = [jnp.zeros((36, 128), f32) for _ in range(trials)]
    for u in range(bands):
        d = u ^ me
        slot = ((d & 1) << 4) | (((d >> 1) & 3) << 2) | (d >> 3)
        blocks = [t_ref[slot, q * 36 : q * 36 + 36, :] for q in range(4)]
        fields = [*blocks[:3], unpack_last(*blocks[:3]), blocks[3]]
        here = slice(u * 36, u * 36 + 36)
        for p in range(5):
            field_ref[p, here, :] = fields[p]
        o = o_ref[here, :]
        square = o * o
        norm = norm + square
        for p in range(trials):
            corr[p] = corr[p] + fields[p] * square
    norm = total(norm)
    mean = [total(c) / norm for c in corr]

    size = 96

    def weigh(i, sums):
        at = pl.ds(pl.multiple_of(i * size, size), size)
        o = o_ref[at, :]
        out = []
        for p in range(trials):
            w = (field_ref[p, at, :] - mean[p]) * o
            high[at, p * 128 : p * 128 + 128], low[at, p * 128 : p * 128 + 128] = split(w)
            out.append(sums[p] + fold(w * w))
        high[at, 512:640], low[at, 512:640] = split(o)
        return tuple(out)

    second = lax.fori_loop(0, rows // size, weigh, tuple(jnp.zeros((8, 128), f32) for _ in range(trials)))
    second = [total(s) for s in second]
    stat_ref[...] = tile_of((8, 128), [(0, 0, norm)] + [(0, 1 + p, mean[p]) for p in range(trials)])

    big = 384

    def along_z(i, _):
        at = pl.ds(pl.multiple_of(i * big, big), big)
        a = right_table(high[at, :], low[at, :], w1h[...], w1l[...])
        real[at, :] = a[:, :128]
        imag[at, :] = a[:, 128:]
        return 0

    lax.fori_loop(0, rows // big, along_z, 0)

    row, lane = row_of((points, 128)), lane_of((points, 128))
    ride = jnp.where((row < 8) & (lane == 120), norm, 0.0)
    for p in range(trials):
        ride = jnp.where((row < 8) & (lane == 121 + p), mean[p], ride)
        ride = jnp.where((row >= 8) & (row < 16) & (lane == 120 + p), second[p], ride)
    for x in range(0, planes, 2):
        parts = [
            jnp.concatenate([ref[pl.ds(x + i, points, stride=planes), :] for i in range(2)], axis=1)
            for ref in (real, imag)
        ]
        y = left_table(g1h[...], g1l[...], jnp.concatenate(parts, axis=0))
        for i in range(2):
            mine = y[:, i * 128 : i * 128 + 128] + ride
            for r in range(12):
                out_ref[pl.ds((x + i) * 12 + r, groups, stride=chunk), :] = mine[8 * r : 8 * r + 8]


def local_kernel(energy_ref, field_ref, o_ref, stat_ref, out_ref):
    energy = energy_ref[0]
    mean = [stat_ref[0:1, 1 + p : 2 + p] for p in range(trials)]
    size = 96

    def step(i, sums):
        at = pl.ds(pl.multiple_of(i * size, size), size)
        o = o_ref[at, :]
        shift = (field_ref[4, at, :] - energy) * o
        out = [sums[0] + fold(shift * o)]
        for p in range(trials):
            w = (field_ref[p, at, :] - mean[p]) * o
            both = shift * (field_ref[p, at, :] - mean[p])
            out.append(sums[1 + p] + fold(both * o))
            out.append(sums[5 + p] + fold(both * w))
        return (out[0], *out[1::2], *out[2::2])

    sums = lax.fori_loop(0, rows // size, step, tuple(jnp.zeros((8, 128), f32) for _ in range(9)))
    out_ref[...] = tile_of((8, 128), [(0, n, total(s)) for n, s in enumerate(sums)])


def wave_kernel(place_ref, in_ref, stat_ref, sums_ref, g2h, g2l, g3h, g3l, out_ref, scal_ref):
    owner = place_ref[0]
    s0 = in_ref[pl.ds(0, points, stride=planes), :]
    s1 = in_ref[pl.ds(1, points, stride=planes), :]
    weight = s0[:, 120:121]
    whole = jnp.sum(weight, axis=0, keepdims=True)
    lane = lane_of((points, 128))
    coef = jnp.zeros((points, 128), f32)
    alpha, start = [], []
    for p in range(trials):
        mean = s0[:, 121 + p : 122 + p]
        a = jnp.sum(weight * mean, axis=0, keepdims=True) / whole
        off = a - mean
        spread_sum = jnp.sum(s1[:, 120 + p : 121 + p] + weight * off * off, axis=0, keepdims=True)
        alpha.append(a)
        start.append(spread_sum / planes)
        coef = jnp.where((lane >= p * half) & (lane < (p + 1) * half), off, coef)

    def source_of(r):
        d = in_ref[pl.ds(r, points, stride=planes), :]
        o = jnp.where((lane >= 96) & (lane < 120), d, 0.0)
        o = pltpu.roll(o, 32, 1)
        o = o + pltpu.roll(o, 24, 1)
        o = o + pltpu.roll(o, 48, 1)
        return jnp.where(lane < 96, coef * o - d, 0.0)

    wide = (2 * half, 128)
    m = row_of(wide) - half
    k = lane_of(wide)
    k = k - jnp.where(k >= 72, 72, jnp.where(k >= 48, 48, jnp.where(k >= 24, 24, 0)))
    doubled = jnp.where(k == 0, 1.0, 2.0) * (prefactor / float(points**3))
    energy = jnp.zeros((1, 128), f32)
    own = [jnp.where(lane_of((1, 128)) == 0, 0.0, 0.0)]
    for pair in (2, 1, 0):
        parts = [
            jnp.concatenate([source_of(2 * (2 * pair + i) + c) for i in range(2)], axis=1)
            for c in range(2)
        ]
        u = left_table(g2h[...], g2l[...], jnp.concatenate(parts, axis=0))
        weights = []
        for i in range(2):
            j = owner * 6 + (2 * pair + i) - half
            square = m * m + k * k + j * j
            weights.append(jnp.where(square < half * half, doubled * square.astype(f32), 0.0))
        w = jnp.concatenate(weights, axis=1)
        t = u * jnp.concatenate([w, w], axis=0)
        product = jnp.sum(u * t, axis=0, keepdims=True)
        energy = energy + product[:, :128] + product[:, 128:]
        e = left_table(g3h[...], g3l[...], t)
        if pair == 0:
            l1 = lane_of((1, 128))
            ride = jnp.zeros((1, 128), f32)
            entries = []
            for p in range(trials):
                kinetic = jnp.sum(jnp.where((l1 >= p * half) & (l1 < (p + 1) * half), energy, 0.0), axis=1, keepdims=True)
                off = alpha[p] - stat_ref[0:1, 1 + p : 2 + p]
                at_p = sums_ref[0:1, 5 + p : 6 + p] - 2.0 * off * sums_ref[0:1, 1 + p : 2 + p] + off * off * sums_ref[0:1, 0:1]
                ride = jnp.where(l1 == 96 + p, kinetic + at_p, ride)
                entries += [(0, p, alpha[p]), (0, 4 + p, start[p])]
            scal_ref[...] = tile_of((8, 128), entries)
            e = e + jnp.concatenate([ride, jnp.zeros((1, 128), f32)], axis=1)
        for i in range(2):
            for c in range(2):
                out_ref[pl.ds(2 * (2 * pair + i) + c, points, stride=planes), :] = (
                    e[c * points : (c + 1) * points, i * 128 : i * 128 + 128]
                )


def image_kernel(energy_ref, in_ref, scal_ref, field_ref, o_ref, g4h, g4l, w2h, w2l,
                 source_ref, residual_ref, norm_ref, coef_ref, real, imag):
    energy = energy_ref[0]
    shares = in_ref[pl.ds(0, groups, stride=chunk), :]
    curvature = jnp.sum(shares, axis=0, keepdims=True)
    alpha = [scal_ref[0:1, p : p + 1] for p in range(trials)]
    step = [scal_ref[0:1, 4 + p : 5 + p] / curvature[:, 96 + p : 97 + p] for p in range(trials)]
    coef = tile_of((8, 128), [(0, p, step[p]) for p in range(trials)] + [(0, 4 + p, alpha[p]) for p in range(trials)])
    for v in range(bands):
        coef_ref[v, :, :] = coef
    for x in range(0, planes, 2):
        b = jnp.concatenate(
            [
                jnp.concatenate(
                    [in_ref[pl.ds((x + i) * 12 + r, groups, stride=chunk), :] for r in range(12)], axis=0
                )
                for i in range(2)
            ],
            axis=1,
        )
        v = left_table(g4h[...], g4l[...], b)
        for i in range(2):
            real[pl.ds(x + i, points, stride=planes), :] = v[:points, i * 128 : i * 128 + 128]
            imag[pl.ds(x + i, points, stride=planes), :] = v[points:, i * 128 : i * 128 + 128]
    size = 96

    def back(i, sums):
        at = pl.ds(pl.multiple_of(i * size, size), size)
        vh, vl = split(jnp.concatenate([real[at, :], imag[at, :]], axis=1))
        kinetic = right_table(vh, vl, w2h[...], w2l[...])
        o = o_ref[at, :]
        shift = field_ref[4, at, :] - energy
        out = []
        for p in range(trials):
            source = (alpha[p] - field_ref[p, at, :]) * o
            image = kinetic[:, p * 128 : p * 128 + 128] + shift * source
            residual = source - step[p] * image
            source_ref[p, at, :] = source
            residual_ref[p, at, :] = residual
            out.append(sums[p] + fold(residual * residual))
        return tuple(out)

    sums = lax.fori_loop(0, rows // size, back, tuple(jnp.zeros((8, 128), f32) for _ in range(trials)))
    norms = tile_of((8, 128), [(0, p, total(s)) for p, s in enumerate(sums)])
    for g in range(groups):
        norm_ref[g, :, :] = norms


def flat_of(ref, q):
    c = [ref[0, (4 * q + i) * planes : (4 * q + i + 1) * planes, :] for i in range(4)]
    lane = lane_of((planes, 128))
    r1, r2, r3 = pltpu.roll(c[1], 96, 1), pltpu.roll(c[2], 64, 1), pltpu.roll(c[3], 32, 1)
    return jnp.where(lane < 96, c[0], r1), jnp.where(lane < 64, r1, r2), jnp.where(lane < 32, r2, r3)


def lane_value(tile, at):
    lane = lane_of((1, 128))
    return jnp.sum(jnp.where(lane == at, tile, 0.0), axis=1, keepdims=True)


def flat_kernel(coef_ref, source_ref, residual_ref, response_out, residual_out):
    step = lane_value(coef_ref[0, 0:1, :], pl.program_id(0))
    for q in range(points // 4):
        for i, (s, r) in enumerate(zip(flat_of(source_ref, q), flat_of(residual_ref, q))):
            at = slice(384 * q + 128 * i, 384 * q + 128 * i + 128)
            response_out[0, 0, :, at] = step * s
            residual_out[0, 0, :, at] = r


def direction_kernel(coef_ref, scal_ref, norm_ref, response_ref, residual_ref, out_ref):
    p = pl.program_id(0)
    step = lane_value(coef_ref[0, 0:1, :], p)
    start = lane_value(scal_ref[0:1, :], 4 + p)
    new = lane_value(jnp.sum(norm_ref[:, 0, :], axis=0, keepdims=True), p)
    ratio = new / start / step
    out_ref[...] = residual_ref[...] + ratio * response_ref[...]


def density_kernel(coef_ref, packed_ref, o_ref, out_ref):
    blocks = [packed_ref[q * 36 : q * 36 + 36, :] for q in range(3)]
    fields = [*blocks, unpack_last(*blocks)]
    sums = [jnp.zeros((36, 128), f32) for _ in range(trials)]
    for v in range(bands):
        square = o_ref[v, :, :]
        square = square * square
        for p in range(trials):
            step = coef_ref[v, 0:1, p : p + 1]
            alpha = coef_ref[v, 0:1, 4 + p : 5 + p]
            sums[p] = sums[p] + (step * (alpha - fields[p])) * square
    lane = lane_of((planes, 128))
    for p in range(trials):
        c = [sums[p][12 * i : 12 * i + 12] * (4.0 / bands) for i in range(3)]
        r1, r2 = pltpu.roll(c[1], 96, 1), pltpu.roll(c[2], 64, 1)
        out_ref[p, :, 0:128] = jnp.where(lane < 96, c[0], r1)
        out_ref[p, :, 128:256] = jnp.where(lane < 64, r1, r2)
        out_ref[p, :, 256:288] = r2[:, 0:32]


vmem = pl.BlockSpec(memory_space=pltpu.VMEM)
smem = pl.BlockSpec(memory_space=pltpu.SMEM)
params = pltpu.CompilerParams(vmem_limit_bytes=40 * 1024 * 1024)


def shape(*dims, dtype=f32):
    return jax.ShapeDtypeStruct(dims, dtype)


def call(kernel, ins, outs, scratch=(), name=None):
    return pl.pallas_call(
        kernel, out_shape=outs, in_specs=ins, out_specs=jax.tree.map(lambda _: vmem, outs),
        scratch_shapes=scratch, compiler_params=params, name=name,
    )


def pack(trial, local):
    return call(pack_kernel, [vmem] * 2, shape(144, 128), name="pack")(trial, local)


def orbital_rows(orbitals):
    return call(orbital_kernel, [vmem], shape(rows, 128), name="orbital_rows")(orbitals)


def forward(me, gathered, o, tables):
    return call(
        forward_kernel, [smem] + [vmem] * 6,
        (shape(5, rows, 128), shape(rows, 128), shape(8, 128)),
        [pltpu.VMEM((rows, 640), bf16), pltpu.VMEM((rows, 640), bf16),
         pltpu.VMEM((rows, 128), f32), pltpu.VMEM((rows, 128), f32)],
        name="forward",
    )(me, gathered, o, *tables["w1"], *tables["g1"])


def local_sums(energies, fields, o, stat):
    return call(local_kernel, [smem] + [vmem] * 3, shape(8, 128), name="local_sums")(energies, fields, o, stat)


def waves(place, arrived, stat, sums, tables):
    return call(
        wave_kernel, [smem] + [vmem] * 7, (shape(rows, 128), shape(8, 128)), name="waves"
    )(place, arrived, stat, sums, *tables["g2"], *tables["g3"])


def image(energies, arrived, scal, fields, o, tables):
    return call(
        image_kernel, [smem] + [vmem] * 8,
        (shape(trials, rows, 128), shape(trials, rows, 128), shape(groups, 8, 128), shape(bands, 8, 128)),
        [pltpu.VMEM((rows, 128), f32), pltpu.VMEM((rows, 128), f32)],
        name="image",
    )(energies, arrived, scal, fields, o, *tables["g4"], *tables["w2"])


def flat(coef, source, residual):
    small = pl.BlockSpec((bands, 8, 128), lambda p: (0, 0, 0))
    block = pl.BlockSpec((1, rows, 128), lambda p: (p, 0, 0))
    out = pl.BlockSpec((1, 1, planes, points * points), lambda p: (0, p, 0, 0))
    return pl.pallas_call(
        flat_kernel, grid=(trials,), in_specs=[small, block, block], out_specs=(out, out),
        out_shape=(shape(1, trials, planes, points * points),) * 2, compiler_params=params, name="flat",
    )(coef, source, residual)


def direct(coef, scal, norms, response, residual):
    out = pl.BlockSpec((1, 1, planes, points * points), lambda p: (0, p, 0, 0))
    return pl.pallas_call(
        direction_kernel, grid=(trials,),
        in_specs=[
            pl.BlockSpec((bands, 8, 128), lambda p: (0, 0, 0)),
            pl.BlockSpec((8, 128), lambda p: (0, 0)),
            pl.BlockSpec((groups, 8, 128), lambda p: (0, 0, 0)),
            out, out,
        ],
        out_specs=out, out_shape=shape(1, trials, planes, points * points),
        compiler_params=params, name="direction",
    )(coef, scal, norms, response, residual)


def density_of(coef, packed, o):
    return call(density_kernel, [vmem] * 3, shape(trials, planes, 288), name="density")(coef, packed, o)


def swapped(value, axis, size, mask):
    return lax.ppermute(value, axis, [(s, s ^ mask) for s in range(size)])


def gather_bands(packed):
    value = packed[None]
    for masks in ((8, 16, 24), (2, 4, 6), (1,)):
        value = jnp.concatenate([value] + [swapped(value, "band", bands, m) for m in masks], axis=0)
    return value


def on_device(orbitals, energies, local_pot, trial_pot):
    tables = {name: tuple(jnp.asarray(t) for t in pair) for name, pair in build_tables().items()}
    me = lax.axis_index("band").astype(jnp.int32).reshape(1)
    place = lax.axis_index("grid").astype(jnp.int32).reshape(1)
    packed = pack(trial_pot, local_pot)
    o = orbital_rows(orbitals)
    gathered = gather_bands(packed)
    o_bands = lax.all_to_all(o.reshape(bands, 36, 128), "band", 0, 0, tiled=True)
    fields, sent, stat = forward(me, gathered, o, tables)
    arrived = lax.all_to_all(sent.reshape(groups, chunk, 128), "grid", 0, 0, tiled=True).reshape(rows, 128)
    sums = local_sums(energies, fields, o, stat)
    back, scal = waves(place, arrived, stat, sums, tables)
    back = lax.all_to_all(back.reshape(groups, chunk, 128), "grid", 0, 0, tiled=True).reshape(rows, 128)
    source, residual, norms, coef = image(energies, back, scal, fields, o, tables)
    norms = lax.all_to_all(norms, "grid", 0, 0, tiled=True)
    coefs = lax.all_to_all(coef, "band", 0, 0, tiled=True)
    response, residual = flat(coef, source, residual)
    direction = direct(coef, scal, norms, response, residual)
    density = density_of(coefs, packed, o_bands)
    return response, residual, direction, density


def solution(mesh):
    return jax.shard_map(
        on_device,
        mesh=mesh,
        in_specs=(P("band", "grid", None), P("band"), P("grid", "band"), P(None, "grid", "band")),
        out_specs=(
            P("band", None, "grid", None),
            P("band", None, "grid", None),
            P("band", None, "grid", None),
            P(None, "grid", "band"),
        ),
        check_vma=False,
    )
```

time: 809 us -> 152 us (0.19); the launches traced: 796 us -> 151 us
  waiting for transfers between devices: 458 us -> 42.3 us
  blocking collectives: 147 us -> 8.35 us
  matrix products: 67.1 us -> 0 us
  local copies, waits for them, and re-layouts: 75.1 us -> 39.7 us
  starting transfers between devices: 11.6 us -> 41 us
  other arithmetic: 21.5 us -> 0.02 us
  Pallas kernels: 0 us -> 17.8 us
  between operations: 15.3 us -> 1.49 us
    psum x1 -> x0, waiting for transfers between devices: 286 us -> none  [on_device(): summed = lax.psum(partial_value, 'band')]
    all_gather x1 -> x0, waiting for transfers between devices: 121 us -> none  [on_device(): lax.all_gather(trial_pot, 'band', axis=2, tiled=True)]
    all_gather x1 -> x0, blocking collectives: 88.2 us -> none  [on_device(): lax.all_gather(local_pot, 'band', axis=1, tiled=True)]
    dot_general x20 -> x0, matrix products: 67.1 us -> none  [the longest x4 15.5 us: turn_pair(): imag_c = jnp.einsum(pattern, imag_part, cosine, precision=highest)]
    psum x3 -> x0, blocking collectives: 59.1 us -> none  [the longest x1 27.5 us: on_device(): correlation, norms = lax.psum((correlation_part, norm_part), 'grid')]
    unnamed x36 -> x66, local copies, waits for them, and re-layouts: 3.17 us -> 36.8 us
    all_to_all x2 -> x4, waiting for transfers between devices: 50.8 us -> 23.4 us  [the longest x1 8.14 us: on_device(): lax.all_to_all(back.reshape(groups, chunk, 128), 'grid', 0, 0, tiled=True)]
    ppermute x0 -> x7, waiting for transfers between devices: none -> 18.9 us  [swapped(): return lax.ppermute(value, axis, [(s, s ^ mask) for s in range(size)])]
  transfers between devices with their start and end apart: 4 -> 11, of which waited for: 3 -> 9; matrix products, arithmetic and copies ran while one was open for 1% -> 8% of each run, Pallas kernels for 0% -> 6%
where the time goes in v1:
time: 152 us; the launch traced here: 151 us
  waiting for transfers between devices  42.3 us (28%)
  starting transfers between devices  41 us (27%)
  local copies, waits for them, and re-layouts  39.7 us (26%)
  Pallas kernels  17.8 us (12%)
  blocking collectives  8.35 us (5%)
    unnamed x66, local copies, waits for them, and re-layouts  36.8 us
    ppermute x7, waiting for transfers between devices, swapped(): return lax.ppermute(value, axis, [(s, s ^ mask) for s in range(size)])  18.9 us
    ppermute x7, starting transfers between devices, swapped(): return lax.ppermute(value, axis, [(s, s ^ mask) for s in range(size)])  15.6 us
    all_to_all x1, starting transfers between devices, on_device(): lax.all_to_all(o.reshape(bands, 36, 128), 'band', 0, 0, tiled=True)  10.8 us
    all_to_all x1, blocking collectives, on_device(): norms = lax.all_to_all(norms, 'grid', 0, 0, tiled=True)  8.35 us
    all_to_all x1, waiting for transfers between devices, on_device(): lax.all_to_all(back.reshape(groups, chunk, 128), 'grid', 0, 0, tiled=True)  8.14 us
    all_to_all x1, waiting for transfers between devices, on_device(): lax.all_to_all(o.reshape(bands, 36, 128), 'band', 0, 0, tiled=True)  7.89 us
    all_to_all x1, waiting for transfers between devices, on_device(): lax.all_to_all(sent.reshape(groups, chunk, 128), 'grid', 0, 0, tiled=True)  7.39 us
  transfers between devices with their start and end apart: 11, of which 9 were waited for; matrix products, arithmetic and copies ran while one was open for 8% of the time, Pallas kernels for 6%

profile of v1, /device:TPU:1, one launch (start us, length us, event | category | flops | bytes accessed | tf_op | source)
XLA Modules:
  0.0 150.7 jit_solution(17910429008254162759)
XLA Ops:
  0.6 0.9 copy.26.trial_ref
  1.5 0.7 copy-done.25
  2.4 3.9 %collective-permute-start = (f32[1,144,128]{2,1,0:T(8,128)S(1)}, f32[1,144,128]{2,1,0:T(8,128)S(1)}, u32[]{:S(2)}, u32[]{:S(2)}) collective-permute-start(f32[1,144,128]{2,1,0:T(8,128)S(1)} %bitcast.9), channel_id=1, source_target_pairs={{0,64},{8,72},{16,80},{24,88},{32,96},{40,104},{48,112},{56,120},{... | collective-permute-start | bytes 221192 | tf_op jit(solution)/shard_map/ppermute | solution.py:493
  6.3 5.1 %collective-permute-start.1 = (f32[1,144,128]{2,1,0:T(8,128)S(1)}, f32[1,144,128]{2,1,0:T(8,128)S(1)}, u32[]{:S(2)}, u32[]{:S(2)}) collective-permute-start(f32[1,144,128]{2,1,0:T(8,128)S(1)} %bitcast.10), channel_id=1, source_target_pairs={{0,128},{8,136},{16,144},{24,152},{32,160},{40,168},{48,176},{56,1... | collective-permute-start | bytes 221192 | tf_op jit(solution)/shard_map/ppermute | solution.py:493
  11.5 0.6 constant_dynamic-update-slice_fusion.6
  12.1 2.5 %collective-permute-done.1 = f32[1,144,128]{2,1,0:T(8,128)S(1)} collective-permute-done((f32[1,144,128]{2,1,0:T(8,128)S(1)}, f32[1,144,128]{2,1,0:T(8,128)S(1)}, u32[]{:S(2)}, u32[]{:S(2)}) %collective-permute-start.1) | collective-permute-done | bytes 73760 | tf_op jit(solution)/shard_map/ppermute | solution.py:493
  14.6 2.9 %collective-permute-done.2 = f32[1,144,128]{2,1,0:T(8,128)S(1)} collective-permute-done((f32[1,144,128]{2,1,0:T(8,128)S(1)}, f32[1,144,128]{2,1,0:T(8,128)S(1)}, u32[]{:S(2)}, u32[]{:S(2)}) %collective-permute-start.2) | collective-permute-done | bytes 73760 | tf_op jit(solution)/shard_map/ppermute | solution.py:493
  17.5 1.4 collective-permute-start.3
  18.9 2.6 %collective-permute-start.4 = (f32[4,144,128]{2,1,0:T(8,128)S(1)}, f32[4,144,128]{2,1,0:T(8,128)S(1)}, u32[]{:S(2)}, u32[]{:S(2)}) collective-permute-start(f32[4,144,128]{2,1,0:T(8,128)S(1)} %pad_maximum_fusion), channel_id=1, source_target_pairs={{0,32},{8,40},{16,48},{24,56},{32,0},{40,8},{48,16},{56,24},{64,96... | collective-permute-start | bytes 884744 | tf_op jit(solution)/shard_map/ppermute | solution.py:493
  21.5 0.6 constant_dynamic-update-slice_fusion.5
  22.2 0.6 constant_dynamic-update-slice_fusion.4
  22.8 0.6 constant_dynamic-update-slice_fusion.3
  23.5 1.0 collective-permute-done.3
  24.4 0.8 constant_dynamic-update-slice_fusion.2
  25.2 8.1 %collective-permute-done.4 = f32[4,144,128]{2,1,0:T(8,128)S(1)} collective-permute-done((f32[4,144,128]{2,1,0:T(8,128)S(1)}, f32[4,144,128]{2,1,0:T(8,128)S(1)}, u32[]{:S(2)}, u32[]{:S(2)}) %collective-permute-start.4) | collective-permute-done | bytes 294944 | tf_op jit(solution)/shard_map/ppermute | solution.py:493
  33.3 0.8 constant_dynamic-update-slice_fusion.1
  34.0 1.9 %collective-permute-done.5 = f32[4,144,128]{2,1,0:T(8,128)S(1)} collective-permute-done((f32[4,144,128]{2,1,0:T(8,128)S(1)}, f32[4,144,128]{2,1,0:T(8,128)S(1)}, u32[]{:S(2)}, u32[]{:S(2)}) %collective-permute-start.5) | collective-permute-done | bytes 294944 | tf_op jit(solution)/shard_map/ppermute | solution.py:493
  36.0 0.8 constant_dynamic-update-slice_fusion
  36.7 2.5 %collective-permute-start.6 = (f32[16,144,128]{2,1,0:T(8,128)}, f32[16,144,128]{2,1,0:T(8,128)}, u32[]{:S(2)}, u32[]{:S(2)}) collective-permute-start(f32[16,144,128]{2,1,0:T(8,128)} %get-tuple-element.34), channel_id=1, source_target_pairs={{0,8},{8,0},{16,24},{24,16},{32,40},{40,32},{48,56},{56,48},{64,72... | collective-permute-start | bytes 3538952 | tf_op jit(solution)/shard_map/ppermute | solution.py:493
  39.6 2.5 %collective-permute-done.6 = f32[16,144,128]{2,1,0:T(8,128)} collective-permute-done((f32[16,144,128]{2,1,0:T(8,128)}, f32[16,144,128]{2,1,0:T(8,128)}, u32[]{:S(2)}, u32[]{:S(2)}) %collective-permute-start.6) | collective-permute-done | bytes 1179680 | tf_op jit(solution)/shard_map/ppermute | solution.py:493
  42.0 1.3 constant_dynamic-update-slice_fusion.7.t_ref
  43.4 1.4 copy-done
  44.8 1.7 %copy-done.1 = f32[32,144,128]{2,1,0:T(8,128)S(1)} copy-done((f32[32,144,128]{2,1,0:T(8,128)S(1)}, f32[32,144,128]{2,1,0:T(8,128)}, u32[]{:S(2)}) %copy-start.1) | copy-done | bytes 2359320
  46.5 1.0 copy-done.12
  47.4 1.0 copy-done.13
  48.4 0.8 copy-done.18
  49.2 0.8 copy-done.19
  50.0 4.0 %forward.1 = (f32[5,1152,128]{2,1,0:T(8,128)S(1)}, f32[1152,128]{1,0:T(8,128)S(1)}, f32[8,128]{1,0:T(8,128)S(1)}) custom-call(s32[1]{0:T(128)} %bitcast.1.me_ref, f32[32,144,128]{2,1,0:T(8,128)S(1)} %copy-done.1, f32[1152,128]{1,0:T(8,128)S(1)} %orbital_rows.1.o_ref, bf16[640,256]{1,0:T(8,128)(2,1)S(1)} %copy-done.12, bf16[640,256]{1,0:T(8,128)(2,1)S(1)} %copy-done.13, ...), custom_call_target="tpu_custom_call" | custom-call | tf_op jit(solution)/shard_map/forward/pallas_call | solution.py:435
  54.0 0.8 copy-done.10
  54.8 4.2 %all-to-all-start = ((f32[8,144,128]{2,1,0:T(8,128)}), f32[8,144,128]{2,1,0:T(8,128)}, u32[]{:S(2)}, u32[]{:S(2)}) async-start(f32[8,144,128]{2,1,0:T(8,128)} %bitcast.13), calls=%async_computation | async-start | bytes 1179648 | tf_op jit(solution)/shard_map/all_to_all | solution.py:512
  59.7 2.0 %local_sums.1.sums_ref = f32[8,128]{1,0:T(8,128)S(1)} custom-call(f32[1]{0:T(128)S(6)} %copy.45.energy_ref, f32[5,1152,128]{2,1,0:T(8,128)S(1)} %get-tuple-element.17.field_ref, f32[1152,128]{1,0:T(8,128)S(1)} %orbital_rows.1.o_ref, f32[8,128]{1,0:T(8,128)S(1)} %get-tuple-element.16.stat_ref), custom_call_target="tpu_custom_call" | custom-call | tf_op jit(solution)/shard_map/local_sums/pallas_call | solution.py:445
  61.6 7.4 %all-to-all-done = f32[8,144,128]{2,1,0:T(8,128)} async-done(((f32[8,144,128]{2,1,0:T(8,128)}), f32[8,144,128]{2,1,0:T(8,128)}, u32[]{:S(2)}, u32[]{:S(2)}) %all-to-all-start) | async-done | bytes 589856 | tf_op jit(solution)/shard_map/all_to_all | solution.py:512
  69.0 0.8 copy-done.20
  69.8 0.8 copy-done.21
  70.6 0.8 copy-done.22
  71.4 0.8 copy-done.23
  72.2 2.3 %waves.1 = (f32[1152,128]{1,0:T(8,128)S(1)}, f32[8,128]{1,0:T(8,128)S(1)}) custom-call(s32[1]{0:T(128)} %bitcast.place_ref, f32[1152,128]{1,0:T(8,128)} %bitcast.4.in_ref, f32[8,128]{1,0:T(8,128)S(1)} %get-tuple-element.16.stat_ref, f32[8,128]{1,0:T(8,128)S(1)} %local_sums.1.sums_ref, bf16[96,192]{1,0:T(8,128)(2,1)S(1)} %copy-done.20, ...), custom_call_target="tpu_custom_call" | custom-call | tf_op jit(solution)/shard_map/waves/pallas_call | solution.py:449
  74.5 0.8 copy-done.11
  75.3 4.2 %all-to-all-start.1 = ((f32[8,144,128]{2,1,0:T(8,128)}), f32[8,144,128]{2,1,0:T(8,128)}, u32[]{:S(2)}, u32[]{:S(2)}) async-start(f32[8,144,128]{2,1,0:T(8,128)} %bitcast.14), calls=%async_computation.1 | async-start | bytes 1179648 | tf_op jit(solution)/shard_map/all_to_all | solution.py:515
  79.5 0.9 reshape.35
  80.4 8.1 %all-to-all-done.1 = f32[8,144,128]{2,1,0:T(8,128)} async-done(((f32[8,144,128]{2,1,0:T(8,128)}), f32[8,144,128]{2,1,0:T(8,128)}, u32[]{:S(2)}, u32[]{:S(2)}) %all-to-all-start.1) | async-done | bytes 589856 | tf_op jit(solution)/shard_map/all_to_all | solution.py:515
  88.6 10.8 %all-to-all-start.4 = ((f32[32,36,128]{2,1,0:T(8,128)}), f32[32,36,128]{2,1,0:T(8,128)}, u32[]{:S(2)}, u32[]{:S(2)}) async-start(f32[32,36,128]{2,1,0:T(8,128)} %reshape.35), calls=%async_computation.4 | async-start | bytes 1310720 | tf_op jit(solution)/shard_map/all_to_all | solution.py:510
  99.3 0.9 copy-done.14
  100.3 0.9 copy-done.15
  101.2 0.8 copy-done.16
  102.0 0.8 copy-done.17
  102.8 5.2 %image.1 = (f32[4,1152,128]{2,1,0:T(8,128)S(1)}, f32[4,1152,128]{2,1,0:T(8,128)S(1)}, f32[8,8,128]{2,1,0:T(8,128)S(1)}, f32[32,8,128]{2,1,0:T(8,128)S(1)}) custom-call(f32[1]{0:T(128)S(6)} %copy.45.energy_ref, f32[1152,128]{1,0:T(8,128)} %bitcast.6.in_ref, f32[8,128]{1,0:T(8,128)S(1)} %get-tuple-element.19.scal_ref, ...), custom_call_target="tpu_custom_call" | custom-call | tf_op jit(solution)/shard_map/image/pallas_call | solution.py:455
  108.1 1.4 copy-done.2
  109.5 1.4 copy-done.4
  110.9 0.7 copy-done.6
  111.6 0.6 copy-done.24
  112.2 7.9 %all-to-all-done.4.o_ref = f32[32,36,128]{2,1,0:T(8,128)} async-done(((f32[32,36,128]{2,1,0:T(8,128)}), f32[32,36,128]{2,1,0:T(8,128)}, u32[]{:S(2)}, u32[]{:S(2)}) %all-to-all-start.4) | async-done | bytes 589856 | tf_op jit(solution)/shard_map/all_to_all | solution.py:510
  120.1 8.4 %all_to_all.25.norm_ref = f32[8,8,128]{2,1,0:T(8,128)S(1)} all-to-all(f32[8,8,128]{2,1,0:T(8,128)} %copy-done.24), channel_id=1, replica_groups=mesh['band'=32,'grid'=8] {'grid'}, dimensions={0} | all-to-all | bytes 65536 | tf_op jit(solution)/shard_map/all_to_all | solution.py:517
  128.4 6.3 %all-to-all-start.3 = ((f32[32,8,128]{2,1,0:T(8,128)}), f32[32,8,128]{2,1,0:T(8,128)S(1)}, u32[]{:S(2)}, u32[]{:S(2)}) async-start(f32[32,8,128]{2,1,0:T(8,128)} %copy-done.6), calls=%async_computation.3 | async-start | bytes 262144 | tf_op jit(solution)/shard_map/all_to_all | solution.py:518
  134.8 1.7 %copy-done.3 = f32[4,1152,128]{2,1,0:T(8,128)S(1)} copy-done((f32[4,1152,128]{2,1,0:T(8,128)S(1)}, f32[4,1152,128]{2,1,0:T(8,128)}, u32[]{:S(2)}) %copy-start.3) | copy-done | bytes 2359320
  136.4 1.7 %copy-done.5 = f32[4,1152,128]{2,1,0:T(8,128)S(1)} copy-done((f32[4,1152,128]{2,1,0:T(8,128)S(1)}, f32[4,1152,128]{2,1,0:T(8,128)}, u32[]{:S(2)}) %copy-start.5) | copy-done | bytes 2359320
  138.1 0.9 copy-done.7
  139.0 1.5 %flat.1 = (f32[1,4,12,9216]{3,2,1,0:T(8,128)S(1)}, f32[1,4,12,9216]{3,2,1,0:T(8,128)S(1)}) custom-call(f32[32,8,128]{2,1,0:T(8,128)S(1)} %copy-done.7, f32[4,1152,128]{2,1,0:T(8,128)S(1)} %copy-done.3, f32[4,1152,128]{2,1,0:T(8,128)S(1)} %copy-done.5), custom_call_target="tpu_custom_call" | custom-call | tf_op jit(solution)/shard_map/flat/pallas_call | solution.py:467
  140.6 2.3 %copy.28 = f32[1,4,12,9216]{3,1,2,0:T(4,128)} copy(f32[1,4,12,9216]{3,2,1,0:T(8,128)S(1)} %get-tuple-element.30.response_ref) | data formatting | bytes 3538944
  142.9 2.3 %copy.29 = f32[1,4,12,9216]{3,1,2,0:T(4,128)} copy(f32[1,4,12,9216]{3,2,1,0:T(8,128)S(1)} %get-tuple-element.31.residual_ref) | data formatting | bytes 3538944
  145.2 0.7 direction.1
  146.0 2.3 %copy.30 = f32[1,4,12,9216]{3,1,2,0:T(4,128)} copy(f32[1,4,12,9216]{3,2,1,0:T(8,128)S(1)} %direction.1) | data formatting | bytes 3538944
  148.4 1.7 %density.1 = f32[4,12,288]{2,1,0:T(8,128)S(1)} custom-call(f32[32,8,128]{2,1,0:T(8,128)S(1)} %all-to-all-done.3.coef_ref, f32[144,128]{1,0:T(8,128)S(1)} %copy-done.9, f32[32,36,128]{2,1,0:T(8,128)} %all-to-all-done.4.o_ref), custom_call_target="tpu_custom_call" | custom-call | tf_op jit(solution)/shard_map/density/pallas_call | solution.py:489
  150.0 0.7 copy.31
  (38 shorter events, 0.6 us)
Async XLA Ops:
  1.5 0.7 copy-start.25
  2.3 37.0 %copy-start.26 = (f32[1,12,9216]{2,0,1:T(1,128)S(1)}, f32[1,12,9216]{2,0,1:T(1,128)}, u32[]{:S(2)}) copy-start(f32[1,12,9216]{2,0,1:T(1,128)} %param.16) | copy-start | bytes 1327108
  2.4 36.8 %copy-start.8 = (f32[144,128]{1,0:T(8,128)}, f32[144,128]{1,0:T(8,128)S(1)}, u32[]{:S(2)}) copy-start(f32[144,128]{1,0:T(8,128)S(1)} %pack.1.packed_ref) | copy-start | bytes 221188
  2.4 9.7 %collective-permute-start = (f32[1,144,128]{2,1,0:T(8,128)S(1)}, f32[1,144,128]{2,1,0:T(8,128)S(1)}, u32[]{:S(2)}, u32[]{:S(2)}) collective-permute-start(f32[1,144,128]{2,1,0:T(8,128)S(1)} %bitcast.9), channel_id=1, source_target_pairs={{0,64},{8,72},{16,80},{24,88},{32,96},{40,104},{48,112},{56,120},{... | collective-permute-start | bytes 221192 | tf_op jit(solution)/shard_map/ppermute | solution.py:493
  6.3 8.2 %collective-permute-start.1 = (f32[1,144,128]{2,1,0:T(8,128)S(1)}, f32[1,144,128]{2,1,0:T(8,128)S(1)}, u32[]{:S(2)}, u32[]{:S(2)}) collective-permute-start(f32[1,144,128]{2,1,0:T(8,128)S(1)} %bitcast.10), channel_id=1, source_target_pairs={{0,128},{8,136},{16,144},{24,152},{32,160},{40,168},{48,176},{56,1... | collective-permute-start | bytes 221192 | tf_op jit(solution)/shard_map/ppermute | solution.py:493
  11.5 6.0 %collective-permute-start.2 = (f32[1,144,128]{2,1,0:T(8,128)S(1)}, f32[1,144,128]{2,1,0:T(8,128)S(1)}, u32[]{:S(2)}, u32[]{:S(2)}) collective-permute-start(f32[1,144,128]{2,1,0:T(8,128)S(1)} %bitcast.11), channel_id=1, source_target_pairs={{0,192},{8,200},{16,208},{24,216},{32,224},{40,232},{48,240},{56,2... | collective-permute-start | bytes 221192 | tf_op jit(solution)/shard_map/ppermute | solution.py:493
  17.5 6.9 %collective-permute-start.3 = (f32[4,144,128]{2,1,0:T(8,128)S(1)}, f32[4,144,128]{2,1,0:T(8,128)S(1)}, u32[]{:S(2)}, u32[]{:S(2)}) collective-permute-start(f32[4,144,128]{2,1,0:T(8,128)S(1)} %pad_maximum_fusion), channel_id=1, source_target_pairs={{0,16},{8,24},{16,0},{24,8},{32,48},{40,56},{48,32},{56,40},{64,80... | collective-permute-start | bytes 884744 | tf_op jit(solution)/shard_map/ppermute | solution.py:493
  18.9 14.4 %collective-permute-start.4 = (f32[4,144,128]{2,1,0:T(8,128)S(1)}, f32[4,144,128]{2,1,0:T(8,128)S(1)}, u32[]{:S(2)}, u32[]{:S(2)}) collective-permute-start(f32[4,144,128]{2,1,0:T(8,128)S(1)} %pad_maximum_fusion), channel_id=1, source_target_pairs={{0,32},{8,40},{16,48},{24,56},{32,0},{40,8},{48,16},{56,24},{64,96... | collective-permute-start | bytes 884744 | tf_op jit(solution)/shard_map/ppermute | solution.py:493
  21.5 14.4 %collective-permute-start.5 = (f32[4,144,128]{2,1,0:T(8,128)S(1)}, f32[4,144,128]{2,1,0:T(8,128)S(1)}, u32[]{:S(2)}, u32[]{:S(2)}) collective-permute-start(f32[4,144,128]{2,1,0:T(8,128)S(1)} %pad_maximum_fusion), channel_id=1, source_target_pairs={{0,48},{8,56},{16,32},{24,40},{32,16},{40,24},{48,0},{56,8},{64,11... | collective-permute-start | bytes 884744 | tf_op jit(solution)/shard_map/ppermute | solution.py:493
  36.7 5.3 %collective-permute-start.6 = (f32[16,144,128]{2,1,0:T(8,128)}, f32[16,144,128]{2,1,0:T(8,128)}, u32[]{:S(2)}, u32[]{:S(2)}) collective-permute-start(f32[16,144,128]{2,1,0:T(8,128)} %get-tuple-element.34), channel_id=1, source_target_pairs={{0,8},{8,0},{16,24},{24,16},{32,40},{40,32},{48,56},{56,48},{64,72... | collective-permute-start | bytes 3538952 | tf_op jit(solution)/shard_map/ppermute | solution.py:493
  43.4 1.4 copy-start
  44.8 1.7 %copy-start.1 = (f32[32,144,128]{2,1,0:T(8,128)S(1)}, f32[32,144,128]{2,1,0:T(8,128)}, u32[]{:S(2)}) copy-start(f32[32,144,128]{2,1,0:T(8,128)} %copy-done) | copy-start | bytes 7077892
  46.5 1.0 copy-start.12
  47.4 1.0 copy-start.13
  48.4 0.8 copy-start.18
  49.2 0.8 copy-start.19
  54.0 0.8 copy-start.10
  54.8 14.2 %all-to-all-start = ((f32[8,144,128]{2,1,0:T(8,128)}), f32[8,144,128]{2,1,0:T(8,128)}, u32[]{:S(2)}, u32[]{:S(2)}) async-start(f32[8,144,128]{2,1,0:T(8,128)} %bitcast.13), calls=%async_computation | async-start | bytes 1179648 | tf_op jit(solution)/shard_map/all_to_all | solution.py:512
  69.0 0.8 copy-start.20
  69.8 0.8 copy-start.21
  70.6 0.8 copy-start.22
  71.4 0.8 copy-start.23
  74.5 0.8 copy-start.11
  75.3 13.2 %all-to-all-start.1 = ((f32[8,144,128]{2,1,0:T(8,128)}), f32[8,144,128]{2,1,0:T(8,128)}, u32[]{:S(2)}, u32[]{:S(2)}) async-start(f32[8,144,128]{2,1,0:T(8,128)} %bitcast.14), calls=%async_computation.1 | async-start | bytes 1179648 | tf_op jit(solution)/shard_map/all_to_all | solution.py:515
  88.6 31.5 %all-to-all-start.4 = ((f32[32,36,128]{2,1,0:T(8,128)}), f32[32,36,128]{2,1,0:T(8,128)}, u32[]{:S(2)}, u32[]{:S(2)}) async-start(f32[32,36,128]{2,1,0:T(8,128)} %reshape.35), calls=%async_computation.4 | async-start | bytes 1310720 | tf_op jit(solution)/shard_map/all_to_all | solution.py:510
  99.3 1.0 copy-start.14
  100.3 0.9 copy-start.15
  101.2 0.8 copy-start.16
  102.0 0.8 copy-start.17
  108.1 1.4 copy-start.2
  109.5 1.4 copy-start.4
  110.9 0.7 copy-start.6
  111.6 0.6 copy-start.24
  128.4 19.9 %all-to-all-start.3 = ((f32[32,8,128]{2,1,0:T(8,128)}), f32[32,8,128]{2,1,0:T(8,128)S(1)}, u32[]{:S(2)}, u32[]{:S(2)}) async-start(f32[32,8,128]{2,1,0:T(8,128)} %copy-done.6), calls=%async_computation.3 | async-start | bytes 262144 | tf_op jit(solution)/shard_map/all_to_all | solution.py:518
  134.8 1.7 %copy-start.3 = (f32[4,1152,128]{2,1,0:T(8,128)S(1)}, f32[4,1152,128]{2,1,0:T(8,128)}, u32[]{:S(2)}) copy-start(f32[4,1152,128]{2,1,0:T(8,128)} %copy-done.2) | copy-start | bytes 7077892
  136.4 1.7 %copy-start.5 = (f32[4,1152,128]{2,1,0:T(8,128)S(1)}, f32[4,1152,128]{2,1,0:T(8,128)}, u32[]{:S(2)}) copy-start(f32[4,1152,128]{2,1,0:T(8,128)} %copy-done.4) | copy-start | bytes 7077892
  138.1 0.9 copy-start.7
  146.0 2.4 %copy-start.9 = (f32[144,128]{1,0:T(8,128)S(1)}, f32[144,128]{1,0:T(8,128)}, u32[]{:S(2)}) copy-start(f32[144,128]{1,0:T(8,128)} %copy-done.8) | copy-start | bytes 221188

commit v2 on v1

--- a/solution.py
+++ b/solution.py
@@ -124,8 +124,8 @@
     fill = jnp.zeros((planes, 96), f32)
 
     def pieces(ref, *at):
-        t2 = jnp.concatenate([ref[(*at, slice(None), slice(256, 288))], fill], axis=1)
-        return spread(ref[(*at, slice(None), slice(0, 128))], ref[(*at, slice(None), slice(128, 256))], t2)
+        t2 = jnp.concatenate([ref[(slice(None), *at, slice(256, 288))], fill], axis=1)
+        return spread(ref[(slice(None), *at, slice(0, 128))], ref[(slice(None), *at, slice(128, 256))], t2)
 
     last = pieces(trial_ref, 3)
     for q in range(3):
@@ -241,7 +241,7 @@
     out_ref[...] = tile_of((8, 128), [(0, n, total(s)) for n, s in enumerate(sums)])
 
 
-def wave_kernel(place_ref, in_ref, stat_ref, sums_ref, g2h, g2l, g3h, g3l, out_ref, scal_ref):
+def wave_kernel(place_ref, in_ref, stat_ref, sums_ref, g2h, g2l, g3h, g3l, out_ref, scal_ref, coef_ref):
     owner = place_ref[0]
     s0 = in_ref[pl.ds(0, points, stride=planes), :]
     s1 = in_ref[pl.ds(1, points, stride=planes), :]
@@ -301,6 +301,10 @@
                 ride = jnp.where(l1 == 96 + p, kinetic + at_p, ride)
                 entries += [(0, p, alpha[p]), (0, 4 + p, start[p])]
             scal_ref[...] = tile_of((8, 128), entries)
+            mine = jnp.where(row_of((8, 128)) == 0, pltpu.roll(jnp.where(l1 < 100, ride, 0.0), 32, 1), 0.0)
+            mine = mine + pltpu.roll(tile_of((8, 128), entries), 4, 1)
+            for v in range(bands):
+                coef_ref[v, :, :] = mine
             e = e + jnp.concatenate([ride, jnp.zeros((1, 128), f32)], axis=1)
         for i in range(2):
             for c in range(2):
@@ -309,16 +313,26 @@
                 )
 
 
+def fold_bands(tile, at):
+    lane = lane_of((8, 128))
+    out = jnp.zeros((8, 128), f32)
+    for b in range(4):
+        part = jnp.where((lane >= at) & (lane < at + 4), tile[8 * b : 8 * b + 8], 0.0)
+        out = out + pltpu.roll(part, (16 * b - at) % 128, 1)
+    return out
+
+
 def image_kernel(energy_ref, in_ref, scal_ref, field_ref, o_ref, g4h, g4l, w2h, w2l,
-                 source_ref, residual_ref, norm_ref, coef_ref, real, imag):
+                 source_ref, residual_ref, norm_ref, step_ref, real, imag):
     energy = energy_ref[0]
     shares = in_ref[pl.ds(0, groups, stride=chunk), :]
     curvature = jnp.sum(shares, axis=0, keepdims=True)
     alpha = [scal_ref[0:1, p : p + 1] for p in range(trials)]
     step = [scal_ref[0:1, 4 + p : 5 + p] / curvature[:, 96 + p : 97 + p] for p in range(trials)]
-    coef = tile_of((8, 128), [(0, p, step[p]) for p in range(trials)] + [(0, 4 + p, alpha[p]) for p in range(trials)])
-    for v in range(bands):
-        coef_ref[v, :, :] = coef
+    step_ref[...] = tile_of(
+        (8, 128),
+        [(0, p, step[p]) for p in range(trials)] + [(0, 4 + p, scal_ref[0:1, 4 + p : 5 + p]) for p in range(trials)],
+    )
     for x in range(0, planes, 2):
         b = jnp.concatenate(
             [
@@ -346,22 +360,20 @@
             source = (alpha[p] - field_ref[p, at, :]) * o
             image = kinetic[:, p * 128 : p * 128 + 128] + shift * source
             residual = source - step[p] * image
-            source_ref[p, at, :] = source
-            residual_ref[p, at, :] = residual
+            there = pl.ds(i * (size * trials) + p, size, stride=trials)
+            source_ref[there, :] = source
+            residual_ref[there, :] = residual
             out.append(sums[p] + fold(residual * residual))
         return tuple(out)
 
     sums = lax.fori_loop(0, rows // size, back, tuple(jnp.zeros((8, 128), f32) for _ in range(trials)))
-    norms = tile_of((8, 128), [(0, p, total(s)) for p, s in enumerate(sums)])
+    norm_ref[...] = tile_of((8, 128), [(0, 64 + p, total(s)) for p, s in enumerate(sums)])
+
+
+def share_kernel(norm_ref, coef_ref, out_ref):
+    tile = norm_ref[...] + fold_bands(coef_ref[:, 0, :], 0)
     for g in range(groups):
-        norm_ref[g, :, :] = norms
-
-
-def flat_of(ref, q):
-    c = [ref[0, (4 * q + i) * planes : (4 * q + i + 1) * planes, :] for i in range(4)]
-    lane = lane_of((planes, 128))
-    r1, r2, r3 = pltpu.roll(c[1], 96, 1), pltpu.roll(c[2], 64, 1), pltpu.roll(c[3], 32, 1)
-    return jnp.where(lane < 96, c[0], r1), jnp.where(lane < 64, r1, r2), jnp.where(lane < 32, r2, r3)
+        out_ref[g, :, :] = tile
 
 
 def lane_value(tile, at):
@@ -369,25 +381,46 @@
     return jnp.sum(jnp.where(lane == at, tile, 0.0), axis=1, keepdims=True)
 
 
-def flat_kernel(coef_ref, source_ref, residual_ref, response_out, residual_out):
-    step = lane_value(coef_ref[0, 0:1, :], pl.program_id(0))
-    for q in range(points // 4):
-        for i, (s, r) in enumerate(zip(flat_of(source_ref, q), flat_of(residual_ref, q))):
+def per_trial(count, values):
+    r = row_of((count, 128)) & 3
+    out = jnp.zeros((count, 128), f32)
+    for p in range(trials):
+        out = jnp.where(r == p, values[p], out)
+    return out
+
+
+def flat_kernel(step_ref, source_ref, residual_ref, response_out, residual_out):
+    size = planes * trials
+    lane = lane_of((size, 128))
+    step = per_trial(size, [step_ref[0:1, p : p + 1] for p in range(trials)])
+
+    def tiles(ref, q):
+        c = [ref[(4 * q + i) * size : (4 * q + i + 1) * size, :] for i in range(4)]
+        r1, r2, r3 = pltpu.roll(c[1], 96, 1), pltpu.roll(c[2], 64, 1), pltpu.roll(c[3], 32, 1)
+        return jnp.where(lane < 96, c[0], r1), jnp.where(lane < 64, r1, r2), jnp.where(lane < 32, r2, r3)
+
+    for q in range(4):
+        for i, (s, r) in enumerate(zip(tiles(source_ref, q), tiles(residual_ref, q))):
             at = slice(384 * q + 128 * i, 384 * q + 128 * i + 128)
-            response_out[0, 0, :, at] = step * s
-            residual_out[0, 0, :, at] = r
-
-
-def direction_kernel(coef_ref, scal_ref, norm_ref, response_ref, residual_ref, out_ref):
-    p = pl.program_id(0)
-    step = lane_value(coef_ref[0, 0:1, :], p)
-    start = lane_value(scal_ref[0:1, :], 4 + p)
-    new = lane_value(jnp.sum(norm_ref[:, 0, :], axis=0, keepdims=True), p)
-    ratio = new / start / step
-    out_ref[...] = residual_ref[...] + ratio * response_ref[...]
-
-
-def density_kernel(coef_ref, packed_ref, o_ref, out_ref):
+            response_out[:, :, at] = (step * s).reshape(planes, trials, 128)
+            residual_out[:, :, at] = r.reshape(planes, trials, 128)
+
+
+def direction_kernel(step_ref, norm_ref, response_ref, residual_ref, out_ref):
+    new = jnp.sum(norm_ref[:, 0, :], axis=0, keepdims=True)
+    ratio = [
+        new[:, 64 + p : 65 + p] / step_ref[0:1, 4 + p : 5 + p] / step_ref[0:1, p : p + 1] for p in range(trials)
+    ]
+    ratio = per_trial(trials, ratio)[:, 0:1]
+    out_ref[...] = residual_ref[...] + ratio[None] * response_ref[...]
+
+
+def density_kernel(norm_ref, coef_ref, packed_ref, o_ref, out_ref):
+    curvature = norm_ref[0]
+    for g in range(1, groups):
+        curvature = curvature + norm_ref[g]
+    alphas = fold_bands(coef_ref[:, 0, :], 4)
+    steps = fold_bands(coef_ref[:, 0, :], 8) / jnp.where(curvature == 0.0, 1.0, curvature)
     blocks = [packed_ref[q * 36 : q * 36 + 36, :] for q in range(3)]
     fields = [*blocks, unpack_last(*blocks)]
     sums = [jnp.zeros((36, 128), f32) for _ in range(trials)]
@@ -395,36 +428,39 @@
         square = o_ref[v, :, :]
         square = square * square
         for p in range(trials):
-            step = coef_ref[v, 0:1, p : p + 1]
-            alpha = coef_ref[v, 0:1, 4 + p : 5 + p]
+            r, l = v % 8, 16 * (v // 8) + p
+            step, alpha = steps[r : r + 1, l : l + 1], alphas[r : r + 1, l : l + 1]
             sums[p] = sums[p] + (step * (alpha - fields[p])) * square
     lane = lane_of((planes, 128))
     for p in range(trials):
         c = [sums[p][12 * i : 12 * i + 12] * (4.0 / bands) for i in range(3)]
         r1, r2 = pltpu.roll(c[1], 96, 1), pltpu.roll(c[2], 64, 1)
-        out_ref[p, :, 0:128] = jnp.where(lane < 96, c[0], r1)
-        out_ref[p, :, 128:256] = jnp.where(lane < 64, r1, r2)
-        out_ref[p, :, 256:288] = r2[:, 0:32]
+        out_ref[:, p, 0:128] = jnp.where(lane < 96, c[0], r1)
+        out_ref[:, p, 128:256] = jnp.where(lane < 64, r1, r2)
+        out_ref[:, p, 256:288] = r2[:, 0:32]
 
 
 vmem = pl.BlockSpec(memory_space=pltpu.VMEM)
 smem = pl.BlockSpec(memory_space=pltpu.SMEM)
-params = pltpu.CompilerParams(vmem_limit_bytes=40 * 1024 * 1024)
+
+
+def params(mebibytes):
+    return pltpu.CompilerParams(vmem_limit_bytes=mebibytes * 1024 * 1024)
 
 
 def shape(*dims, dtype=f32):
     return jax.ShapeDtypeStruct(dims, dtype)
 
 
-def call(kernel, ins, outs, scratch=(), name=None):
+def call(kernel, ins, outs, scratch=(), name=None, room=4):
     return pl.pallas_call(
         kernel, out_shape=outs, in_specs=ins, out_specs=jax.tree.map(lambda _: vmem, outs),
-        scratch_shapes=scratch, compiler_params=params, name=name,
+        scratch_shapes=scratch, compiler_params=params(room), name=name,
     )
 
 
 def pack(trial, local):
-    return call(pack_kernel, [vmem] * 2, shape(144, 128), name="pack")(trial, local)
+    return call(pack_kernel, [vmem] * 2, shape(144, 128), name="pack")(jnp.transpose(trial, (1, 0, 2)), local)
 
 
 def orbital_rows(orbitals):
@@ -437,7 +473,7 @@
         (shape(5, rows, 128), shape(rows, 128), shape(8, 128)),
         [pltpu.VMEM((rows, 640), bf16), pltpu.VMEM((rows, 640), bf16),
          pltpu.VMEM((rows, 128), f32), pltpu.VMEM((rows, 128), f32)],
-        name="forward",
+        name="forward", room=8,
     )(me, gathered, o, *tables["w1"], *tables["g1"])
 
 
@@ -447,46 +483,53 @@
 
 def waves(place, arrived, stat, sums, tables):
     return call(
-        wave_kernel, [smem] + [vmem] * 7, (shape(rows, 128), shape(8, 128)), name="waves"
+        wave_kernel, [smem] + [vmem] * 7, (shape(rows, 128), shape(8, 128), shape(bands, 8, 128)), name="waves"
     )(place, arrived, stat, sums, *tables["g2"], *tables["g3"])
 
 
 def image(energies, arrived, scal, fields, o, tables):
     return call(
         image_kernel, [smem] + [vmem] * 8,
-        (shape(trials, rows, 128), shape(trials, rows, 128), shape(groups, 8, 128), shape(bands, 8, 128)),
+        (shape(trials * rows, 128), shape(trials * rows, 128), shape(8, 128), shape(8, 128)),
         [pltpu.VMEM((rows, 128), f32), pltpu.VMEM((rows, 128), f32)],
-        name="image",
+        name="image", room=8,
     )(energies, arrived, scal, fields, o, *tables["g4"], *tables["w2"])
 
 
-def flat(coef, source, residual):
-    small = pl.BlockSpec((bands, 8, 128), lambda p: (0, 0, 0))
-    block = pl.BlockSpec((1, rows, 128), lambda p: (p, 0, 0))
-    out = pl.BlockSpec((1, 1, planes, points * points), lambda p: (0, p, 0, 0))
+def share(norm, coefs):
+    return call(share_kernel, [vmem] * 2, shape(groups, 8, 128), name="share")(norm, coefs)
+
+
+steps_flat = 6
+cell_block = pl.BlockSpec((planes, trials, points * points // steps_flat), lambda i: (0, 0, i))
+cell_shape = shape(planes, trials, points * points)
+small_block = pl.BlockSpec((8, 128), lambda i: (0, 0))
+
+
+def flat(step, source, residual):
+    block = pl.BlockSpec((trials * rows // steps_flat, 128), lambda i: (i, 0))
     return pl.pallas_call(
-        flat_kernel, grid=(trials,), in_specs=[small, block, block], out_specs=(out, out),
-        out_shape=(shape(1, trials, planes, points * points),) * 2, compiler_params=params, name="flat",
-    )(coef, source, residual)
-
-
-def direct(coef, scal, norms, response, residual):
-    out = pl.BlockSpec((1, 1, planes, points * points), lambda p: (0, p, 0, 0))
+        flat_kernel, grid=(steps_flat,), in_specs=[small_block, block, block],
+        out_specs=(cell_block, cell_block), out_shape=(cell_shape, cell_shape),
+        compiler_params=params(8), name="flat",
+        cost_estimate=pl.CostEstimate(flops=10**7, bytes_accessed=10**7, transcendentals=0),
+    )(step, source, residual)
+
+
+def direct(step, norms, response, residual):
     return pl.pallas_call(
-        direction_kernel, grid=(trials,),
-        in_specs=[
-            pl.BlockSpec((bands, 8, 128), lambda p: (0, 0, 0)),
-            pl.BlockSpec((8, 128), lambda p: (0, 0)),
-            pl.BlockSpec((groups, 8, 128), lambda p: (0, 0, 0)),
-            out, out,
-        ],
-        out_specs=out, out_shape=shape(1, trials, planes, points * points),
-        compiler_params=params, name="direction",
-    )(coef, scal, norms, response, residual)
-
-
-def density_of(coef, packed, o):
-    return call(density_kernel, [vmem] * 3, shape(trials, planes, 288), name="density")(coef, packed, o)
+        direction_kernel, grid=(steps_flat,),
+        in_specs=[small_block, pl.BlockSpec((groups, 8, 128), lambda i: (0, 0, 0)), cell_block, cell_block],
+        out_specs=cell_block, out_shape=cell_shape, compiler_params=params(8), name="direction",
+    )(step, norms, response, residual)
+
+
+def density_of(norms, coefs, packed, o):
+    return call(density_kernel, [vmem] * 4, shape(planes, trials, 288), name="density")(norms, coefs, packed, o)
+
+
+def outward(value):
+    return jnp.transpose(value, (1, 0, 2))
 
 
 def swapped(value, axis, size, mask):
@@ -511,15 +554,15 @@
     fields, sent, stat = forward(me, gathered, o, tables)
     arrived = lax.all_to_all(sent.reshape(groups, chunk, 128), "grid", 0, 0, tiled=True).reshape(rows, 128)
     sums = local_sums(energies, fields, o, stat)
-    back, scal = waves(place, arrived, stat, sums, tables)
+    back, scal, coef = waves(place, arrived, stat, sums, tables)
     back = lax.all_to_all(back.reshape(groups, chunk, 128), "grid", 0, 0, tiled=True).reshape(rows, 128)
-    source, residual, norms, coef = image(energies, back, scal, fields, o, tables)
-    norms = lax.all_to_all(norms, "grid", 0, 0, tiled=True)
     coefs = lax.all_to_all(coef, "band", 0, 0, tiled=True)
-    response, residual = flat(coef, source, residual)
-    direction = direct(coef, scal, norms, response, residual)
-    density = density_of(coefs, packed, o_bands)
-    return response, residual, direction, density
+    source, residual, norm, step = image(energies, back, scal, fields, o, tables)
+    norms = lax.all_to_all(share(norm, coefs), "grid", 0, 0, tiled=True)
+    response, residual = flat(step, source, residual)
+    direction = direct(step, norms, response, residual)
+    density = density_of(norms, coefs, packed, o_bands)
+    return outward(response)[None], outward(residual)[None], outward(direction)[None], outward(density)
 
 
 def solution(mesh):

time: 152 us -> 157 us (1.033)
  blocking collectives: 8.35 us -> 20.7 us
  starting transfers between devices: 41 us -> 32.4 us
  local copies, waits for them, and re-layouts: 39.7 us -> 32 us
  Pallas kernels: 17.8 us -> 23.9 us
  waiting for transfers between devices: 42.3 us -> 44.9 us
    all_to_all x1, blocking collectives: 8.35 us -> 20.7 us  [on_device(): coefs = lax.all_to_all(coef, 'band', 0, 0, tiled=True)]
    unnamed x66 -> x65, local copies, waits for them, and re-layouts: 36.8 us -> 29.1 us
    pallas_call x6 -> x7, Pallas kernels: 11.6 us -> 17.7 us  [the longest x1 5.4 us: image(): call(image_kernel, [smem] + [vmem] * 8, (shape(trials * rows, 128), shape...]
    all_to_all x1, starting transfers between devices: 10.8 us -> 5.2 us  [on_device(): lax.all_to_all(o.reshape(bands, 36, 128), 'band', 0, 0, tiled=True)]
    all_to_all x1, starting transfers between devices: 6.33 us -> 3.31 us  [on_device(): norms = lax.all_to_all(share(norm, coefs), 'grid', 0, 0, tiled=True)]
    all_to_all x1, waiting for transfers between devices: 8.14 us -> 9.94 us  [on_device(): lax.all_to_all(back.reshape(groups, chunk, 128), 'grid', 0, 0, tiled=True)]
  transfers between devices with their start and end apart: 11 -> 11, of which waited for: 9 -> 9; matrix products, arithmetic and copies ran while one was open for 8% -> 3% of each run, Pallas kernels for 6% -> 7%
where the time goes in v2:
time: 157 us; the launch traced here: 155 us
  waiting for transfers between devices  44.9 us (29%)
  starting transfers between devices  32.4 us (21%)
  local copies, waits for them, and re-layouts  32 us (20%)
  Pallas kernels  23.9 us (15%)
  blocking collectives  20.7 us (13%)
    unnamed x65, local copies, waits for them, and re-layouts  29.1 us
    all_to_all x1, blocking collectives, on_device(): coefs = lax.all_to_all(coef, 'band', 0, 0, tiled=True)  20.7 us
    ppermute x7, waiting for transfers between devices, swapped(): return lax.ppermute(value, axis, [(s, s ^ mask) for s in range(size)])  18.9 us
    ppermute x7, starting transfers between devices, swapped(): return lax.ppermute(value, axis, [(s, s ^ mask) for s in range(size)])  15.6 us
    all_to_all x1, waiting for transfers between devices, on_device(): lax.all_to_all(back.reshape(groups, chunk, 128), 'grid', 0, 0, tiled=True)  9.94 us
    all_to_all x1, waiting for transfers between devices, on_device(): lax.all_to_all(o.reshape(bands, 36, 128), 'band', 0, 0, tiled=True)  8.69 us
    all_to_all x1, waiting for transfers between devices, on_device(): lax.all_to_all(sent.reshape(groups, chunk, 128), 'grid', 0, 0, tiled=True)  7.38 us
    pallas_call x1, Pallas kernels, image(): call(image_kernel, [smem] + [vmem] * 8, (shape(trials * rows, 128), shape...  5.4 us
  transfers between devices with their start and end apart: 11, of which 9 were waited for; matrix products, arithmetic and copies ran while one was open for 3% of the time, Pallas kernels for 7%

profile of v2, /device:TPU:1, one launch (start us, length us, event | category | flops | bytes accessed | tf_op | source)
XLA Modules:
  0.0 155.4 jit_solution(16396362827163970229)
XLA Ops:
  0.6 0.9 copy-done.18
  1.5 0.7 copy-done.27
  2.3 0.2 pack.1.packed_ref
  2.4 0.0 copy-start.8
  2.4 3.9 %collective-permute-start = (f32[1,144,128]{2,1,0:T(8,128)S(1)}, f32[1,144,128]{2,1,0:T(8,128)S(1)}, u32[]{:S(2)}, u32[]{:S(2)}) collective-permute-start(f32[1,144,128]{2,1,0:T(8,128)S(1)} %bitcast.22), channel_id=1, source_target_pairs={{0,64},{8,72},{16,80},{24,88},{32,96},{40,104},{48,112},{56,120},{... | collective-permute-start | bytes 221192 | tf_op jit(solution)/shard_map/ppermute | solution.py:536
  6.3 5.1 %collective-permute-start.1 = (f32[1,144,128]{2,1,0:T(8,128)S(1)}, f32[1,144,128]{2,1,0:T(8,128)S(1)}, u32[]{:S(2)}, u32[]{:S(2)}) collective-permute-start(f32[1,144,128]{2,1,0:T(8,128)S(1)} %bitcast.23), channel_id=1, source_target_pairs={{0,128},{8,136},{16,144},{24,152},{32,160},{40,168},{48,176},{56,1... | collective-permute-start | bytes 221192 | tf_op jit(solution)/shard_map/ppermute | solution.py:536
  11.5 0.6 constant_dynamic-update-slice_fusion.6
  12.1 2.5 %collective-permute-done.1 = f32[1,144,128]{2,1,0:T(8,128)S(1)} collective-permute-done((f32[1,144,128]{2,1,0:T(8,128)S(1)}, f32[1,144,128]{2,1,0:T(8,128)S(1)}, u32[]{:S(2)}, u32[]{:S(2)}) %collective-permute-start.1) | collective-permute-done | bytes 73760 | tf_op jit(solution)/shard_map/ppermute | solution.py:536
  14.6 2.9 %collective-permute-done.2 = f32[1,144,128]{2,1,0:T(8,128)S(1)} collective-permute-done((f32[1,144,128]{2,1,0:T(8,128)S(1)}, f32[1,144,128]{2,1,0:T(8,128)S(1)}, u32[]{:S(2)}, u32[]{:S(2)}) %collective-permute-start.2) | collective-permute-done | bytes 73760 | tf_op jit(solution)/shard_map/ppermute | solution.py:536
  17.5 1.4 collective-permute-start.3
  18.9 2.6 %collective-permute-start.4 = (f32[4,144,128]{2,1,0:T(8,128)S(1)}, f32[4,144,128]{2,1,0:T(8,128)S(1)}, u32[]{:S(2)}, u32[]{:S(2)}) collective-permute-start(f32[4,144,128]{2,1,0:T(8,128)S(1)} %pad_maximum_fusion), channel_id=1, source_target_pairs={{0,32},{8,40},{16,48},{24,56},{32,0},{40,8},{48,16},{56,24},{64,96... | collective-permute-start | bytes 884744 | tf_op jit(solution)/shard_map/ppermute | solution.py:536
  21.5 0.6 constant_dynamic-update-slice_fusion.5
  22.2 0.6 constant_dynamic-update-slice_fusion.4
  22.8 0.6 constant_dynamic-update-slice_fusion.3
  23.5 1.0 collective-permute-done.3
  24.4 0.8 constant_dynamic-update-slice_fusion.2
  25.2 8.1 %collective-permute-done.4 = f32[4,144,128]{2,1,0:T(8,128)S(1)} collective-permute-done((f32[4,144,128]{2,1,0:T(8,128)S(1)}, f32[4,144,128]{2,1,0:T(8,128)S(1)}, u32[]{:S(2)}, u32[]{:S(2)}) %collective-permute-start.4) | collective-permute-done | bytes 294944 | tf_op jit(solution)/shard_map/ppermute | solution.py:536
  33.3 0.8 constant_dynamic-update-slice_fusion.1
  34.0 1.9 %collective-permute-done.5 = f32[4,144,128]{2,1,0:T(8,128)S(1)} collective-permute-done((f32[4,144,128]{2,1,0:T(8,128)S(1)}, f32[4,144,128]{2,1,0:T(8,128)S(1)}, u32[]{:S(2)}, u32[]{:S(2)}) %collective-permute-start.5) | collective-permute-done | bytes 294944 | tf_op jit(solution)/shard_map/ppermute | solution.py:536
  35.9 0.8 constant_dynamic-update-slice_fusion
  36.7 2.5 %collective-permute-start.6 = (f32[16,144,128]{2,1,0:T(8,128)}, f32[16,144,128]{2,1,0:T(8,128)}, u32[]{:S(2)}, u32[]{:S(2)}) collective-permute-start(f32[16,144,128]{2,1,0:T(8,128)} %get-tuple-element.28), channel_id=1, source_target_pairs={{0,8},{8,0},{16,24},{24,16},{32,40},{40,32},{48,56},{56,48},{64,72... | collective-permute-start | bytes 3538952 | tf_op jit(solution)/shard_map/ppermute | solution.py:536
  39.2 0.1 copy.21.o_ref
  39.3 0.2 orbital_rows.1.o_ref
  39.6 2.5 %collective-permute-done.6 = f32[16,144,128]{2,1,0:T(8,128)} collective-permute-done((f32[16,144,128]{2,1,0:T(8,128)}, f32[16,144,128]{2,1,0:T(8,128)}, u32[]{:S(2)}, u32[]{:S(2)}) %collective-permute-start.6) | collective-permute-done | bytes 1179680 | tf_op jit(solution)/shard_map/ppermute | solution.py:536
  42.0 1.3 constant_dynamic-update-slice_fusion.7.t_ref
  43.4 1.4 copy-done
  44.8 1.7 %copy-done.1 = f32[32,144,128]{2,1,0:T(8,128)S(1)} copy-done((f32[32,144,128]{2,1,0:T(8,128)S(1)}, f32[32,144,128]{2,1,0:T(8,128)}, u32[]{:S(2)}) %copy-start.1) | copy-done | bytes 2359320
  46.5 1.0 copy-done.14
  47.5 1.0 copy-done.15
  48.4 0.8 copy-done.21
  49.2 0.8 copy-done.22
  50.0 4.0 %forward.1 = (f32[5,1152,128]{2,1,0:T(8,128)S(1)}, f32[1152,128]{1,0:T(8,128)S(1)}, f32[8,128]{1,0:T(8,128)S(1)}) custom-call(s32[1]{0:T(128)} %bitcast.1.me_ref, f32[32,144,128]{2,1,0:T(8,128)S(1)} %copy-done.1, f32[1152,128]{1,0:T(8,128)S(1)} %orbital_rows.1.o_ref, bf16[640,256]{1,0:T(8,128)(2,1)S(1)} %copy-done.14, bf16[640,256]{1,0:T(8,128)(2,1)S(1)} %copy-done.15, ...), custom_call_target="tpu_custom_call" | custom-call | tf_op jit(solution)/shard_map/forward/pallas_call | solution.py:471
  54.0 0.8 copy-done.12
  54.8 4.2 %all-to-all-start = ((f32[8,144,128]{2,1,0:T(8,128)}), f32[8,144,128]{2,1,0:T(8,128)}, u32[]{:S(2)}, u32[]{:S(2)}) async-start(f32[8,144,128]{2,1,0:T(8,128)} %bitcast.26), calls=%async_computation | async-start | bytes 1179648 | tf_op jit(solution)/shard_map/all_to_all | solution.py:555
  59.7 2.0 %local_sums.1.sums_ref = f32[8,128]{1,0:T(8,128)S(1)} custom-call(f32[1]{0:T(128)S(6)} %copy.35.energy_ref, f32[5,1152,128]{2,1,0:T(8,128)S(1)} %get-tuple-element.18.field_ref, f32[1152,128]{1,0:T(8,128)S(1)} %orbital_rows.1.o_ref, f32[8,128]{1,0:T(8,128)S(1)} %get-tuple-element.17.stat_ref), custom_call_target="tpu_custom_call" | custom-call | tf_op jit(solution)/shard_map/local_sums/pallas_call | solution.py:481
  61.6 7.4 %all-to-all-done = f32[8,144,128]{2,1,0:T(8,128)} async-done(((f32[8,144,128]{2,1,0:T(8,128)}), f32[8,144,128]{2,1,0:T(8,128)}, u32[]{:S(2)}, u32[]{:S(2)}) %all-to-all-start) | async-done | bytes 589856 | tf_op jit(solution)/shard_map/all_to_all | solution.py:555
  69.0 0.8 copy-done.23
  69.8 0.8 copy-done.24
  70.6 0.8 copy-done.25
  71.4 0.8 copy-done.26
  72.2 2.3 %waves.1 = (f32[1152,128]{1,0:T(8,128)S(1)}, f32[8,128]{1,0:T(8,128)S(1)}, f32[32,8,128]{2,1,0:T(8,128)S(1)}) custom-call(s32[1]{0:T(128)} %bitcast.place_ref, f32[1152,128]{1,0:T(8,128)} %bitcast.5.in_ref, f32[8,128]{1,0:T(8,128)S(1)} %get-tuple-element.17.stat_ref, f32[8,128]{1,0:T(8,128)S(1)} %local_sums.1.sums_ref, bf16[96,192]{1,0:T(8,128)(2,1)S(1)} %copy-done.23, ...), custom_call_target="tpu_custom_call" | custom-call | tf_op jit(solution)/shard_map/waves/pallas_call | solution.py:485
  74.5 20.7 %all_to_all.25.coef_ref = f32[32,8,128]{2,1,0:T(8,128)} all-to-all(f32[32,8,128]{2,1,0:T(8,128)S(1)} %get-tuple-element.27), channel_id=1, replica_groups=mesh['band'=32,'grid'=8] {'band'}, dimensions={0} | all-to-all | bytes 262144 | tf_op jit(solution)/shard_map/all_to_all | solution.py:559
  95.2 4.2 %all-to-all-start.1 = ((f32[8,144,128]{2,1,0:T(8,128)}), f32[8,144,128]{2,1,0:T(8,128)}, u32[]{:S(2)}, u32[]{:S(2)}) async-start(f32[8,144,128]{2,1,0:T(8,128)} %bitcast.27), calls=%async_computation.1 | async-start | bytes 1179648 | tf_op jit(solution)/shard_map/all_to_all | solution.py:558
  99.4 0.9 reshape.35
  100.3 9.9 %all-to-all-done.1 = f32[8,144,128]{2,1,0:T(8,128)} async-done(((f32[8,144,128]{2,1,0:T(8,128)}), f32[8,144,128]{2,1,0:T(8,128)}, u32[]{:S(2)}, u32[]{:S(2)}) %all-to-all-start.1) | async-done | bytes 589856 | tf_op jit(solution)/shard_map/all_to_all | solution.py:558
  110.2 5.2 %all-to-all-start.4 = ((f32[32,36,128]{2,1,0:T(8,128)}), f32[32,36,128]{2,1,0:T(8,128)}, u32[]{:S(2)}, u32[]{:S(2)}) async-start(f32[32,36,128]{2,1,0:T(8,128)} %reshape.35), calls=%async_computation.4 | async-start | bytes 1310720 | tf_op jit(solution)/shard_map/all_to_all | solution.py:553
  115.4 0.0 copy-start.16
  115.4 0.9 copy-done.16
  116.4 0.9 copy-done.17
  117.3 0.8 copy-done.19
  118.1 0.8 copy-done.20
  118.9 5.4 %image.1 = (f32[4608,128]{1,0:T(8,128)S(1)}, f32[4608,128]{1,0:T(8,128)S(1)}, f32[8,128]{1,0:T(8,128)S(1)}, f32[8,128]{1,0:T(8,128)S(1)}) custom-call(f32[1]{0:T(128)S(6)} %copy.35.energy_ref, f32[1152,128]{1,0:T(8,128)} %bitcast.7.in_ref, f32[8,128]{1,0:T(8,128)S(1)} %get-tuple-element.20.scal_ref, f32[5,1152,128]{2,1,0:T(8,128)S(1)} %get-tuple-element.18.field_ref, ...), custom_call_target="tpu_custom_call" | custom-call | tf_op jit(solution)/shard_map/image/pallas_call | solution.py:491
  124.3 1.4 copy-done.2
  125.7 1.4 copy-done.4
  127.2 0.7 share.1
  127.9 8.7 %all-to-all-done.4.o_ref = f32[32,36,128]{2,1,0:T(8,128)} async-done(((f32[32,36,128]{2,1,0:T(8,128)}), f32[32,36,128]{2,1,0:T(8,128)}, u32[]{:S(2)}, u32[]{:S(2)}) %all-to-all-start.4) | async-done | bytes 589856 | tf_op jit(solution)/shard_map/all_to_all | solution.py:553
  136.6 3.3 %all-to-all-start.3 = ((f32[8,8,128]{2,1,0:T(8,128)}), f32[8,8,128]{2,1,0:T(8,128)S(1)}, u32[]{:S(2)}, u32[]{:S(2)}) async-start(f32[8,8,128]{2,1,0:T(8,128)} %share.1), calls=%async_computation.3 | async-start | bytes 65536 | tf_op jit(solution)/shard_map/all_to_all | solution.py:561
  139.9 1.7 %copy-done.3 = f32[4608,128]{1,0:T(8,128)S(1)} copy-done((f32[4608,128]{1,0:T(8,128)S(1)}, f32[4608,128]{1,0:T(8,128)}, u32[]{:S(2)}) %copy-start.3) | copy-done | bytes 2359320
  141.6 1.7 %copy-done.5 = f32[4608,128]{1,0:T(8,128)S(1)} copy-done((f32[4608,128]{1,0:T(8,128)S(1)}, f32[4608,128]{1,0:T(8,128)}, u32[]{:S(2)}) %copy-start.5) | copy-done | bytes 2359320
  143.2 3.4 %flat.1 = (f32[12,4,9216]{2,1,0:T(4,128)}, f32[12,4,9216]{2,1,0:T(4,128)}) custom-call(f32[8,128]{1,0:T(8,128)S(1)} %get-tuple-element.21.step_ref, f32[4608,128]{1,0:T(8,128)S(1)} %copy-done.3, f32[4608,128]{1,0:T(8,128)S(1)} %copy-done.5), custom_call_target="tpu_custom_call" | custom-call | flops 10000000 | bytes 10000000 | tf_op jit(solution)/shard_map/flat/pallas_call | solution.py:511
  146.6 2.4 %density.1 = f32[12,4,288]{2,1,0:T(4,128)} custom-call(f32[8,8,128]{2,1,0:T(8,128)S(1)} %all-to-all-done.3.norm_ref, f32[32,8,128]{2,1,0:T(8,128)S(1)} %copy-done.11, f32[144,128]{1,0:T(8,128)S(1)} %copy-done.9, f32[32,36,128]{2,1,0:T(8,128)} %all-to-all-done.4.o_ref), custom_call_target="tpu_custom_call" | custom-call | tf_op jit(solution)/shard_map/density/pallas_call | solution.py:528
  149.1 1.5 copy-done.6
  150.5 1.5 copy-done.7
  152.0 3.4 %direction.1 = f32[12,4,9216]{2,1,0:T(4,128)} custom-call(f32[8,128]{1,0:T(8,128)S(1)} %get-tuple-element.21.step_ref, f32[8,8,128]{2,1,0:T(8,128)S(1)} %all-to-all-done.3.norm_ref, f32[12,4,9216]{2,1,0:T(4,128)S(1)} %copy-done.6, f32[12,4,9216]{2,1,0:T(4,128)S(1)} %copy-done.7), custom_call_target="tpu_custom_call" | custom-call | tf_op jit(solution)/shard_map/direction/pallas_call | solution.py:520
  (38 shorter events, 0.1 us)
Async XLA Ops:
  0.6 0.9 copy-start.18
  1.5 0.7 copy-start.27
  2.3 37.0 %copy-start.28 = (f32[1,12,9216]{2,0,1:T(1,128)S(1)}, f32[1,12,9216]{2,0,1:T(1,128)}, u32[]{:S(2)}) copy-start(f32[1,12,9216]{2,0,1:T(1,128)} %param.16) | copy-start | bytes 1327108
  2.4 22.0 %copy-start.8 = (f32[144,128]{1,0:T(8,128)}, f32[144,128]{1,0:T(8,128)S(1)}, u32[]{:S(2)}) copy-start(f32[144,128]{1,0:T(8,128)S(1)} %pack.1.packed_ref) | copy-start | bytes 221188
  2.4 9.7 %collective-permute-start = (f32[1,144,128]{2,1,0:T(8,128)S(1)}, f32[1,144,128]{2,1,0:T(8,128)S(1)}, u32[]{:S(2)}, u32[]{:S(2)}) collective-permute-start(f32[1,144,128]{2,1,0:T(8,128)S(1)} %bitcast.22), channel_id=1, source_target_pairs={{0,64},{8,72},{16,80},{24,88},{32,96},{40,104},{48,112},{56,120},{... | collective-permute-start | bytes 221192 | tf_op jit(solution)/shard_map/ppermute | solution.py:536
  6.3 8.2 %collective-permute-start.1 = (f32[1,144,128]{2,1,0:T(8,128)S(1)}, f32[1,144,128]{2,1,0:T(8,128)S(1)}, u32[]{:S(2)}, u32[]{:S(2)}) collective-permute-start(f32[1,144,128]{2,1,0:T(8,128)S(1)} %bitcast.23), channel_id=1, source_target_pairs={{0,128},{8,136},{16,144},{24,152},{32,160},{40,168},{48,176},{56,1... | collective-permute-start | bytes 221192 | tf_op jit(solution)/shard_map/ppermute | solution.py:536
  11.5 6.0 %collective-permute-start.2 = (f32[1,144,128]{2,1,0:T(8,128)S(1)}, f32[1,144,128]{2,1,0:T(8,128)S(1)}, u32[]{:S(2)}, u32[]{:S(2)}) collective-permute-start(f32[1,144,128]{2,1,0:T(8,128)S(1)} %bitcast.24), channel_id=1, source_target_pairs={{0,192},{8,200},{16,208},{24,216},{32,224},{40,232},{48,240},{56,2... | collective-permute-start | bytes 221192 | tf_op jit(solution)/shard_map/ppermute | solution.py:536
  17.5 6.9 %collective-permute-start.3 = (f32[4,144,128]{2,1,0:T(8,128)S(1)}, f32[4,144,128]{2,1,0:T(8,128)S(1)}, u32[]{:S(2)}, u32[]{:S(2)}) collective-permute-start(f32[4,144,128]{2,1,0:T(8,128)S(1)} %pad_maximum_fusion), channel_id=1, source_target_pairs={{0,16},{8,24},{16,0},{24,8},{32,48},{40,56},{48,32},{56,40},{64,80... | collective-permute-start | bytes 884744 | tf_op jit(solution)/shard_map/ppermute | solution.py:536
  18.9 14.4 %collective-permute-start.4 = (f32[4,144,128]{2,1,0:T(8,128)S(1)}, f32[4,144,128]{2,1,0:T(8,128)S(1)}, u32[]{:S(2)}, u32[]{:S(2)}) collective-permute-start(f32[4,144,128]{2,1,0:T(8,128)S(1)} %pad_maximum_fusion), channel_id=1, source_target_pairs={{0,32},{8,40},{16,48},{24,56},{32,0},{40,8},{48,16},{56,24},{64,96... | collective-permute-start | bytes 884744 | tf_op jit(solution)/shard_map/ppermute | solution.py:536
  21.5 14.4 %collective-permute-start.5 = (f32[4,144,128]{2,1,0:T(8,128)S(1)}, f32[4,144,128]{2,1,0:T(8,128)S(1)}, u32[]{:S(2)}, u32[]{:S(2)}) collective-permute-start(f32[4,144,128]{2,1,0:T(8,128)S(1)} %pad_maximum_fusion), channel_id=1, source_target_pairs={{0,48},{8,56},{16,32},{24,40},{32,16},{40,24},{48,0},{56,8},{64,11... | collective-permute-start | bytes 884744 | tf_op jit(solution)/shard_map/ppermute | solution.py:536
  36.7 5.3 %collective-permute-start.6 = (f32[16,144,128]{2,1,0:T(8,128)}, f32[16,144,128]{2,1,0:T(8,128)}, u32[]{:S(2)}, u32[]{:S(2)}) collective-permute-start(f32[16,144,128]{2,1,0:T(8,128)} %get-tuple-element.28), channel_id=1, source_target_pairs={{0,8},{8,0},{16,24},{24,16},{32,40},{40,32},{48,56},{56,48},{64,72... | collective-permute-start | bytes 3538952 | tf_op jit(solution)/shard_map/ppermute | solution.py:536
  43.4 1.4 copy-start
  44.8 1.7 %copy-start.1 = (f32[32,144,128]{2,1,0:T(8,128)S(1)}, f32[32,144,128]{2,1,0:T(8,128)}, u32[]{:S(2)}) copy-start(f32[32,144,128]{2,1,0:T(8,128)} %copy-done) | copy-start | bytes 7077892
  46.5 1.0 copy-start.14
  47.5 1.0 copy-start.15
  48.4 0.8 copy-start.21
  49.2 0.8 copy-start.22
  54.0 0.8 copy-start.12
  54.8 14.2 %all-to-all-start = ((f32[8,144,128]{2,1,0:T(8,128)}), f32[8,144,128]{2,1,0:T(8,128)}, u32[]{:S(2)}, u32[]{:S(2)}) async-start(f32[8,144,128]{2,1,0:T(8,128)} %bitcast.26), calls=%async_computation | async-start | bytes 1179648 | tf_op jit(solution)/shard_map/all_to_all | solution.py:555
  69.0 0.8 copy-start.23
  69.8 0.8 copy-start.24
  70.6 0.8 copy-start.25
  71.4 0.8 copy-start.26
  74.5 20.7 %copy-start.13 = (f32[1152,128]{1,0:T(8,128)}, f32[1152,128]{1,0:T(8,128)S(1)}, u32[]{:S(2)}) copy-start(f32[1152,128]{1,0:T(8,128)S(1)} %get-tuple-element.19) | copy-start | bytes 1769476
  95.2 15.0 %all-to-all-start.1 = ((f32[8,144,128]{2,1,0:T(8,128)}), f32[8,144,128]{2,1,0:T(8,128)}, u32[]{:S(2)}, u32[]{:S(2)}) async-start(f32[8,144,128]{2,1,0:T(8,128)} %bitcast.27), calls=%async_computation.1 | async-start | bytes 1179648 | tf_op jit(solution)/shard_map/all_to_all | solution.py:558
  110.2 26.4 %all-to-all-start.4 = ((f32[32,36,128]{2,1,0:T(8,128)}), f32[32,36,128]{2,1,0:T(8,128)}, u32[]{:S(2)}, u32[]{:S(2)}) async-start(f32[32,36,128]{2,1,0:T(8,128)} %reshape.35), calls=%async_computation.4 | async-start | bytes 1310720 | tf_op jit(solution)/shard_map/all_to_all | solution.py:553
  115.4 1.0 copy-start.16
  116.4 0.9 copy-start.17
  117.3 0.8 copy-start.19
  118.1 0.8 copy-start.20
  118.9 8.3 %copy-start.10 = (f32[32,8,128]{2,1,0:T(8,128)S(1)}, f32[32,8,128]{2,1,0:T(8,128)}, u32[]{:S(2)}) copy-start(f32[32,8,128]{2,1,0:T(8,128)} %all_to_all.25.coef_ref) | copy-start | bytes 393220
  124.3 1.4 copy-start.2
  125.7 1.4 copy-start.4
  136.6 10.0 %all-to-all-start.3 = ((f32[8,8,128]{2,1,0:T(8,128)}), f32[8,8,128]{2,1,0:T(8,128)S(1)}, u32[]{:S(2)}, u32[]{:S(2)}) async-start(f32[8,8,128]{2,1,0:T(8,128)} %share.1), calls=%async_computation.3 | async-start | bytes 65536 | tf_op jit(solution)/shard_map/all_to_all | solution.py:561
  139.9 1.7 %copy-start.3 = (f32[4608,128]{1,0:T(8,128)S(1)}, f32[4608,128]{1,0:T(8,128)}, u32[]{:S(2)}) copy-start(f32[4608,128]{1,0:T(8,128)} %copy-done.2) | copy-start | bytes 7077892
  141.6 1.7 %copy-start.5 = (f32[4608,128]{1,0:T(8,128)S(1)}, f32[4608,128]{1,0:T(8,128)}, u32[]{:S(2)}) copy-start(f32[4608,128]{1,0:T(8,128)} %copy-done.4) | copy-start | bytes 7077892
  143.2 3.4 %copy-start.9 = (f32[144,128]{1,0:T(8,128)S(1)}, f32[144,128]{1,0:T(8,128)}, u32[]{:S(2)}) copy-start(f32[144,128]{1,0:T(8,128)} %copy-done.8) | copy-start | bytes 221188
  143.2 3.4 %copy-start.11 = (f32[32,8,128]{2,1,0:T(8,128)S(1)}, f32[32,8,128]{2,1,0:T(8,128)}, u32[]{:S(2)}) copy-start(f32[32,8,128]{2,1,0:T(8,128)} %all_to_all.25.coef_ref) | copy-start | bytes 393220
  149.1 1.5 copy-start.6
  150.5 1.5 copy-start.7

commit v3 on v1

v3 whole, which is shorter than its diff:
```python
import math

import jax
import jax.numpy as jnp
import ml_dtypes
import numpy as np
from jax import lax
from jax.experimental import pallas as pl
from jax.experimental.pallas import tpu as pltpu
from jax.sharding import PartitionSpec as P

points = 96
planes = 12
trials = 4
bands = 32
half = 24
groups = 8
rows = points * planes
chunk = rows // groups
spacing = 0.49
prefactor = 0.5 * (2.0 * math.pi / (points * spacing)) ** 2
f32 = jnp.float32
bf16 = jnp.bfloat16


def split_np(table):
    table = np.asarray(table, np.float32)
    high = table.astype(ml_dtypes.bfloat16)
    low = (table - high.astype(np.float32)).astype(ml_dtypes.bfloat16)
    return np.stack([high, low])


def angle(a, b):
    return (np.outer(a, b) % points) * (2.0 * np.pi / points)


def build_tables():
    grid = np.arange(points)
    signed = np.arange(2 * half) - half
    kz = np.arange(half)
    w1 = np.zeros((5 * 128, 256))
    az = angle(grid, kz)
    for p in range(5):
        w1[p * 128 : p * 128 + points, p * half : (p + 1) * half] = np.cos(az)
        w1[p * 128 : p * 128 + points, 128 + p * half : 128 + (p + 1) * half] = -np.sin(az)
    order = np.zeros(points, np.int64)
    part = np.zeros(points, np.int64)
    for jj in range(6):
        for c in range(2):
            for g in range(groups):
                order[(2 * jj + c) * 8 + g] = signed[6 * g + jj]
                part[(2 * jj + c) * 8 + g] = c
    ay = angle(order, grid)
    real = part[:, None] == 0
    g1 = np.concatenate(
        [np.where(real, np.cos(ay), -np.sin(ay)), np.where(real, np.sin(ay), np.cos(ay))], 1
    )
    g4 = np.concatenate(
        [np.where(real, np.cos(ay), -np.sin(ay)), np.where(real, np.sin(ay), np.cos(ay))], 1
    ).T
    ax = angle(signed, grid)
    cx, sx = np.cos(ax), np.sin(ax)
    g2 = np.block([[cx, sx], [-sx, cx]])
    g3 = np.block([[cx.T, -sx.T], [sx.T, cx.T]])
    w2 = np.zeros((256, 4 * 128))
    for p in range(4):
        w2[p * half : (p + 1) * half, p * 128 : p * 128 + points] = np.cos(az).T
        w2[128 + p * half : 128 + (p + 1) * half, p * 128 : p * 128 + points] = -np.sin(az).T
    return {"w1": split_np(w1), "g1": split_np(g1), "g2": split_np(g2), "g3": split_np(g3),
            "g4": split_np(g4), "w2": split_np(w2)}


def dot(a, b):
    return lax.dot_general(a, b, (((1,), (0,)), ((), ())), preferred_element_type=f32)


def split(value):
    high = value.astype(bf16)
    return high, (value - high.astype(f32)).astype(bf16)


def left_table(table, value):
    vh, vl = split(value)
    return dot(table[0], vh) + dot(table[0], vl) + dot(table[1], vh)


def right_table(vh, vl, table):
    return dot(vh, table[0]) + dot(vl, table[0]) + dot(vh, table[1])


def begin(source, target, sem):
    copy = pltpu.make_async_copy(source, target, sem)
    copy.start()
    return copy


def lane_of(shape):
    return lax.broadcasted_iota(jnp.int32, shape, 1)


def row_of(shape):
    return lax.broadcasted_iota(jnp.int32, shape, 0)


def total(value):
    return jnp.sum(jnp.sum(value, axis=0, keepdims=True), axis=1, keepdims=True)


def fold(value):
    return jnp.sum(value.reshape(value.shape[0] // 8, 8, 128), axis=0)


def tile_of(shape, entries):
    row, lane = row_of(shape), lane_of(shape)
    out = jnp.zeros(shape, f32)
    for r, l, value in entries:
        out = jnp.where((row == r) & (lane == l), value, out)
    return out


def spread(t0, t1, t2):
    lane = lane_of(t0.shape)
    c1 = pltpu.roll(jnp.where(lane >= 96, t0, t1), 32, 1)
    c2 = pltpu.roll(jnp.where(lane >= 64, t1, t2), 64, 1)
    return t0, c1, c2


def pack_kernel(trial_ref, local_ref, out_ref):
    lane = lane_of((planes, 128))
    fill = jnp.zeros((planes, 96), f32)

    def pieces(ref, *at):
        t2 = jnp.concatenate([ref[(slice(None), *at, slice(256, 288))], fill], axis=1)
        return spread(ref[(slice(None), *at, slice(0, 128))], ref[(slice(None), *at, slice(128, 256))], t2)

    last = pieces(trial_ref, 3)
    for q in range(3):
        mine = pieces(trial_ref, q)
        for i in range(3):
            tail = pltpu.roll(last[i], 96 - 32 * q, 1)
            out_ref[q * 36 + i * 12 : q * 36 + i * 12 + 12, :] = jnp.where(lane < 96, mine[i], tail)
    mine = pieces(local_ref)
    for i in range(3):
        out_ref[108 + i * 12 : 120 + i * 12, :] = jnp.where(lane < 96, mine[i], 0.0)


def unpack_last(b0, b1, b2):
    lane = lane_of(b0.shape)
    r0, r1, r2 = pltpu.roll(b0, 32, 1), pltpu.roll(b1, 64, 1), pltpu.roll(b2, 96, 1)
    return jnp.where(lane < 32, r0, jnp.where(lane < 64, r1, r2))


def orbital_kernel(o_ref, packed_ref, far_out, base_out, packed_out, out_ref, base_ref, sems):
    kept = begin(packed_ref, packed_out, sems.at[0])
    lane = lane_of((planes, 128))
    for q in range(points // 4):
        t = [o_ref[0, :, 384 * q + 128 * i : 384 * q + 128 * i + 128] for i in range(3)]
        c = [*spread(*t), pltpu.roll(t[2], 96, 1)]
        for i in range(4):
            at = (4 * q + i) * planes
            out_ref[at : at + planes, :] = jnp.where(lane < 96, c[i], 0.0)
    for u in range(bands):
        mine = out_ref[u * 36 : u * 36 + 36, :]
        base_ref[u, 0:36, :] = mine
        base_ref[u, 36:40, :] = jnp.zeros((4, 128), f32)
    copies = [begin(out_ref, far_out, sems.at[2]), begin(base_ref, base_out, sems.at[1]), kept]
    for copy in copies:
        copy.wait()


def forward_kernel(p0, p1, p2, p3, p4, p5, p6, p7, o_far, w1_ref, g1_ref,
                   field_out, result_ref, stat_ref,
                   o_ref, field_ref, t_ref, w1, g1, out_ref, high, low, real, imag, sems):
    me = lax.axis_index("band")
    arrivals = [
        begin(piece, t_ref.at[pl.ds(4 * n, 4)], sems.at[n]) for n, piece in enumerate((p0, p1, p2, p3, p4, p5, p6, p7))
    ]
    arrivals.append(begin(o_far, o_ref, sems.at[10]))
    tables = [begin(w1_ref, w1, sems.at[8]), begin(g1_ref, g1, sems.at[9])]
    for copy in arrivals:
        copy.wait()
    norm = jnp.zeros((36, 128), f32)
    corr = [jnp.zeros((36, 128), f32) for _ in range(trials)]
    for u in range(bands):
        d = u ^ me
        slot = ((d & 1) << 4) | (((d >> 1) & 3) << 2) | (d >> 3)
        blocks = [t_ref[slot, q * 36 : q * 36 + 36, :] for q in range(4)]
        fields = [*blocks[:3], unpack_last(*blocks[:3]), blocks[3]]
        here = slice(u * 36, u * 36 + 36)
        for p in range(5):
            field_ref[p, here, :] = fields[p]
        o = o_ref[here, :]
        square = o * o
        norm = norm + square
        for p in range(trials):
            corr[p] = corr[p] + fields[p] * square
    kept = begin(field_ref, field_out, sems.at[1])
    norm = total(norm)
    mean = [total(c) / norm for c in corr]

    size = 96

    def weigh(i, sums):
        at = pl.ds(pl.multiple_of(i * size, size), size)
        o = o_ref[at, :]
        out = []
        for p in range(trials):
            w = (field_ref[p, at, :] - mean[p]) * o
            high[at, p * 128 : p * 128 + 128], low[at, p * 128 : p * 128 + 128] = split(w)
            out.append(sums[p] + fold(w * w))
        high[at, 512:640], low[at, 512:640] = split(o)
        return tuple(out)

    second = lax.fori_loop(0, rows // size, weigh, tuple(jnp.zeros((8, 128), f32) for _ in range(trials)))
    second = [total(s) for s in second]
    stat_ref[...] = tile_of((8, 128), [(0, 0, norm)] + [(0, 1 + p, mean[p]) for p in range(trials)])

    for copy in tables:
        copy.wait()
    big = 384

    def along_z(i, _):
        at = pl.ds(pl.multiple_of(i * big, big), big)
        a = right_table(high[at, :], low[at, :], w1)
        real[at, :] = a[:, :128]
        imag[at, :] = a[:, 128:]
        return 0

    lax.fori_loop(0, rows // big, along_z, 0)

    row, lane = row_of((points, 128)), lane_of((points, 128))
    ride = jnp.where((row < 8) & (lane == 120), norm, 0.0)
    for p in range(trials):
        ride = jnp.where((row < 8) & (lane == 121 + p), mean[p], ride)
        ride = jnp.where((row >= 8) & (row < 16) & (lane == 120 + p), second[p], ride)
    for x in range(0, planes, 2):
        parts = [
            jnp.concatenate([ref[pl.ds(x + i, points, stride=planes), :] for i in range(2)], axis=1)
            for ref in (real, imag)
        ]
        y = left_table(g1, jnp.concatenate(parts, axis=0))
        for i in range(2):
            mine = y[:, i * 128 : i * 128 + 128] + ride
            for r in range(12):
                out_ref[pl.ds((x + i) * 12 + r, groups, stride=chunk), :] = mine[8 * r : 8 * r + 8]
    begin(out_ref, result_ref, sems.at[0]).wait()
    kept.wait()


def local_kernel(energy_ref, field_ref, o_ref, stat_ref, g2_ref, g3_ref, g4_ref, w2_ref,
                 out_ref, g2, g3, g4, w2, sums, sems):
    step = pl.program_id(0)
    pairs = ((g2_ref, g2), (g3_ref, g3), (g4_ref, g4), (w2_ref, w2))

    @pl.when(step == 0)
    def _():
        sums[...] = jnp.zeros(sums.shape, f32)
        for n, (source, target) in enumerate(pairs):
            pltpu.make_async_copy(source, target, sems.at[n]).start()

    o = o_ref[...]
    shift = (field_ref[4] - energy_ref[0]) * o
    sums[0] += fold(shift * o)
    for p in range(trials):
        off = field_ref[p] - stat_ref[0:1, 1 + p : 2 + p]
        both = shift * off
        sums[1 + p] += fold(both * o)
        sums[5 + p] += fold(both * (off * o))

    @pl.when(step == pl.num_programs(0) - 1)
    def _():
        out_ref[...] = tile_of((8, 128), [(0, n, total(sums[n])) for n in range(9)])
        for n, (source, target) in enumerate(pairs):
            pltpu.make_async_copy(source, target, sems.at[n]).wait()


def wave_kernel(in_ref, stat_ref, sums_ref, g2, g3, base_ref, out_ref, scal_ref, tail_ref, sems):
    owner = lax.axis_index("grid")
    fetch = begin(base_ref.at[:, pl.ds(32, 8), :], tail_ref, sems.at[0])
    s0 = in_ref[pl.ds(0, points, stride=planes), :]
    s1 = in_ref[pl.ds(1, points, stride=planes), :]
    weight = s0[:, 120:121]
    whole = jnp.sum(weight, axis=0, keepdims=True)
    lane = lane_of((points, 128))
    coef = jnp.zeros((points, 128), f32)
    alpha, start = [], []
    for p in range(trials):
        mean = s0[:, 121 + p : 122 + p]
        a = jnp.sum(weight * mean, axis=0, keepdims=True) / whole
        off = a - mean
        spread_sum = jnp.sum(s1[:, 120 + p : 121 + p] + weight * off * off, axis=0, keepdims=True)
        alpha.append(a)
        start.append(spread_sum / planes)
        coef = jnp.where((lane >= p * half) & (lane < (p + 1) * half), off, coef)

    def source_of(r):
        d = in_ref[pl.ds(r, points, stride=planes), :]
        o = jnp.where((lane >= 96) & (lane < 120), d, 0.0)
        o = pltpu.roll(o, 32, 1)
        o = o + pltpu.roll(o, 24, 1)
        o = o + pltpu.roll(o, 48, 1)
        return jnp.where(lane < 96, coef * o - d, 0.0)

    wide = (2 * half, 128)
    m = row_of(wide) - half
    k = lane_of(wide)
    k = k - jnp.where(k >= 72, 72, jnp.where(k >= 48, 48, jnp.where(k >= 24, 24, 0)))
    doubled = jnp.where(k == 0, 1.0, 2.0) * (prefactor / float(points**3))
    energy = jnp.zeros((1, 128), f32)
    own = [jnp.where(lane_of((1, 128)) == 0, 0.0, 0.0)]
    for pair in (2, 1, 0):
        parts = [
            jnp.concatenate([source_of(2 * (2 * pair + i) + c) for i in range(2)], axis=1)
            for c in range(2)
        ]
        u = left_table(g2, jnp.concatenate(parts, axis=0))
        weights = []
        for i in range(2):
            j = owner * 6 + (2 * pair + i) - half
            square = m * m + k * k + j * j
            weights.append(jnp.where(square < half * half, doubled * square.astype(f32), 0.0))
        w = jnp.concatenate(weights, axis=1)
        t = u * jnp.concatenate([w, w], axis=0)
        product = jnp.sum(u * t, axis=0, keepdims=True)
        energy = energy + product[:, :128] + product[:, 128:]
        e = left_table(g3, t)
        if pair == 0:
            l1 = lane_of((1, 128))
            ride = jnp.zeros((1, 128), f32)
            entries = []
            for p in range(trials):
                kinetic = jnp.sum(jnp.where((l1 >= p * half) & (l1 < (p + 1) * half), energy, 0.0), axis=1, keepdims=True)
                off = alpha[p] - stat_ref[0:1, 1 + p : 2 + p]
                at_p = sums_ref[0:1, 5 + p : 6 + p] - 2.0 * off * sums_ref[0:1, 1 + p : 2 + p] + off * off * sums_ref[0:1, 0:1]
                ride = jnp.where(l1 == 96 + p, kinetic + at_p, ride)
                entries += [(0, p, alpha[p]), (0, 4 + p, start[p])]
            scal_ref[...] = tile_of((8, 128), entries)
            e = e + jnp.concatenate([ride, jnp.zeros((1, 128), f32)], axis=1)
        for i in range(2):
            for c in range(2):
                out_ref[pl.ds(2 * (2 * pair + i) + c, points, stride=planes), :] = (
                    e[c * points : (c + 1) * points, i * 128 : i * 128 + 128]
                )
    fetch.wait()


def step_kernel(in_ref, scal_ref, tail_ref, base_ref, step_ref, out_ref, tail, sems):
    shares = jnp.sum(in_ref[pl.ds(0, groups, stride=chunk), :], axis=0, keepdims=True)
    lane = lane_of((1, 128))
    start = jnp.where((lane >= 4) & (lane < 8), scal_ref[0:1, :], 0.0)
    curvature = pltpu.roll(jnp.where((lane >= 96) & (lane < 100), shares, 0.0), 36, 1)
    step = start / jnp.where((lane >= 4) & (lane < 8), curvature, 1.0)
    row = jnp.where(lane < 8, scal_ref[0:1, :], 0.0) + pltpu.roll(step, 4, 1)
    step_ref[...] = jnp.broadcast_to(row, (8, 128))
    last = jnp.where(row_of((8, 128)) == 4, row, 0.0)
    for v in range(bands):
        tail[v, :, :] = tail_ref[v, :, :] + last
    begin(tail, out_ref.at[:, pl.ds(32, 8), :], sems.at[0]).wait()


def image_kernel(energy_ref, in_ref, step_ref, field_far, o_far, g4, w2,
                 response_ref, residual_ref, norm_ref,
                 field_ref, o_ref, real, imag, mixed_s, mixed_r, flat_s, flat_r, sems, out_sems):
    energy = energy_ref[0]
    copies = [begin(field_far, field_ref, sems.at[0]), begin(o_far, o_ref, sems.at[1])]
    alpha = [step_ref[0:1, p : p + 1] for p in range(trials)]
    step = [step_ref[0:1, 8 + p : 9 + p] for p in range(trials)]
    for x in range(0, planes, 2):
        b = jnp.concatenate(
            [
                jnp.concatenate(
                    [in_ref[pl.ds((x + i) * 12 + r, groups, stride=chunk), :] for r in range(12)], axis=0
                )
                for i in range(2)
            ],
            axis=1,
        )
        v = left_table(g4, b)
        for i in range(2):
            real[pl.ds(x + i, points, stride=planes), :] = v[:points, i * 128 : i * 128 + 128]
            imag[pl.ds(x + i, points, stride=planes), :] = v[points:, i * 128 : i * 128 + 128]
    for copy in copies:
        copy.wait()
    size = 96
    mixed = planes * trials
    lane = lane_of((mixed, 128))

    def tiles(ref, q):
        c = [ref[(4 * q + i) * mixed : (4 * q + i + 1) * mixed, :] for i in range(4)]
        r1, r2, r3 = pltpu.roll(c[1], 96, 1), pltpu.roll(c[2], 64, 1), pltpu.roll(c[3], 32, 1)
        return jnp.where(lane < 96, c[0], r1), jnp.where(lane < 64, r1, r2), jnp.where(lane < 32, r2, r3)

    def back(i, sums):
        at = pl.ds(pl.multiple_of(i * size, size), size)
        vh, vl = split(jnp.concatenate([real[at, :], imag[at, :]], axis=1))
        kinetic = right_table(vh, vl, w2)
        o = o_ref[at, :]
        shift = field_ref[4, at, :] - energy
        out = []
        for p in range(trials):
            source = (alpha[p] - field_ref[p, at, :]) * o
            image = kinetic[:, p * 128 : p * 128 + 128] + shift * source
            residual = source - step[p] * image
            there = pl.ds(p, size, stride=trials)
            mixed_s[there, :] = step[p] * source
            mixed_r[there, :] = residual
            out.append(sums[p] + fold(residual * residual))
        for flat, ref in ((flat_s, mixed_s), (flat_r, mixed_r)):
            for q in range(2):
                for n, tile in enumerate(tiles(ref, q)):
                    flat[i, :, :, 384 * q + 128 * n : 384 * q + 128 * n + 128] = tile.reshape(planes, trials, 128)
        cells = pl.ds(pl.multiple_of(i * 768, 768), 768)
        begin(flat_s.at[i], response_ref.at[:, :, cells], out_sems.at[0, i])
        begin(flat_r.at[i], residual_ref.at[:, :, cells], out_sems.at[1, i])
        return tuple(out)

    sums = lax.fori_loop(0, rows // size, back, tuple(jnp.zeros((8, 128), f32) for _ in range(trials)))
    norm_ref[...] = tile_of((8, 128), [(0, p, total(s)) for p, s in enumerate(sums)])
    for i in range(rows // size):
        cells = pl.ds(i * 768, 768)
        pltpu.make_async_copy(flat_s.at[i], response_ref.at[:, :, cells], out_sems.at[0, i]).wait()
        pltpu.make_async_copy(flat_r.at[i], residual_ref.at[:, :, cells], out_sems.at[1, i]).wait()


def last_kernel(step_ref, n0, n1, n2, n3, n4, n5, n6, n7, packed_far, band_ref, response_ref, residual_ref,
                direction_ref, density_ref, packed_ref, bands_in, first, second, result, sems, out_sems):
    parts = 6
    width = points * points // parts
    arrival = begin(band_ref, bands_in, sems.at[2, 0])
    kept = begin(packed_far, packed_ref, sems.at[2, 1])
    loads = []
    for i in range(parts):
        cells = pl.ds(i * width, width)
        loads.append((begin(response_ref.at[:, :, cells], first.at[i], sems.at[0, i]),
                      begin(residual_ref.at[:, :, cells], second.at[i], sems.at[1, i])))
    new = n0[0:1, :]
    for part in (n1, n2, n3, n4, n5, n6, n7):
        new = new + part[0:1, :]
    ratio = [new[:, p : p + 1] / step_ref[0:1, 4 + p : 5 + p] / step_ref[0:1, 8 + p : 9 + p] for p in range(trials)]
    r = row_of((trials, 128))
    ratios = jnp.zeros((trials, 128), f32)
    for p in range(trials):
        ratios = jnp.where(r == p, ratio[p], ratios)
    ratios = ratios[:, 0:1][None]
    stores = []
    for i in range(parts):
        for copy in loads[i]:
            copy.wait()
        result[i, :, :, :] = second[i] + ratios * first[i]
        stores.append(begin(result.at[i], direction_ref.at[:, :, pl.ds(i * width, width)], out_sems.at[i]))
    arrival.wait()
    kept.wait()
    blocks = [packed_ref[q * 36 : q * 36 + 36, :] for q in range(3)]
    fields = [*blocks, unpack_last(*blocks)]
    sums = [jnp.zeros((36, 128), f32) for _ in range(trials)]
    for v in range(bands):
        square = bands_in[v, 0:36, :]
        square = square * square
        for p in range(trials):
            alpha, step = bands_in[v, 36:37, p : p + 1], bands_in[v, 36:37, 8 + p : 9 + p]
            sums[p] = sums[p] + (step * (alpha - fields[p])) * square
    lane = lane_of((planes, 128))
    for p in range(trials):
        c = [sums[p][12 * i : 12 * i + 12] * (4.0 / bands) for i in range(3)]
        r1, r2 = pltpu.roll(c[1], 96, 1), pltpu.roll(c[2], 64, 1)
        density_ref[:, p, 0:128] = jnp.where(lane < 96, c[0], r1)
        density_ref[:, p, 128:256] = jnp.where(lane < 64, r1, r2)
        density_ref[:, p, 256:288] = r2[:, 0:32]
    for copy in stores:
        copy.wait()


vmem = pl.BlockSpec(memory_space=pltpu.VMEM)
smem = pl.BlockSpec(memory_space=pltpu.SMEM)
hbm = pl.BlockSpec(memory_space=pl.ANY)
far = pl.BlockSpec(memory_space=pltpu.HBM)


BIG = 56000000
HUGE = 60000000


def shape(*dims, dtype=f32):
    return jax.ShapeDtypeStruct(dims, dtype)


def call(kernel, ins, outs, scratch=(), name=None, room=4 * 2**20, places=None, aliases=None, flops=10**6):
    return pl.pallas_call(
        kernel, out_shape=outs, in_specs=ins,
        out_specs=places if places is not None else jax.tree.map(lambda _: vmem, outs),
        scratch_shapes=scratch, compiler_params=pltpu.CompilerParams(vmem_limit_bytes=room), name=name, input_output_aliases=aliases or {},
        cost_estimate=pl.CostEstimate(flops=flops, bytes_accessed=10**6, transcendentals=0),
    )


def pack(trial, local):
    return call(pack_kernel, [vmem] * 2, shape(144, 128), name="pack")(jnp.transpose(trial, (1, 0, 2)), local)


def orbital_rows(orbitals, packed):
    return call(
        orbital_kernel, [vmem, vmem],
        (shape(rows, 128), shape(bands, 40, 128), shape(144, 128)),
        [buffer(rows, 128), buffer(bands, 40, 128), pltpu.SemaphoreType.DMA((3,))],
        name="orbital_rows", places=(far, far, far), room=BIG,
    )(orbitals, packed)


def buffer(*dims, dtype=f32):
    return pltpu.VMEM(dims, dtype)


def forward(pieces, o, tables):
    return call(
        forward_kernel, [far] * 11,
        (shape(5, rows, 128), shape(rows, 128), shape(8, 128)),
        [buffer(rows, 128), buffer(5, rows, 128), buffer(bands, 144, 128), buffer(2, 640, 256, dtype=bf16), buffer(2, 96, 192, dtype=bf16), buffer(rows, 128),
         buffer(rows, 640, dtype=bf16), buffer(rows, 640, dtype=bf16), buffer(rows, 128), buffer(rows, 128),
         pltpu.SemaphoreType.DMA((11,))],
        name="forward", room=HUGE, places=(far, far, vmem),
    )(*pieces, o, tables["w1"], tables["g1"])


def local_sums(energies, fields, o, stat, tables):
    size, count = 192, rows // 192
    tile = pl.BlockSpec((8, 128), lambda i: (0, 0))
    kinds = [tables[name] for name in ("g2", "g3", "g4", "w2")]
    return pl.pallas_call(
        local_kernel, grid=(count,),
        in_specs=[smem, pl.BlockSpec((5, size, 128), lambda i: (0, i, 0)), pl.BlockSpec((size, 128), lambda i: (i, 0)),
                  tile] + [far] * 4,
        out_specs=(tile, *[vmem] * 4),
        out_shape=(shape(8, 128), *[shape(*t.shape, dtype=bf16) for t in kinds]),
        scratch_shapes=[buffer(9, 8, 128), pltpu.SemaphoreType.DMA((4,))],
        compiler_params=pltpu.CompilerParams(vmem_limit_bytes=BIG), name="local_sums",
        cost_estimate=pl.CostEstimate(flops=10**7, bytes_accessed=10**7, transcendentals=0),
    )(energies, fields, o, stat, *kinds)


def waves(arrived, stat, sums, g2, g3, base):
    return call(
        wave_kernel, [vmem] * 5 + [far], (shape(rows, 128), shape(8, 128), shape(bands, 8, 128)),
        [pltpu.SemaphoreType.DMA((1,))], name="waves", room=8 * 2**20,
    )(arrived, stat, sums, g2, g3, base)


def steps(arrived, scal, tail, base):
    return call(
        step_kernel, [vmem] * 3 + [far], (shape(8, 128), shape(bands, 40, 128)),
        [buffer(bands, 8, 128), pltpu.SemaphoreType.DMA((1,))],
        name="steps", places=(vmem, far), aliases={3: 1},
    )(arrived, scal, tail, base)


def image(energies, arrived, step, fields, o, g4, w2):
    cells = shape(planes, trials, points * points)
    return call(
        image_kernel, [smem, vmem, vmem, far, far, vmem, vmem], (cells, cells, shape(8, 128)),
        [buffer(5, rows, 128), buffer(rows, 128), buffer(rows, 128), buffer(rows, 128),
         buffer(384, 128), buffer(384, 128),
         buffer(12, planes, trials, 768), buffer(12, planes, trials, 768),
         pltpu.SemaphoreType.DMA((2,)), pltpu.SemaphoreType.DMA((2, 12))],
        name="image", room=BIG, places=(far, far, vmem), flops=2 * 10**10,
    )(energies, arrived, step, fields, o, g4, w2)


def last(step, norms, packed, band, response, residual):
    cells = shape(planes, trials, points * points)
    part = buffer(6, planes, trials, points * points // 6)
    return call(
        last_kernel, [vmem] * 9 + [far] * 4, (cells, shape(planes, trials, 288)),
        [buffer(144, 128), buffer(bands, 40, 128), part, part, part, pltpu.SemaphoreType.DMA((3, 6)), pltpu.SemaphoreType.DMA((6,))],
        name="last", room=BIG, places=(far, vmem),
    )(step, *norms, packed, band, response, residual)


def outward(value):
    return jnp.transpose(value, (1, 0, 2))


def swapped(value, axis, size, mask):
    return lax.ppermute(value, axis, [(s, s ^ mask) for s in range(size)])


def gather_rows(packed):
    value = packed[None]
    return jnp.concatenate([value] + [swapped(value, "band", bands, m) for m in (8, 16, 24)], axis=0)


def gather_planes(quad):
    quads = [quad] + [swapped(quad, "band", bands, m) for m in (2, 4, 6)]
    return quads + [swapped(q, "band", bands, 1) for q in quads]


def on_device(orbitals, energies, local_pot, trial_pot):
    tables = {name: jnp.asarray(table) for name, table in build_tables().items()}
    packed = pack(trial_pot, local_pot)
    quad = gather_rows(packed)
    o_far, base, packed_far = orbital_rows(orbitals, packed)
    quad, o_far = lax.optimization_barrier((quad, o_far))
    pieces = gather_planes(quad)
    fields, sent, stat = forward(pieces, o_far, tables)
    arrived = lax.all_to_all(sent.reshape(groups, chunk, 128), "grid", 0, 0, tiled=True).reshape(rows, 128)
    sums, g2, g3, g4, w2 = local_sums(energies, fields, o_far, stat, tables)
    back, scal, tail = waves(arrived, stat, sums, g2, g3, base)
    back = lax.all_to_all(back.reshape(groups, chunk, 128), "grid", 0, 0, tiled=True).reshape(rows, 128)
    step, payload = steps(back, scal, tail, base)
    band = lax.all_to_all(payload, "band", 0, 0, tiled=True)
    response, residual, norm = image(energies, back, step, fields, o_far, g4, w2)
    norms = [norm] + [swapped(norm, "grid", groups, m) for m in range(1, groups)]
    direction, density = last(step, norms, packed_far, band, response, residual)
    return outward(response)[None], outward(residual)[None], outward(direction)[None], outward(density)


def solution(mesh):
    return jax.shard_map(
        on_device,
        mesh=mesh,
        in_specs=(P("band", "grid", None), P("band"), P("grid", "band"), P(None, "grid", "band")),
        out_specs=(
            P("band", None, "grid", None),
            P("band", None, "grid", None),
            P("band", None, "grid", None),
            P(None, "grid", "band"),
        ),
        check_vma=False,
    )
```

time: 152 us -> 114 us (0.75)
  local copies, waits for them, and re-layouts: 39.7 us -> 6.08 us
  waiting for transfers between devices: 42.3 us -> 18.8 us
  Pallas kernels: 17.8 us -> 30.5 us
  blocking collectives: 8.35 us -> 13.1 us
    unnamed x66 -> x33, local copies, waits for them, and re-layouts: 36.8 us -> 6.08 us
    all_to_all x3 -> x1, waiting for transfers between devices: 16 us -> 1 us  [on_device(): band = lax.all_to_all(payload, 'band', 0, 0, tiled=True)]
    pallas_call x9 -> x8, Pallas kernels: 17.8 us -> 30.5 us  [the longest x1 8.72 us: image(): call(image_kernel, [smem, vmem, vmem, far, far, vmem, vmem], (cells, cell...]
    ppermute x7 -> x17, starting transfers between devices: 15.6 us -> 27.4 us  [swapped(): return lax.ppermute(value, axis, [(s, s ^ mask) for s in range(size)])]
    all_to_all x3 -> x1, starting transfers between devices: 21.3 us -> 10.9 us  [on_device(): band = lax.all_to_all(payload, 'band', 0, 0, tiled=True)]
    all_to_all x1, blocking collectives: 8.35 us -> 13.1 us  [on_device(): lax.all_to_all(back.reshape(groups, chunk, 128), 'grid', 0, 0, tiled=True)]
    ppermute x7 -> x17, waiting for transfers between devices: 18.9 us -> 14.6 us  [swapped(): return lax.ppermute(value, axis, [(s, s ^ mask) for s in range(size)])]
    all_to_all x1, waiting for transfers between devices: 7.39 us -> 3.2 us  [on_device(): lax.all_to_all(sent.reshape(groups, chunk, 128), 'grid', 0, 0, tiled=True)]
  transfers between devices with their start and end apart: 11 -> 19, of which waited for: 9 -> 10; matrix products, arithmetic and copies ran while one was open for 8% -> 2% of each run, Pallas kernels for 6% -> 15%
where the time goes in v3:
time: 114 us; the launch traced here: 112 us
  starting transfers between devices  42.4 us (37%)
  Pallas kernels  30.5 us (27%)
  waiting for transfers between devices  18.8 us (16%)
  blocking collectives  13.1 us (11%)
  local copies, waits for them, and re-layouts  6.08 us (5%)
  between operations  1.63 us (1%)
    ppermute x17, starting transfers between devices, swapped(): return lax.ppermute(value, axis, [(s, s ^ mask) for s in range(size)])  27.4 us
    ppermute x17, waiting for transfers between devices, swapped(): return lax.ppermute(value, axis, [(s, s ^ mask) for s in range(size)])  14.6 us
    all_to_all x1, blocking collectives, on_device(): lax.all_to_all(back.reshape(groups, chunk, 128), 'grid', 0, 0, tiled=True)  13.1 us
    all_to_all x1, starting transfers between devices, on_device(): band = lax.all_to_all(payload, 'band', 0, 0, tiled=True)  10.9 us
    pallas_call x1, Pallas kernels, image(): call(image_kernel, [smem, vmem, vmem, far, far, vmem, vmem], (cells, cell...  8.72 us
    pallas_call x1, Pallas kernels, forward(): call(forward_kernel, [far] * 11, (shape(5, rows, 128), shape(rows, 128),...  7.2 us
    unnamed x33, local copies, waits for them, and re-layouts  6.08 us
    pallas_call x1, Pallas kernels, local_sums(): pl.pallas_call(local_kernel, grid=(count,), in_specs=[smem, pl.BlockSpec(...  5.34 us
  transfers between devices with their start and end apart: 19, of which 10 were waited for; matrix products, arithmetic and copies ran while one was open for 2% of the time, Pallas kernels for 15%

profile of v3, /device:TPU:1, one launch (start us, length us, event | category | flops | bytes accessed | tf_op | source)
XLA Modules:
  0.0 112.5 jit_solution(4819180765052100397)
XLA Ops:
  0.6 0.0 copy-start.3
  0.6 0.9 copy-done.3
  1.5 0.7 copy-done.4
  2.3 0.2 pack.1.packed_ref
  2.4 6.9 %collective-permute-start.2 = (f32[1,144,128]{2,1,0:T(8,128)S(1)}, f32[1,144,128]{2,1,0:T(8,128)S(1)}, u32[]{:S(2)}, u32[]{:S(2)}) collective-permute-start(f32[1,144,128]{2,1,0:T(8,128)S(1)} %bitcast.19), channel_id=1, source_target_pairs={{0,192},{8,200},{16,208},{24,216},{32,224},{40,232},{48,240},{56,2... | collective-permute-start | bytes 221192 | tf_op jit(solution)/shard_map/ppermute | solution.py:582
  9.4 1.0 collective-permute-start.1
  10.3 1.2 %collective-permute-start = (f32[1,144,128]{2,1,0:T(8,128)S(1)}, f32[1,144,128]{2,1,0:T(8,128)S(1)}, u32[]{:S(2)}, u32[]{:S(2)}) collective-permute-start(f32[1,144,128]{2,1,0:T(8,128)S(1)} %bitcast.21), channel_id=1, source_target_pairs={{0,64},{8,72},{16,80},{24,88},{32,96},{40,104},{48,112},{56,120},{... | collective-permute-start | bytes 221192 | tf_op jit(solution)/shard_map/ppermute | solution.py:582
  11.5 1.9 %copy.15.o_ref = f32[1,12,9216]{2,1,0:T(8,128)} copy(f32[1,12,9216]{2,0,1:T(1,128)} %param.10) | data formatting | bytes 884736 | tf_op args[0]
  13.5 2.5 %orbital_rows.1 = (f32[1152,128]{1,0:T(8,128)}, f32[32,40,128]{2,1,0:T(8,128)}, f32[144,128]{1,0:T(8,128)S(1)}) custom-call(f32[1,12,9216]{2,1,0:T(8,128)} %copy.15.o_ref, f32[144,128]{1,0:T(8,128)S(1)} %pack.1.packed_ref), custom_call_target="tpu_custom_call" | custom-call | flops 1000000 | bytes 1000000 | tf_op jit(solution)/shard_map/orbital_rows/pallas_call | solution.py:501
  15.9 0.0 collective-permute-done.2
  15.9 1.0 collective-permute-done.1
  17.0 1.7 %collective-permute-done = f32[1,144,128]{2,1,0:T(8,128)S(1)} collective-permute-done((f32[1,144,128]{2,1,0:T(8,128)S(1)}, f32[1,144,128]{2,1,0:T(8,128)S(1)}, u32[]{:S(2)}, u32[]{:S(2)}) %collective-permute-start) | collective-permute-done | bytes 73760 | tf_op jit(solution)/shard_map/ppermute | solution.py:582
  18.7 0.0 copy-start.8
  18.7 0.0 copy-start.1
  18.7 0.0 copy-start.2
  18.7 2.8 %collective-permute-start.5 = (f32[4,144,128]{2,1,0:T(8,128)S(1)}, f32[4,144,128]{2,1,0:T(8,128)S(1)}, u32[]{:S(2)}, u32[]{:S(2)}) collective-permute-start(f32[4,144,128]{2,1,0:T(8,128)S(1)} %pad_maximum_fusion.p0), channel_id=1, source_target_pairs={{0,48},{8,56},{16,32},{24,40},{32,16},{40,24},{48,0},{56,8},{64,11... | collective-permute-start | bytes 884744 | tf_op jit(solution)/shard_map/ppermute | solution.py:582
  21.5 0.3 collective-permute-start.4
  21.9 0.3 collective-permute-start.3
  22.2 3.1 %collective-permute-start.6 = (f32[4,144,128]{2,1,0:T(8,128)S(1)}, f32[4,144,128]{2,1,0:T(8,128)S(1)}, u32[]{:S(2)}, u32[]{:S(2)}) collective-permute-start(f32[4,144,128]{2,1,0:T(8,128)S(1)} %pad_maximum_fusion.p0), channel_id=1, source_target_pairs={{0,8},{8,0},{16,24},{24,16},{32,40},{40,32},{48,56},{56,48},{64,72... | collective-permute-start | bytes 884744 | tf_op jit(solution)/shard_map/ppermute | solution.py:582
  25.3 8.8 %collective-permute-done.5.p3 = f32[4,144,128]{2,1,0:T(8,128)S(1)} collective-permute-done((f32[4,144,128]{2,1,0:T(8,128)S(1)}, f32[4,144,128]{2,1,0:T(8,128)S(1)}, u32[]{:S(2)}, u32[]{:S(2)}) %collective-permute-start.5) | collective-permute-done | bytes 294944 | tf_op jit(solution)/shard_map/ppermute | solution.py:582
  34.1 1.7 %collective-permute-start.9 = (f32[4,144,128]{2,1,0:T(8,128)S(1)}, f32[4,144,128]{2,1,0:T(8,128)S(1)}, u32[]{:S(2)}, u32[]{:S(2)}) collective-permute-start(f32[4,144,128]{2,1,0:T(8,128)S(1)} %collective-permute-done.5.p3), channel_id=1, source_target_pairs={{0,8},{8,0},{16,24},{24,16},{32,40},{40,32},{48,56},{56,48},{64,72... | collective-permute-start | bytes 884744 | tf_op jit(solution)/shard_map/ppermute | solution.py:582
  35.8 0.0 collective-permute-done.4.p2
  35.8 0.1 collective-permute-start.8
  35.9 0.0 collective-permute-done.3.p1
  35.9 0.6 collective-permute-start.7
  36.5 0.0 collective-permute-done.6.p4
  36.5 0.5 collective-permute-done.9.p7
  37.0 0.4 collective-permute-done.8.p6
  37.4 0.4 collective-permute-done.7.p5
  37.9 0.0 copy-done.8
  37.9 0.0 copy-done.9
  37.9 0.0 copy-done.11
  37.9 0.3 copy-done.14
  38.2 0.7 copy-done.15
  38.9 7.2 %forward.1 = (f32[5,1152,128]{2,1,0:T(8,128)}, f32[1152,128]{1,0:T(8,128)}, f32[8,128]{1,0:T(8,128)}) custom-call(f32[4,144,128]{2,1,0:T(8,128)} %copy-done.8, f32[4,144,128]{2,1,0:T(8,128)} %copy-done.11, f32[4,144,128]{2,1,0:T(8,128)} %copy-done.10, f32[4,144,128]{2,1,0:T(8,128)} %copy-done.9, f32[4,144,128]{2,1,0:T(8,128)} %copy-done.12, ...), custom_call_target="tpu_custom_call" | custom-call | flops 1000000 | bytes 1000000 | tf_op jit(solution)/shard_map/forward/pallas_call | solution.py:514
  46.1 4.0 %all-to-all-start = ((f32[8,144,128]{2,1,0:T(8,128)}), f32[8,144,128]{2,1,0:T(8,128)S(1)}, u32[]{:S(2)}, u32[]{:S(2)}) async-start(f32[8,144,128]{2,1,0:T(8,128)} %bitcast.27), calls=%async_computation | async-start | bytes 1179648 | tf_op jit(solution)/shard_map/all_to_all | solution.py:603
  50.8 0.0 copy-done.1
  50.8 0.0 copy-done.2
  50.8 0.0 copy-start.5
  50.8 0.7 copy-done.5
  51.5 5.3 %local_sums.1 = (f32[8,128]{1,0:T(8,128)S(1)}, bf16[2,96,192]{2,1,0:T(8,128)(2,1)S(1)}, bf16[2,192,96]{2,1,0:T(8,128)(2,1)S(1)}, bf16[2,192,96]{2,1,0:T(8,128)(2,1)S(1)}, bf16[2,256,512]{2,1,0:T(8,128)(2,1)}) custom-call(f32[1]{0:T(128)S(6)} %copy.17.energy_ref, f32[5,1152,128]{2,1,0:T(8,128)} %get-tuple-element.32.field_ref.field_far, ...), custom_call_target="tpu_custom_call" | custom-call | flops 10000000 | bytes 10000000 | tf_op jit(solution)/shard_map/local_sums/pallas_call | solution.py:528
  56.8 3.2 %all-to-all-done = f32[8,144,128]{2,1,0:T(8,128)S(1)} async-done(((f32[8,144,128]{2,1,0:T(8,128)}), f32[8,144,128]{2,1,0:T(8,128)S(1)}, u32[]{:S(2)}, u32[]{:S(2)}) %all-to-all-start) | async-done | bytes 589856 | tf_op jit(solution)/shard_map/all_to_all | solution.py:603
  60.0 2.0 %waves.1 = (f32[1152,128]{1,0:T(8,128)S(1)}, f32[8,128]{1,0:T(8,128)S(1)}, f32[32,8,128]{2,1,0:T(8,128)S(1)}) custom-call(f32[1152,128]{1,0:T(8,128)S(1)} %bitcast.16, f32[8,128]{1,0:T(8,128)S(1)} %copy-done.6, f32[8,128]{1,0:T(8,128)S(1)} %get-tuple-element.33.sums_ref, bf16[2,96,192]{2,1,0:T(8,128)(2,1)S(1)} %get-tuple-element.34.g2, ...), custom_call_target="tpu_custom_call" | custom-call | flops 1000000 | bytes 1000000 | tf_op jit(solution)/shard_map/waves/pallas_call | solution.py:541
  62.0 13.1 %all_to_all.15 = f32[8,144,128]{2,1,0:T(8,128)S(1)} all-to-all(f32[8,144,128]{2,1,0:T(8,128)S(1)} %bitcast.23), channel_id=1, replica_groups=mesh['band'=32,'grid'=8] {'grid'}, dimensions={0} | all-to-all | bytes 1179648 | tf_op jit(solution)/shard_map/all_to_all | solution.py:606
  75.2 0.9 steps.1
  76.0 10.9 %all-to-all-start.2 = ((f32[32,40,128]{2,1,0:T(8,128)}), f32[32,40,128]{2,1,0:T(8,128)S(1)}, u32[]{:S(2)}, u32[]{:S(2)}) async-start(f32[32,40,128]{2,1,0:T(8,128)} %get-tuple-element.47), calls=%async_computation.2 | async-start | bytes 1310720 | tf_op jit(solution)/shard_map/all_to_all | solution.py:608
  87.0 8.7 %image.1 = (f32[12,4,9216]{2,1,0:T(4,128)}, f32[12,4,9216]{2,1,0:T(4,128)}, f32[8,128]{1,0:T(8,128)S(1)}) custom-call(f32[1]{0:T(128)S(6)} %copy.17.energy_ref, f32[1152,128]{1,0:T(8,128)} %bitcast.18, f32[8,128]{1,0:T(8,128)S(1)} %get-tuple-element.40.step_ref, f32[5,1152,128]{2,1,0:T(8,128)} %get-tuple-element.32.field_ref.field_far, ...), custom_call_target="tpu_custom_call" | custom-call | flops 20000000000 | bytes 1000000 | tf_op jit(solution)/shard_map/image/pallas_call | solution.py:557
  95.7 1.1 %collective-permute-start.16 = (f32[8,128]{1,0:T(8,128)S(1)}, f32[8,128]{1,0:T(8,128)S(1)}, u32[]{:S(2)}, u32[]{:S(2)}) collective-permute-start(f32[8,128]{1,0:T(8,128)S(1)} %get-tuple-element.45.n0), channel_id=1, source_target_pairs={{0,7},{1,6},{2,5},{3,4},{4,3},{5,2},{6,1},{7,0},{8,15},{9,14},{10,... | collective-permute-start | bytes 12296 | tf_op jit(solution)/shard_map/ppermute | solution.py:582
  96.8 1.8 %collective-permute-start.15 = (f32[8,128]{1,0:T(8,128)S(1)}, f32[8,128]{1,0:T(8,128)S(1)}, u32[]{:S(2)}, u32[]{:S(2)}) collective-permute-start(f32[8,128]{1,0:T(8,128)S(1)} %get-tuple-element.45.n0), channel_id=1, source_target_pairs={{0,6},{1,7},{2,4},{3,5},{4,2},{5,3},{6,0},{7,1},{8,14},{9,15},{10,... | collective-permute-start | bytes 12296 | tf_op jit(solution)/shard_map/ppermute | solution.py:582
  98.6 0.5 collective-permute-start.14
  99.2 3.2 %collective-permute-start.13 = (f32[8,128]{1,0:T(8,128)S(1)}, f32[8,128]{1,0:T(8,128)S(1)}, u32[]{:S(2)}, u32[]{:S(2)}) collective-permute-start(f32[8,128]{1,0:T(8,128)S(1)} %get-tuple-element.45.n0), channel_id=1, source_target_pairs={{0,4},{1,5},{2,6},{3,7},{4,0},{5,1},{6,2},{7,3},{8,12},{9,13},{10,... | collective-permute-start | bytes 12296 | tf_op jit(solution)/shard_map/ppermute | solution.py:582
  102.3 0.0 collective-permute-start.12
  102.4 0.0 collective-permute-done.16.n7
  102.4 1.6 %collective-permute-start.11 = (f32[8,128]{1,0:T(8,128)S(1)}, f32[8,128]{1,0:T(8,128)S(1)}, u32[]{:S(2)}, u32[]{:S(2)}) collective-permute-start(f32[8,128]{1,0:T(8,128)S(1)} %get-tuple-element.45.n0), channel_id=1, source_target_pairs={{0,2},{1,3},{2,0},{3,1},{4,6},{5,7},{6,4},{7,5},{8,10},{9,11},{10,... | collective-permute-start | bytes 12296 | tf_op jit(solution)/shard_map/ppermute | solution.py:582
  104.0 0.0 collective-permute-done.15.n6
  104.0 1.0 collective-permute-start.10
  105.0 0.0 collective-permute-done.14.n5
  105.0 0.0 collective-permute-done.13.n4
  105.0 1.0 collective-permute-done.12.n3
  106.0 0.0 collective-permute-done.11.n2
  106.0 0.7 collective-permute-done.10.n1
  106.7 1.0 all-to-all-done.2.band_ref
  107.7 0.8 copy-done.7
  108.6 3.8 %last.1 = (f32[12,4,9216]{2,1,0:T(4,128)}, f32[12,4,288]{2,1,0:T(4,128)}) custom-call(f32[8,128]{1,0:T(8,128)S(1)} %get-tuple-element.40.step_ref, f32[8,128]{1,0:T(8,128)S(1)} %get-tuple-element.45.n0, f32[8,128]{1,0:T(8,128)S(1)} %collective-permute-done.10.n1, f32[8,128]{1,0:T(8,128)S(1)} %collective-permute-done.11.n2, ...), custom_call_target="tpu_custom_call" | custom-call | flops 1000000 | bytes 1000000 | tf_op jit(solution)/shard_map/last/pallas_call | solution.py:570
  (17 shorter events, 0.0 us)
Async XLA Ops:
  0.6 0.9 copy-start.3
  1.5 0.7 copy-start.4
  2.4 13.5 %collective-permute-start.2 = (f32[1,144,128]{2,1,0:T(8,128)S(1)}, f32[1,144,128]{2,1,0:T(8,128)S(1)}, u32[]{:S(2)}, u32[]{:S(2)}) collective-permute-start(f32[1,144,128]{2,1,0:T(8,128)S(1)} %bitcast.19), channel_id=1, source_target_pairs={{0,192},{8,200},{16,208},{24,216},{32,224},{40,232},{48,240},{56,2... | collective-permute-start | bytes 221192 | tf_op jit(solution)/shard_map/ppermute | solution.py:582
  9.4 7.6 %collective-permute-start.1 = (f32[1,144,128]{2,1,0:T(8,128)S(1)}, f32[1,144,128]{2,1,0:T(8,128)S(1)}, u32[]{:S(2)}, u32[]{:S(2)}) collective-permute-start(f32[1,144,128]{2,1,0:T(8,128)S(1)} %bitcast.20), channel_id=1, source_target_pairs={{0,128},{8,136},{16,144},{24,152},{32,160},{40,168},{48,176},{56,1... | collective-permute-start | bytes 221192 | tf_op jit(solution)/shard_map/ppermute | solution.py:582
  10.3 8.3 %collective-permute-start = (f32[1,144,128]{2,1,0:T(8,128)S(1)}, f32[1,144,128]{2,1,0:T(8,128)S(1)}, u32[]{:S(2)}, u32[]{:S(2)}) collective-permute-start(f32[1,144,128]{2,1,0:T(8,128)S(1)} %bitcast.21), channel_id=1, source_target_pairs={{0,64},{8,72},{16,80},{24,88},{32,96},{40,104},{48,112},{56,120},{... | collective-permute-start | bytes 221192 | tf_op jit(solution)/shard_map/ppermute | solution.py:582
  18.7 19.2 %copy-start.8 = (f32[4,144,128]{2,1,0:T(8,128)}, f32[4,144,128]{2,1,0:T(8,128)S(1)}, u32[]{:S(2)}) copy-start(f32[4,144,128]{2,1,0:T(8,128)S(1)} %pad_maximum_fusion.p0) | copy-start | bytes 884740
  18.7 32.1 %copy-start.1 = (bf16[2,192,96]{2,1,0:T(8,128)(2,1)S(1)}, bf16[2,192,96]{2,1,0:T(8,128)(2,1)}, u32[]{:S(2)}) copy-start(bf16[2,192,96]{2,1,0:T(8,128)(2,1)} %constant.15.clone.g3_ref) | copy-start | bytes 221188
  18.7 32.1 %copy-start.2 = (bf16[2,96,192]{2,1,0:T(8,128)(2,1)S(1)}, bf16[2,96,192]{2,1,0:T(8,128)(2,1)}, u32[]{:S(2)}) copy-start(bf16[2,96,192]{2,1,0:T(8,128)(2,1)} %constant.14.clone.g2_ref) | copy-start | bytes 221188
  18.7 15.4 %collective-permute-start.5 = (f32[4,144,128]{2,1,0:T(8,128)S(1)}, f32[4,144,128]{2,1,0:T(8,128)S(1)}, u32[]{:S(2)}, u32[]{:S(2)}) collective-permute-start(f32[4,144,128]{2,1,0:T(8,128)S(1)} %pad_maximum_fusion.p0), channel_id=1, source_target_pairs={{0,48},{8,56},{16,32},{24,40},{32,16},{40,24},{48,0},{56,8},{64,11... | collective-permute-start | bytes 884744 | tf_op jit(solution)/shard_map/ppermute | solution.py:582
  21.5 14.3 %collective-permute-start.4 = (f32[4,144,128]{2,1,0:T(8,128)S(1)}, f32[4,144,128]{2,1,0:T(8,128)S(1)}, u32[]{:S(2)}, u32[]{:S(2)}) collective-permute-start(f32[4,144,128]{2,1,0:T(8,128)S(1)} %pad_maximum_fusion.p0), channel_id=1, source_target_pairs={{0,32},{8,40},{16,48},{24,56},{32,0},{40,8},{48,16},{56,24},{64,96... | collective-permute-start | bytes 884744 | tf_op jit(solution)/shard_map/ppermute | solution.py:582
  21.9 14.0 %collective-permute-start.3 = (f32[4,144,128]{2,1,0:T(8,128)S(1)}, f32[4,144,128]{2,1,0:T(8,128)S(1)}, u32[]{:S(2)}, u32[]{:S(2)}) collective-permute-start(f32[4,144,128]{2,1,0:T(8,128)S(1)} %pad_maximum_fusion.p0), channel_id=1, source_target_pairs={{0,16},{8,24},{16,0},{24,8},{32,48},{40,56},{48,32},{56,40},{64,80... | collective-permute-start | bytes 884744 | tf_op jit(solution)/shard_map/ppermute | solution.py:582
  22.2 14.3 %collective-permute-start.6 = (f32[4,144,128]{2,1,0:T(8,128)S(1)}, f32[4,144,128]{2,1,0:T(8,128)S(1)}, u32[]{:S(2)}, u32[]{:S(2)}) collective-permute-start(f32[4,144,128]{2,1,0:T(8,128)S(1)} %pad_maximum_fusion.p0), channel_id=1, source_target_pairs={{0,8},{8,0},{16,24},{24,16},{32,40},{40,32},{48,56},{56,48},{64,72... | collective-permute-start | bytes 884744 | tf_op jit(solution)/shard_map/ppermute | solution.py:582
  34.1 3.8 %copy-start.9 = (f32[4,144,128]{2,1,0:T(8,128)}, f32[4,144,128]{2,1,0:T(8,128)S(1)}, u32[]{:S(2)}) copy-start(f32[4,144,128]{2,1,0:T(8,128)S(1)} %collective-permute-done.5.p3) | copy-start | bytes 884740
  34.1 2.9 %collective-permute-start.9 = (f32[4,144,128]{2,1,0:T(8,128)S(1)}, f32[4,144,128]{2,1,0:T(8,128)S(1)}, u32[]{:S(2)}, u32[]{:S(2)}) collective-permute-start(f32[4,144,128]{2,1,0:T(8,128)S(1)} %collective-permute-done.5.p3), channel_id=1, source_target_pairs={{0,8},{8,0},{16,24},{24,16},{32,40},{40,32},{48,56},{56,48},{64,72... | collective-permute-start | bytes 884744 | tf_op jit(solution)/shard_map/ppermute | solution.py:582
  35.8 2.1 %copy-start.10 = (f32[4,144,128]{2,1,0:T(8,128)}, f32[4,144,128]{2,1,0:T(8,128)S(1)}, u32[]{:S(2)}) copy-start(f32[4,144,128]{2,1,0:T(8,128)S(1)} %collective-permute-done.4.p2) | copy-start | bytes 884740
  35.8 1.6 %collective-permute-start.8 = (f32[4,144,128]{2,1,0:T(8,128)S(1)}, f32[4,144,128]{2,1,0:T(8,128)S(1)}, u32[]{:S(2)}, u32[]{:S(2)}) collective-permute-start(f32[4,144,128]{2,1,0:T(8,128)S(1)} %collective-permute-done.4.p2), channel_id=1, source_target_pairs={{0,8},{8,0},{16,24},{24,16},{32,40},{40,32},{48,56},{56,48},{64,72... | collective-permute-start | bytes 884744 | tf_op jit(solution)/shard_map/ppermute | solution.py:582
  35.9 2.0 %copy-start.11 = (f32[4,144,128]{2,1,0:T(8,128)}, f32[4,144,128]{2,1,0:T(8,128)S(1)}, u32[]{:S(2)}) copy-start(f32[4,144,128]{2,1,0:T(8,128)S(1)} %collective-permute-done.3.p1) | copy-start | bytes 884740
  35.9 1.9 %collective-permute-start.7 = (f32[4,144,128]{2,1,0:T(8,128)S(1)}, f32[4,144,128]{2,1,0:T(8,128)S(1)}, u32[]{:S(2)}, u32[]{:S(2)}) collective-permute-start(f32[4,144,128]{2,1,0:T(8,128)S(1)} %collective-permute-done.3.p1), channel_id=1, source_target_pairs={{0,8},{8,0},{16,24},{24,16},{32,40},{40,32},{48,56},{56,48},{64,72... | collective-permute-start | bytes 884744 | tf_op jit(solution)/shard_map/ppermute | solution.py:582
  36.5 1.3 %copy-start.12 = (f32[4,144,128]{2,1,0:T(8,128)}, f32[4,144,128]{2,1,0:T(8,128)S(1)}, u32[]{:S(2)}) copy-start(f32[4,144,128]{2,1,0:T(8,128)S(1)} %collective-permute-done.6.p4) | copy-start | bytes 884740
  37.0 0.9 copy-start.13
  37.4 0.7 copy-start.14
  38.2 0.7 copy-start.15
  46.1 13.9 %all-to-all-start = ((f32[8,144,128]{2,1,0:T(8,128)}), f32[8,144,128]{2,1,0:T(8,128)S(1)}, u32[]{:S(2)}, u32[]{:S(2)}) async-start(f32[8,144,128]{2,1,0:T(8,128)} %bitcast.27), calls=%async_computation | async-start | bytes 1179648 | tf_op jit(solution)/shard_map/all_to_all | solution.py:603
  50.8 0.7 copy-start.5
  51.5 8.5 %copy-start.6 = (f32[8,128]{1,0:T(8,128)S(1)}, f32[8,128]{1,0:T(8,128)}, u32[]{:S(2)}) copy-start(f32[8,128]{1,0:T(8,128)} %get-tuple-element.31.stat_ref) | copy-start | bytes 12292
  75.2 11.8 %copy-start = (f32[8,144,128]{2,1,0:T(8,128)}, f32[8,144,128]{2,1,0:T(8,128)S(1)}, u32[]{:S(2)}) copy-start(f32[8,144,128]{2,1,0:T(8,128)S(1)} %all_to_all.15) | copy-start | bytes 1769476
  76.0 31.7 %all-to-all-start.2 = ((f32[32,40,128]{2,1,0:T(8,128)}), f32[32,40,128]{2,1,0:T(8,128)S(1)}, u32[]{:S(2)}, u32[]{:S(2)}) async-start(f32[32,40,128]{2,1,0:T(8,128)} %get-tuple-element.47), calls=%async_computation.2 | async-start | bytes 1310720 | tf_op jit(solution)/shard_map/all_to_all | solution.py:608
  95.7 6.6 %collective-permute-start.16 = (f32[8,128]{1,0:T(8,128)S(1)}, f32[8,128]{1,0:T(8,128)S(1)}, u32[]{:S(2)}, u32[]{:S(2)}) collective-permute-start(f32[8,128]{1,0:T(8,128)S(1)} %get-tuple-element.45.n0), channel_id=1, source_target_pairs={{0,7},{1,6},{2,5},{3,4},{4,3},{5,2},{6,1},{7,0},{8,15},{9,14},{10,... | collective-permute-start | bytes 12296 | tf_op jit(solution)/shard_map/ppermute | solution.py:582
  96.8 7.1 %collective-permute-start.15 = (f32[8,128]{1,0:T(8,128)S(1)}, f32[8,128]{1,0:T(8,128)S(1)}, u32[]{:S(2)}, u32[]{:S(2)}) collective-permute-start(f32[8,128]{1,0:T(8,128)S(1)} %get-tuple-element.45.n0), channel_id=1, source_target_pairs={{0,6},{1,7},{2,4},{3,5},{4,2},{5,3},{6,0},{7,1},{8,14},{9,15},{10,... | collective-permute-start | bytes 12296 | tf_op jit(solution)/shard_map/ppermute | solution.py:582
  98.6 6.4 %collective-permute-start.14 = (f32[8,128]{1,0:T(8,128)S(1)}, f32[8,128]{1,0:T(8,128)S(1)}, u32[]{:S(2)}, u32[]{:S(2)}) collective-permute-start(f32[8,128]{1,0:T(8,128)S(1)} %get-tuple-element.45.n0), channel_id=1, source_target_pairs={{0,5},{1,4},{2,7},{3,6},{4,1},{5,0},{6,3},{7,2},{8,13},{9,12},{10,... | collective-permute-start | bytes 12296 | tf_op jit(solution)/shard_map/ppermute | solution.py:582
  99.2 5.8 %collective-permute-start.13 = (f32[8,128]{1,0:T(8,128)S(1)}, f32[8,128]{1,0:T(8,128)S(1)}, u32[]{:S(2)}, u32[]{:S(2)}) collective-permute-start(f32[8,128]{1,0:T(8,128)S(1)} %get-tuple-element.45.n0), channel_id=1, source_target_pairs={{0,4},{1,5},{2,6},{3,7},{4,0},{5,1},{6,2},{7,3},{8,12},{9,13},{10,... | collective-permute-start | bytes 12296 | tf_op jit(solution)/shard_map/ppermute | solution.py:582
  102.3 3.7 %collective-permute-start.12 = (f32[8,128]{1,0:T(8,128)S(1)}, f32[8,128]{1,0:T(8,128)S(1)}, u32[]{:S(2)}, u32[]{:S(2)}) collective-permute-start(f32[8,128]{1,0:T(8,128)S(1)} %get-tuple-element.45.n0), channel_id=1, source_target_pairs={{0,3},{1,2},{2,1},{3,0},{4,7},{5,6},{6,5},{7,4},{8,11},{9,10},{10,... | collective-permute-start | bytes 12296 | tf_op jit(solution)/shard_map/ppermute | solution.py:582
  102.4 3.6 %collective-permute-start.11 = (f32[8,128]{1,0:T(8,128)S(1)}, f32[8,128]{1,0:T(8,128)S(1)}, u32[]{:S(2)}, u32[]{:S(2)}) collective-permute-start(f32[8,128]{1,0:T(8,128)S(1)} %get-tuple-element.45.n0), channel_id=1, source_target_pairs={{0,2},{1,3},{2,0},{3,1},{4,6},{5,7},{6,4},{7,5},{8,10},{9,11},{10,... | collective-permute-start | bytes 12296 | tf_op jit(solution)/shard_map/ppermute | solution.py:582
  104.0 2.8 %collective-permute-start.10 = (f32[8,128]{1,0:T(8,128)S(1)}, f32[8,128]{1,0:T(8,128)S(1)}, u32[]{:S(2)}, u32[]{:S(2)}) collective-permute-start(f32[8,128]{1,0:T(8,128)S(1)} %get-tuple-element.45.n0), channel_id=1, source_target_pairs={{0,1},{1,0},{2,3},{3,2},{4,5},{5,4},{6,7},{7,6},{8,9},{9,8},{10,11... | collective-permute-start | bytes 12296 | tf_op jit(solution)/shard_map/ppermute | solution.py:582
  107.7 0.8 copy-start.7

commit v4 on v3

--- a/solution.py
+++ b/solution.py
@@ -80,12 +80,16 @@
 
 
 def left_table(table, value):
+    count = table.shape[1]
     vh, vl = split(value)
-    return dot(table[0], vh) + dot(table[0], vl) + dot(table[1], vh)
+    both = dot(jnp.concatenate([table[0], table[1]], axis=0), vh)
+    return both[:count] + both[count:] + dot(table[0], vl)
 
 
 def right_table(vh, vl, table):
-    return dot(vh, table[0]) + dot(vl, table[0]) + dot(vh, table[1])
+    count = vh.shape[0]
+    both = dot(jnp.concatenate([vh, vl], axis=0), table[0])
+    return both[:count] + both[count:] + dot(vh, table[1])
 
 
 def begin(source, target, sem):
@@ -125,7 +129,9 @@
     return t0, c1, c2
 
 
-def pack_kernel(trial_ref, local_ref, out_ref):
+def pack_kernel(trial_far, local_far, out_ref, trial_ref, local_ref, sems):
+    for copy in [begin(trial_far, trial_ref, sems.at[0]), begin(local_far, local_ref, sems.at[1])]:
+        copy.wait()
     lane = lane_of((planes, 128))
     fill = jnp.zeros((planes, 96), f32)
 
@@ -148,6 +154,19 @@
     lane = lane_of(b0.shape)
     r0, r1, r2 = pltpu.roll(b0, 32, 1), pltpu.roll(b1, 64, 1), pltpu.roll(b2, 96, 1)
     return jnp.where(lane < 32, r0, jnp.where(lane < 64, r1, r2))
+
+
+def tighten(value):
+    lane, tail = lane_of((9, 128)), value[27:36]
+    return jnp.concatenate(
+        [jnp.where(lane < 96, value[9 * t : 9 * t + 9], pltpu.roll(tail, 96 - 32 * t, 1)) for t in range(3)], axis=0
+    )
+
+
+def loosen(value):
+    lane = lane_of((9, 128))
+    r0, r1, r2 = (pltpu.roll(value[9 * t : 9 * t + 9], 32 + 32 * t, 1) for t in range(3))
+    return jnp.concatenate([value, jnp.where(lane < 32, r0, jnp.where(lane < 64, r1, r2))], axis=0)
 
 
 def orbital_kernel(o_ref, packed_ref, far_out, base_out, packed_out, out_ref, base_ref, sems):
@@ -161,8 +180,8 @@
             out_ref[at : at + planes, :] = jnp.where(lane < 96, c[i], 0.0)
     for u in range(bands):
         mine = out_ref[u * 36 : u * 36 + 36, :]
-        base_ref[u, 0:36, :] = mine
-        base_ref[u, 36:40, :] = jnp.zeros((4, 128), f32)
+        base_ref[u, 0:27, :] = tighten(mine)
+        base_ref[u, 27:32, :] = jnp.zeros((5, 128), f32)
     copies = [begin(out_ref, far_out, sems.at[2]), begin(base_ref, base_out, sems.at[1]), kept]
     for copy in copies:
         copy.wait()
@@ -183,7 +202,8 @@
     corr = [jnp.zeros((36, 128), f32) for _ in range(trials)]
     for u in range(bands):
         d = u ^ me
-        slot = ((d & 1) << 4) | (((d >> 1) & 3) << 2) | (d >> 3)
+        along, across = (d >> 3, (d >> 1) & 3) if u & 1 else ((d >> 1) & 3, d >> 3)
+        slot = ((d & 1) << 4) | (along << 2) | across
         blocks = [t_ref[slot, q * 36 : q * 36 + 36, :] for q in range(4)]
         fields = [*blocks[:3], unpack_last(*blocks[:3]), blocks[3]]
         here = slice(u * 36, u * 36 + 36)
@@ -276,7 +296,7 @@
 
 def wave_kernel(in_ref, stat_ref, sums_ref, g2, g3, base_ref, out_ref, scal_ref, tail_ref, sems):
     owner = lax.axis_index("grid")
-    fetch = begin(base_ref.at[:, pl.ds(32, 8), :], tail_ref, sems.at[0])
+    fetch = begin(base_ref.at[:, pl.ds(24, 8), :], tail_ref, sems.at[0])
     s0 = in_ref[pl.ds(0, points, stride=planes), :]
     s1 = in_ref[pl.ds(1, points, stride=planes), :]
     weight = s0[:, 120:121]
@@ -355,12 +375,12 @@
     last = jnp.where(row_of((8, 128)) == 4, row, 0.0)
     for v in range(bands):
         tail[v, :, :] = tail_ref[v, :, :] + last
-    begin(tail, out_ref.at[:, pl.ds(32, 8), :], sems.at[0]).wait()
+    begin(tail, out_ref.at[:, pl.ds(24, 8), :], sems.at[0]).wait()
 
 
 def image_kernel(energy_ref, in_ref, step_ref, field_far, o_far, g4, w2,
                  response_ref, residual_ref, norm_ref,
-                 field_ref, o_ref, real, imag, mixed_s, mixed_r, flat_s, flat_r, sems, out_sems):
+                 field_ref, o_ref, real, imag, kinetic, mixed_s, mixed_r, flat_s, flat_r, sems, out_sems):
     energy = energy_ref[0]
     copies = [begin(field_far, field_ref, sems.at[0]), begin(o_far, o_ref, sems.at[1])]
     alpha = [step_ref[0:1, p : p + 1] for p in range(trials)]
@@ -379,8 +399,6 @@
         for i in range(2):
             real[pl.ds(x + i, points, stride=planes), :] = v[:points, i * 128 : i * 128 + 128]
             imag[pl.ds(x + i, points, stride=planes), :] = v[points:, i * 128 : i * 128 + 128]
-    for copy in copies:
-        copy.wait()
     size = 96
     mixed = planes * trials
     lane = lane_of((mixed, 128))
@@ -390,16 +408,26 @@
         r1, r2, r3 = pltpu.roll(c[1], 96, 1), pltpu.roll(c[2], 64, 1), pltpu.roll(c[3], 32, 1)
         return jnp.where(lane < 96, c[0], r1), jnp.where(lane < 64, r1, r2), jnp.where(lane < 32, r2, r3)
 
+    big = 384
+
+    def along_z(i, _):
+        at = pl.ds(pl.multiple_of(i * big, big), big)
+        vh, vl = split(jnp.concatenate([real[at, :], imag[at, :]], axis=1))
+        kinetic[at, :] = right_table(vh, vl, w2)
+        return 0
+
+    lax.fori_loop(0, rows // big, along_z, 0)
+    for copy in copies:
+        copy.wait()
+
     def back(i, sums):
         at = pl.ds(pl.multiple_of(i * size, size), size)
-        vh, vl = split(jnp.concatenate([real[at, :], imag[at, :]], axis=1))
-        kinetic = right_table(vh, vl, w2)
         o = o_ref[at, :]
         shift = field_ref[4, at, :] - energy
         out = []
         for p in range(trials):
             source = (alpha[p] - field_ref[p, at, :]) * o
-            image = kinetic[:, p * 128 : p * 128 + 128] + shift * source
+            image = kinetic[at, p * 128 : p * 128 + 128] + shift * source
             residual = source - step[p] * image
             there = pl.ds(p, size, stride=trials)
             mixed_s[there, :] = step[p] * source
@@ -422,7 +450,7 @@
         pltpu.make_async_copy(flat_r.at[i], residual_ref.at[:, :, cells], out_sems.at[1, i]).wait()
 
 
-def last_kernel(step_ref, n0, n1, n2, n3, n4, n5, n6, n7, packed_far, band_ref, response_ref, residual_ref,
+def last_kernel(step_ref, n0, n1, n2, n3, packed_far, band_ref, response_ref, residual_ref,
                 direction_ref, density_ref, packed_ref, bands_in, first, second, result, sems, out_sems):
     parts = 6
     width = points * points // parts
@@ -434,7 +462,7 @@
         loads.append((begin(response_ref.at[:, :, cells], first.at[i], sems.at[0, i]),
                       begin(residual_ref.at[:, :, cells], second.at[i], sems.at[1, i])))
     new = n0[0:1, :]
-    for part in (n1, n2, n3, n4, n5, n6, n7):
+    for part in (n1, n2, n3):
         new = new + part[0:1, :]
     ratio = [new[:, p : p + 1] / step_ref[0:1, 4 + p : 5 + p] / step_ref[0:1, 8 + p : 9 + p] for p in range(trials)]
     r = row_of((trials, 128))
@@ -451,17 +479,18 @@
     arrival.wait()
     kept.wait()
     blocks = [packed_ref[q * 36 : q * 36 + 36, :] for q in range(3)]
-    fields = [*blocks, unpack_last(*blocks)]
-    sums = [jnp.zeros((36, 128), f32) for _ in range(trials)]
+    fields = [tighten(field) for field in (*blocks, unpack_last(*blocks))]
+    sums = [jnp.zeros((27, 128), f32) for _ in range(trials)]
     for v in range(bands):
-        square = bands_in[v, 0:36, :]
+        square = bands_in[v, 0:27, :]
         square = square * square
         for p in range(trials):
-            alpha, step = bands_in[v, 36:37, p : p + 1], bands_in[v, 36:37, 8 + p : 9 + p]
+            alpha, step = bands_in[v, 28:29, p : p + 1], bands_in[v, 28:29, 8 + p : 9 + p]
             sums[p] = sums[p] + (step * (alpha - fields[p])) * square
     lane = lane_of((planes, 128))
     for p in range(trials):
-        c = [sums[p][12 * i : 12 * i + 12] * (4.0 / bands) for i in range(3)]
+        loose = loosen(sums[p]) * (4.0 / bands)
+        c = [loose[12 * i : 12 * i + 12] for i in range(3)]
         r1, r2 = pltpu.roll(c[1], 96, 1), pltpu.roll(c[2], 64, 1)
         density_ref[:, p, 0:128] = jnp.where(lane < 96, c[0], r1)
         density_ref[:, p, 128:256] = jnp.where(lane < 64, r1, r2)
@@ -494,14 +523,17 @@
 
 
 def pack(trial, local):
-    return call(pack_kernel, [vmem] * 2, shape(144, 128), name="pack")(jnp.transpose(trial, (1, 0, 2)), local)
+    return call(
+        pack_kernel, [far] * 2, shape(144, 128),
+        [buffer(planes, trials, 288), buffer(planes, 288), pltpu.SemaphoreType.DMA((2,))], name="pack", room=66000000,
+    )(jnp.transpose(trial, (1, 0, 2)), local)
 
 
 def orbital_rows(orbitals, packed):
     return call(
         orbital_kernel, [vmem, vmem],
-        (shape(rows, 128), shape(bands, 40, 128), shape(144, 128)),
-        [buffer(rows, 128), buffer(bands, 40, 128), pltpu.SemaphoreType.DMA((3,))],
+        (shape(rows, 128), shape(bands, 32, 128), shape(144, 128)),
+        [buffer(rows, 128), buffer(bands, 32, 128), pltpu.SemaphoreType.DMA((3,))],
         name="orbital_rows", places=(far, far, far), room=BIG,
     )(orbitals, packed)
 
@@ -546,7 +578,7 @@
 
 def steps(arrived, scal, tail, base):
     return call(
-        step_kernel, [vmem] * 3 + [far], (shape(8, 128), shape(bands, 40, 128)),
+        step_kernel, [vmem] * 3 + [far], (shape(8, 128), shape(bands, 32, 128)),
         [buffer(bands, 8, 128), pltpu.SemaphoreType.DMA((1,))],
         name="steps", places=(vmem, far), aliases={3: 1},
     )(arrived, scal, tail, base)
@@ -556,7 +588,7 @@
     cells = shape(planes, trials, points * points)
     return call(
         image_kernel, [smem, vmem, vmem, far, far, vmem, vmem], (cells, cells, shape(8, 128)),
-        [buffer(5, rows, 128), buffer(rows, 128), buffer(rows, 128), buffer(rows, 128),
+        [buffer(5, rows, 128), buffer(rows, 128), buffer(rows, 128), buffer(rows, 128), buffer(rows, 512),
          buffer(384, 128), buffer(384, 128),
          buffer(12, planes, trials, 768), buffer(12, planes, trials, 768),
          pltpu.SemaphoreType.DMA((2,)), pltpu.SemaphoreType.DMA((2, 12))],
@@ -568,8 +600,8 @@
     cells = shape(planes, trials, points * points)
     part = buffer(6, planes, trials, points * points // 6)
     return call(
-        last_kernel, [vmem] * 9 + [far] * 4, (cells, shape(planes, trials, 288)),
-        [buffer(144, 128), buffer(bands, 40, 128), part, part, part, pltpu.SemaphoreType.DMA((3, 6)), pltpu.SemaphoreType.DMA((6,))],
+        last_kernel, [vmem] * 5 + [far, hbm, far, far], (cells, shape(planes, trials, 288)),
+        [buffer(144, 128), buffer(bands, 32, 128), part, part, part, pltpu.SemaphoreType.DMA((3, 6)), pltpu.SemaphoreType.DMA((6,))],
         name="last", room=BIG, places=(far, vmem),
     )(step, *norms, packed, band, response, residual)
 
@@ -582,23 +614,30 @@
     return lax.ppermute(value, axis, [(s, s ^ mask) for s in range(size)])
 
 
-def gather_rows(packed):
+def crossed(value, even, odd):
+    return lax.ppermute(value, "band", [(s, s ^ (odd if s & 1 else even)) for s in range(bands)])
+
+
+along_z, along_y = (8, 16, 24), (2, 4, 6)
+
+
+def gather_first(packed):
     value = packed[None]
-    return jnp.concatenate([value] + [swapped(value, "band", bands, m) for m in (8, 16, 24)], axis=0)
-
-
-def gather_planes(quad):
-    quads = [quad] + [swapped(quad, "band", bands, m) for m in (2, 4, 6)]
+    return jnp.concatenate([value] + [crossed(value, z, y) for z, y in zip(along_z, along_y)], axis=0)
+
+
+def gather_second(quad):
+    quads = [quad] + [crossed(quad, y, z) for z, y in zip(along_z, along_y)]
     return quads + [swapped(q, "band", bands, 1) for q in quads]
 
 
 def on_device(orbitals, energies, local_pot, trial_pot):
     tables = {name: jnp.asarray(table) for name, table in build_tables().items()}
     packed = pack(trial_pot, local_pot)
-    quad = gather_rows(packed)
+    quad = gather_first(packed)
     o_far, base, packed_far = orbital_rows(orbitals, packed)
     quad, o_far = lax.optimization_barrier((quad, o_far))
-    pieces = gather_planes(quad)
+    pieces = gather_second(quad)
     fields, sent, stat = forward(pieces, o_far, tables)
     arrived = lax.all_to_all(sent.reshape(groups, chunk, 128), "grid", 0, 0, tiled=True).reshape(rows, 128)
     sums, g2, g3, g4, w2 = local_sums(energies, fields, o_far, stat, tables)
@@ -607,7 +646,8 @@
     step, payload = steps(back, scal, tail, base)
     band = lax.all_to_all(payload, "band", 0, 0, tiled=True)
     response, residual, norm = image(energies, back, step, fields, o_far, g4, w2)
-    norms = [norm] + [swapped(norm, "grid", groups, m) for m in range(1, groups)]
+    norm = norm + swapped(norm, "grid", groups, 1)
+    norms = [norm] + [swapped(norm, "grid", groups, m) for m in (2, 4, 6)]
     direction, density = last(step, norms, packed_far, band, response, residual)
     return outward(response)[None], outward(residual)[None], outward(direction)[None], outward(density)
 

time: 114 us -> 108 us (0.947); the launches traced: 112 us -> 108 us
  starting transfers between devices: 42.4 us -> 34.2 us
  waiting for transfers between devices: 18.8 us -> 22.3 us
    ppermute x17 -> x8, starting transfers between devices: 27.4 us -> 7.46 us  [swapped(): return lax.ppermute(value, axis, [(s, s ^ mask) for s in range(size)])]
    ppermute x0 -> x6, starting transfers between devices: none -> 12.6 us  [crossed(): lax.ppermute(value, 'band', [(s, s ^ (odd if s & 1 else even)) for s in r...]
    ppermute x0 -> x6, waiting for transfers between devices: none -> 10.6 us  [crossed(): lax.ppermute(value, 'band', [(s, s ^ (odd if s & 1 else even)) for s in r...]
    ppermute x17 -> x8, waiting for transfers between devices: 14.6 us -> 5.84 us  [swapped(): return lax.ppermute(value, axis, [(s, s ^ mask) for s in range(size)])]
    all_to_all x1, waiting for transfers between devices: 1 us -> 2.46 us  [on_device(): band = lax.all_to_all(payload, 'band', 0, 0, tiled=True)]
    pallas_call x4, Pallas kernels: 7.24 us -> 8.66 us  [the longest x1 3.74 us: last(): call(last_kernel, [vmem] * 5 + [far, hbm, far, far], (cells, shape(planes...]
    unnamed x33 -> x31, local copies, waits for them, and re-layouts: 6.08 us -> 5.03 us
  transfers between devices with their start and end apart: 19 -> 16, of which waited for: 10 -> 8; matrix products, arithmetic and copies ran while one was open for 2% -> 2% of each run, Pallas kernels for 15% -> 14%
where the time goes in v4:
time: 108 us
  starting transfers between devices  34.2 us (32%)
  Pallas kernels  31.1 us (29%)
  waiting for transfers between devices  22.3 us (21%)
  blocking collectives  13.4 us (12%)
  local copies, waits for them, and re-layouts  5.03 us (5%)
  between operations  1.54 us (1%)
    all_to_all x1, blocking collectives, on_device(): lax.all_to_all(back.reshape(groups, chunk, 128), 'grid', 0, 0, tiled=True)  13.4 us
    ppermute x6, starting transfers between devices, crossed(): lax.ppermute(value, 'band', [(s, s ^ (odd if s & 1 else even)) for s in r...  12.6 us
    ppermute x6, waiting for transfers between devices, crossed(): lax.ppermute(value, 'band', [(s, s ^ (odd if s & 1 else even)) for s in r...  10.6 us
    all_to_all x1, starting transfers between devices, on_device(): band = lax.all_to_all(payload, 'band', 0, 0, tiled=True)  10.1 us
    pallas_call x1, Pallas kernels, image(): call(image_kernel, [smem, vmem, vmem, far, far, vmem, vmem], (cells, cell...  7.88 us
    ppermute x8, starting transfers between devices, swapped(): return lax.ppermute(value, axis, [(s, s ^ mask) for s in range(size)])  7.46 us
    pallas_call x1, Pallas kernels, forward(): call(forward_kernel, [far] * 11, (shape(5, rows, 128), shape(rows, 128),...  7.2 us
    ppermute x8, waiting for transfers between devices, swapped(): return lax.ppermute(value, axis, [(s, s ^ mask) for s in range(size)])  5.84 us
  transfers between devices with their start and end apart: 16, of which 8 were waited for; matrix products, arithmetic and copies ran while one was open for 2% of the time, Pallas kernels for 14%

profile of v4, /device:TPU:1, one launch (start us, length us, event | category | flops | bytes accessed | tf_op | source)
XLA Modules:
  0.0 107.7 jit_solution(11326733561420417769)
XLA Ops:
  0.6 1.7 %pack.1.packed_ref = f32[144,128]{1,0:T(8,128)} custom-call(f32[12,4,288]{2,1,0:T(4,128)} %bitcast.27, f32[12,288]{1,0:T(8,128)} %local_far.1), custom_call_target="tpu_custom_call" | custom-call | flops 1000000 | bytes 1000000 | tf_op jit(solution)/shard_map/pack/pallas_call | solution.py:526
  2.3 3.7 %collective-permute-start.2 = (f32[1,144,128]{2,1,0:T(8,128)}, f32[1,144,128]{2,1,0:T(8,128)S(1)}, u32[]{:S(2)}, u32[]{:S(2)}) collective-permute-start(f32[1,144,128]{2,1,0:T(8,128)} %bitcast.19), channel_id=1, source_target_pairs={{0,192},{8,56},{16,208},{24,40},{32,224},{40,24},{48,240},{56,8},{... | collective-permute-start | bytes 221192 | tf_op jit(solution)/shard_map/ppermute | solution.py:618
  6.0 0.3 collective-permute-start.1
  6.3 0.3 collective-permute-start
  6.7 1.9 %copy.15.o_ref = f32[1,12,9216]{2,1,0:T(8,128)} copy(f32[1,12,9216]{2,0,1:T(1,128)} %param.10) | data formatting | bytes 884736 | tf_op args[0]
  8.6 0.9 copy-done.1
  9.5 2.4 %orbital_rows.1 = (f32[1152,128]{1,0:T(8,128)}, f32[32,32,128]{2,1,0:T(8,128)}, f32[144,128]{1,0:T(8,128)S(1)}) custom-call(f32[1,12,9216]{2,1,0:T(8,128)} %copy.15.o_ref, f32[144,128]{1,0:T(8,128)S(1)} %copy-done.1), custom_call_target="tpu_custom_call" | custom-call | flops 1000000 | bytes 1000000 | tf_op jit(solution)/shard_map/orbital_rows/pallas_call | solution.py:533
  11.9 0.0 collective-permute-done.2
  11.9 0.0 collective-permute-done.1
  11.9 0.0 collective-permute-done
  11.9 0.0 copy-start.7
  11.9 0.0 copy-start.2
  11.9 0.0 copy-start.3
  11.9 6.1 %collective-permute-start.5 = (f32[4,144,128]{2,1,0:T(8,128)S(1)}, f32[4,144,128]{2,1,0:T(8,128)S(1)}, u32[]{:S(2)}, u32[]{:S(2)}) collective-permute-start(f32[4,144,128]{2,1,0:T(8,128)S(1)} %pad_maximum_fusion.p0), channel_id=1, source_target_pairs={{0,48},{8,200},{16,32},{24,216},{32,16},{40,232},{48,0},{56,248},{... | collective-permute-start | bytes 884744 | tf_op jit(solution)/shard_map/ppermute | solution.py:618
  18.1 1.0 collective-permute-start.4
  19.0 1.2 %collective-permute-start.3 = (f32[4,144,128]{2,1,0:T(8,128)S(1)}, f32[4,144,128]{2,1,0:T(8,128)S(1)}, u32[]{:S(2)}, u32[]{:S(2)}) collective-permute-start(f32[4,144,128]{2,1,0:T(8,128)S(1)} %pad_maximum_fusion.p0), channel_id=1, source_target_pairs={{0,16},{8,72},{16,0},{24,88},{32,48},{40,104},{48,32},{56,120},{64... | collective-permute-start | bytes 884744 | tf_op jit(solution)/shard_map/ppermute | solution.py:618
  20.2 3.2 %collective-permute-start.6 = (f32[4,144,128]{2,1,0:T(8,128)S(1)}, f32[4,144,128]{2,1,0:T(8,128)S(1)}, u32[]{:S(2)}, u32[]{:S(2)}) collective-permute-start(f32[4,144,128]{2,1,0:T(8,128)S(1)} %pad_maximum_fusion.p0), channel_id=1, source_target_pairs={{0,8},{8,0},{16,24},{24,16},{32,40},{40,32},{48,56},{56,48},{64,72... | collective-permute-start | bytes 884744 | tf_op jit(solution)/shard_map/ppermute | solution.py:614
  23.4 7.8 %collective-permute-done.5.p3 = f32[4,144,128]{2,1,0:T(8,128)S(1)} collective-permute-done((f32[4,144,128]{2,1,0:T(8,128)S(1)}, f32[4,144,128]{2,1,0:T(8,128)S(1)}, u32[]{:S(2)}, u32[]{:S(2)}) %collective-permute-start.5) | collective-permute-done | bytes 294944 | tf_op jit(solution)/shard_map/ppermute | solution.py:618
  31.2 0.0 collective-permute-start.9
  31.3 0.0 collective-permute-done.4.p2
  31.3 0.5 collective-permute-start.8
  31.8 2.7 %collective-permute-done.3.p1 = f32[4,144,128]{2,1,0:T(8,128)S(1)} collective-permute-done((f32[4,144,128]{2,1,0:T(8,128)S(1)}, f32[4,144,128]{2,1,0:T(8,128)S(1)}, u32[]{:S(2)}, u32[]{:S(2)}) %collective-permute-start.3) | collective-permute-done | bytes 294944 | tf_op jit(solution)/shard_map/ppermute | solution.py:618
  34.5 0.0 collective-permute-start.7
  34.5 0.0 collective-permute-done.6.p4
  34.5 0.0 copy-start.11
  34.5 0.0 collective-permute-done.9.p7
  34.5 0.0 copy-start.12
  34.5 0.0 collective-permute-done.8.p6
  34.6 0.0 copy-start.13
  34.6 1.5 %collective-permute-done.7.p5 = f32[4,144,128]{2,1,0:T(8,128)S(1)} collective-permute-done((f32[4,144,128]{2,1,0:T(8,128)S(1)}, f32[4,144,128]{2,1,0:T(8,128)S(1)}, u32[]{:S(2)}, u32[]{:S(2)}) %collective-permute-start.7) | collective-permute-done | bytes 294944 | tf_op jit(solution)/shard_map/ppermute | solution.py:614
  36.1 0.0 copy-done.7
  36.1 0.0 copy-done.8
  36.1 0.0 copy-done.9
  36.1 0.0 copy-done.10
  36.1 0.0 copy-done.11
  36.1 0.0 copy-done.12
  36.1 0.0 copy-done.13
  36.1 0.7 copy-done.14
  36.8 7.2 %forward.1 = (f32[5,1152,128]{2,1,0:T(8,128)}, f32[1152,128]{1,0:T(8,128)}, f32[8,128]{1,0:T(8,128)}) custom-call(f32[4,144,128]{2,1,0:T(8,128)} %copy-done.7, f32[4,144,128]{2,1,0:T(8,128)} %copy-done.10, f32[4,144,128]{2,1,0:T(8,128)} %copy-done.9, f32[4,144,128]{2,1,0:T(8,128)} %copy-done.8, f32[4,144,128]{2,1,0:T(8,128)} %copy-done.11, ...), custom_call_target="tpu_custom_call" | custom-call | flops 1000000 | bytes 1000000 | tf_op jit(solution)/shard_map/forward/pallas_call | solution.py:546
  44.1 4.0 %all-to-all-start = ((f32[8,144,128]{2,1,0:T(8,128)}), f32[8,144,128]{2,1,0:T(8,128)S(1)}, u32[]{:S(2)}, u32[]{:S(2)}) async-start(f32[8,144,128]{2,1,0:T(8,128)} %bitcast.26), calls=%async_computation | async-start | bytes 1179648 | tf_op jit(solution)/shard_map/all_to_all | solution.py:642
  48.7 0.0 copy-done.2
  48.7 0.0 copy-done.3
  48.8 0.0 copy-start.4
  48.8 0.7 copy-done.4
  49.4 5.4 %local_sums.1 = (f32[8,128]{1,0:T(8,128)S(1)}, bf16[2,96,192]{2,1,0:T(8,128)(2,1)S(1)}, bf16[2,192,96]{2,1,0:T(8,128)(2,1)S(1)}, bf16[2,192,96]{2,1,0:T(8,128)(2,1)S(1)}, bf16[2,256,512]{2,1,0:T(8,128)(2,1)}) custom-call(f32[1]{0:T(128)S(6)} %copy.17.energy_ref, f32[5,1152,128]{2,1,0:T(8,128)} %get-tuple-element.32.field_ref.field_far, ...), custom_call_target="tpu_custom_call" | custom-call | flops 10000000 | bytes 10000000 | tf_op jit(solution)/shard_map/local_sums/pallas_call | solution.py:560
  54.8 3.4 %all-to-all-done = f32[8,144,128]{2,1,0:T(8,128)S(1)} async-done(((f32[8,144,128]{2,1,0:T(8,128)}), f32[8,144,128]{2,1,0:T(8,128)S(1)}, u32[]{:S(2)}, u32[]{:S(2)}) %all-to-all-start) | async-done | bytes 589856 | tf_op jit(solution)/shard_map/all_to_all | solution.py:642
  58.3 0.0 copy-done.5
  58.3 2.0 %waves.1 = (f32[1152,128]{1,0:T(8,128)S(1)}, f32[8,128]{1,0:T(8,128)S(1)}, f32[32,8,128]{2,1,0:T(8,128)S(1)}) custom-call(f32[1152,128]{1,0:T(8,128)S(1)} %bitcast.16, f32[8,128]{1,0:T(8,128)S(1)} %copy-done.5, f32[8,128]{1,0:T(8,128)S(1)} %get-tuple-element.33.sums_ref, bf16[2,96,192]{2,1,0:T(8,128)(2,1)S(1)} %get-tuple-element.34.g2, ...), custom_call_target="tpu_custom_call" | custom-call | flops 1000000 | bytes 1000000 | tf_op jit(solution)/shard_map/waves/pallas_call | solution.py:573
  60.2 13.4 %all_to_all.15 = f32[8,144,128]{2,1,0:T(8,128)S(1)} all-to-all(f32[8,144,128]{2,1,0:T(8,128)S(1)} %bitcast.23), channel_id=1, replica_groups=mesh['band'=32,'grid'=8] {'grid'}, dimensions={0} | all-to-all | bytes 1179648 | tf_op jit(solution)/shard_map/all_to_all | solution.py:645
  73.7 0.8 steps.1
  74.5 10.1 %all-to-all-start.2 = ((f32[32,32,128]{2,1,0:T(8,128)}), f32[32,32,128]{2,1,0:T(8,128)S(1)}, u32[]{:S(2)}, u32[]{:S(2)}) async-start(f32[32,32,128]{2,1,0:T(8,128)} %get-tuple-element.47), calls=%async_computation.2 | async-start | bytes 1048576 | tf_op jit(solution)/shard_map/all_to_all | solution.py:647
  84.7 0.0 copy-done
  84.7 7.9 %image.1 = (f32[12,4,9216]{2,1,0:T(4,128)}, f32[12,4,9216]{2,1,0:T(4,128)}, f32[8,128]{1,0:T(8,128)S(1)}) custom-call(f32[1]{0:T(128)S(6)} %copy.17.energy_ref, f32[1152,128]{1,0:T(8,128)} %bitcast.18, f32[8,128]{1,0:T(8,128)S(1)} %get-tuple-element.40.step_ref, f32[5,1152,128]{2,1,0:T(8,128)} %get-tuple-element.32.field_ref.field_far, ...), custom_call_target="tpu_custom_call" | custom-call | flops 20000000000 | bytes 1000000 | tf_op jit(solution)/shard_map/image/pallas_call | solution.py:589
  92.6 0.5 collective-permute-start.10
  93.1 2.4 %collective-permute-done.10 = f32[8,128]{1,0:T(8,128)S(1)} collective-permute-done((f32[8,128]{1,0:T(8,128)S(1)}, f32[8,128]{1,0:T(8,128)S(1)}, u32[]{:S(2)}, u32[]{:S(2)}) %collective-permute-start.10) | collective-permute-done | bytes 4128 | tf_op jit(solution)/shard_map/ppermute | solution.py:614
  95.5 0.9 collective-permute-start.13
  96.4 1.2 %collective-permute-start.12 = (f32[8,128]{1,0:T(8,128)S(1)}, f32[8,128]{1,0:T(8,128)S(1)}, u32[]{:S(2)}, u32[]{:S(2)}) collective-permute-start(f32[8,128]{1,0:T(8,128)S(1)} %add.3.n0), channel_id=1, source_target_pairs={{0,4},{1,5},{2,6},{3,7},{4,0},{5,1},{6,2},{7,3},{8,12},{9,13},{10,... | collective-permute-start | bytes 12296 | tf_op jit(solution)/shard_map/ppermute | solution.py:614
  97.6 1.2 %collective-permute-start.11 = (f32[8,128]{1,0:T(8,128)S(1)}, f32[8,128]{1,0:T(8,128)S(1)}, u32[]{:S(2)}, u32[]{:S(2)}) collective-permute-start(f32[8,128]{1,0:T(8,128)S(1)} %add.3.n0), channel_id=1, source_target_pairs={{0,2},{1,3},{2,0},{3,1},{4,6},{5,7},{6,4},{7,5},{8,10},{9,11},{10,... | collective-permute-start | bytes 12296 | tf_op jit(solution)/shard_map/ppermute | solution.py:614
  98.8 0.7 collective-permute-done.13.n3
  99.5 1.2 %collective-permute-done.12.n2 = f32[8,128]{1,0:T(8,128)S(1)} collective-permute-done((f32[8,128]{1,0:T(8,128)S(1)}, f32[8,128]{1,0:T(8,128)S(1)}, u32[]{:S(2)}, u32[]{:S(2)}) %collective-permute-start.12) | collective-permute-done | bytes 4128 | tf_op jit(solution)/shard_map/ppermute | solution.py:614
  100.7 0.0 collective-permute-done.11.n1
  100.7 2.5 %all-to-all-done.2.band_ref = f32[32,32,128]{2,1,0:T(8,128)S(1)} async-done(((f32[32,32,128]{2,1,0:T(8,128)}), f32[32,32,128]{2,1,0:T(8,128)S(1)}, u32[]{:S(2)}, u32[]{:S(2)}) %all-to-all-start.2) | async-done | bytes 524320 | tf_op jit(solution)/shard_map/all_to_all | solution.py:647
  103.1 0.8 copy-done.6
  103.9 3.7 %last.1 = (f32[12,4,9216]{2,1,0:T(4,128)}, f32[12,4,288]{2,1,0:T(4,128)}) custom-call(f32[8,128]{1,0:T(8,128)S(1)} %get-tuple-element.40.step_ref, f32[8,128]{1,0:T(8,128)S(1)} %add.3.n0, f32[8,128]{1,0:T(8,128)S(1)} %collective-permute-done.11.n1, f32[8,128]{1,0:T(8,128)S(1)} %collective-permute-done.12.n2, f32[8,128]{1,0:T(8,128)S(1)} %collective-permute-done.13.n3, ...), custom_call_target="tpu_custom_call" | custom-call | flops 1000000 | bytes 1000000 | tf_op jit(solution)/shard_map/last/pallas_call | solution.py:602
  (10 shorter events, 0.0 us)
Async XLA Ops:
  2.3 9.5 %collective-permute-start.2 = (f32[1,144,128]{2,1,0:T(8,128)}, f32[1,144,128]{2,1,0:T(8,128)S(1)}, u32[]{:S(2)}, u32[]{:S(2)}) collective-permute-start(f32[1,144,128]{2,1,0:T(8,128)} %bitcast.19), channel_id=1, source_target_pairs={{0,192},{8,56},{16,208},{24,40},{32,224},{40,24},{48,240},{56,8},{... | collective-permute-start | bytes 221192 | tf_op jit(solution)/shard_map/ppermute | solution.py:618
  6.0 5.9 %collective-permute-start.1 = (f32[1,144,128]{2,1,0:T(8,128)}, f32[1,144,128]{2,1,0:T(8,128)S(1)}, u32[]{:S(2)}, u32[]{:S(2)}) collective-permute-start(f32[1,144,128]{2,1,0:T(8,128)} %bitcast.20), channel_id=1, source_target_pairs={{0,128},{8,40},{16,144},{24,56},{32,160},{40,8},{48,176},{56,24},{... | collective-permute-start | bytes 221192 | tf_op jit(solution)/shard_map/ppermute | solution.py:618
  6.3 5.5 %collective-permute-start = (f32[1,144,128]{2,1,0:T(8,128)}, f32[1,144,128]{2,1,0:T(8,128)S(1)}, u32[]{:S(2)}, u32[]{:S(2)}) collective-permute-start(f32[1,144,128]{2,1,0:T(8,128)} %bitcast.21), channel_id=1, source_target_pairs={{0,64},{8,24},{16,80},{24,8},{32,96},{40,56},{48,112},{56,40},{64,... | collective-permute-start | bytes 221192 | tf_op jit(solution)/shard_map/ppermute | solution.py:618
  8.6 0.9 copy-start.1
  11.9 24.2 %copy-start.7 = (f32[4,144,128]{2,1,0:T(8,128)}, f32[4,144,128]{2,1,0:T(8,128)S(1)}, u32[]{:S(2)}) copy-start(f32[4,144,128]{2,1,0:T(8,128)S(1)} %pad_maximum_fusion.p0) | copy-start | bytes 884740
  11.9 36.8 %copy-start.2 = (bf16[2,192,96]{2,1,0:T(8,128)(2,1)S(1)}, bf16[2,192,96]{2,1,0:T(8,128)(2,1)}, u32[]{:S(2)}) copy-start(bf16[2,192,96]{2,1,0:T(8,128)(2,1)} %constant.15.clone.g3_ref) | copy-start | bytes 221188
  11.9 36.8 %copy-start.3 = (bf16[2,96,192]{2,1,0:T(8,128)(2,1)S(1)}, bf16[2,96,192]{2,1,0:T(8,128)(2,1)}, u32[]{:S(2)}) copy-start(bf16[2,96,192]{2,1,0:T(8,128)(2,1)} %constant.14.clone.g2_ref) | copy-start | bytes 221188
  11.9 19.3 %collective-permute-start.5 = (f32[4,144,128]{2,1,0:T(8,128)S(1)}, f32[4,144,128]{2,1,0:T(8,128)S(1)}, u32[]{:S(2)}, u32[]{:S(2)}) collective-permute-start(f32[4,144,128]{2,1,0:T(8,128)S(1)} %pad_maximum_fusion.p0), channel_id=1, source_target_pairs={{0,48},{8,200},{16,32},{24,216},{32,16},{40,232},{48,0},{56,248},{... | collective-permute-start | bytes 884744 | tf_op jit(solution)/shard_map/ppermute | solution.py:618
  18.1 13.2 %collective-permute-start.4 = (f32[4,144,128]{2,1,0:T(8,128)S(1)}, f32[4,144,128]{2,1,0:T(8,128)S(1)}, u32[]{:S(2)}, u32[]{:S(2)}) collective-permute-start(f32[4,144,128]{2,1,0:T(8,128)S(1)} %pad_maximum_fusion.p0), channel_id=1, source_target_pairs={{0,32},{8,136},{16,48},{24,152},{32,0},{40,168},{48,16},{56,184},{... | collective-permute-start | bytes 884744 | tf_op jit(solution)/shard_map/ppermute | solution.py:618
  19.0 15.5 %collective-permute-start.3 = (f32[4,144,128]{2,1,0:T(8,128)S(1)}, f32[4,144,128]{2,1,0:T(8,128)S(1)}, u32[]{:S(2)}, u32[]{:S(2)}) collective-permute-start(f32[4,144,128]{2,1,0:T(8,128)S(1)} %pad_maximum_fusion.p0), channel_id=1, source_target_pairs={{0,16},{8,72},{16,0},{24,88},{32,48},{40,104},{48,32},{56,120},{64... | collective-permute-start | bytes 884744 | tf_op jit(solution)/shard_map/ppermute | solution.py:618
  20.2 14.3 %collective-permute-start.6 = (f32[4,144,128]{2,1,0:T(8,128)S(1)}, f32[4,144,128]{2,1,0:T(8,128)S(1)}, u32[]{:S(2)}, u32[]{:S(2)}) collective-permute-start(f32[4,144,128]{2,1,0:T(8,128)S(1)} %pad_maximum_fusion.p0), channel_id=1, source_target_pairs={{0,8},{8,0},{16,24},{24,16},{32,40},{40,32},{48,56},{56,48},{64,72... | collective-permute-start | bytes 884744 | tf_op jit(solution)/shard_map/ppermute | solution.py:614
  31.2 4.8 %copy-start.8 = (f32[4,144,128]{2,1,0:T(8,128)}, f32[4,144,128]{2,1,0:T(8,128)S(1)}, u32[]{:S(2)}) copy-start(f32[4,144,128]{2,1,0:T(8,128)S(1)} %collective-permute-done.5.p3) | copy-start | bytes 884740
  31.2 3.3 %collective-permute-start.9 = (f32[4,144,128]{2,1,0:T(8,128)S(1)}, f32[4,144,128]{2,1,0:T(8,128)S(1)}, u32[]{:S(2)}, u32[]{:S(2)}) collective-permute-start(f32[4,144,128]{2,1,0:T(8,128)S(1)} %collective-permute-done.5.p3), channel_id=1, source_target_pairs={{0,8},{8,0},{16,24},{24,16},{32,40},{40,32},{48,56},{56,48},{64,72... | collective-permute-start | bytes 884744 | tf_op jit(solution)/shard_map/ppermute | solution.py:614
  31.3 4.8 %copy-start.9 = (f32[4,144,128]{2,1,0:T(8,128)}, f32[4,144,128]{2,1,0:T(8,128)S(1)}, u32[]{:S(2)}) copy-start(f32[4,144,128]{2,1,0:T(8,128)S(1)} %collective-permute-done.4.p2) | copy-start | bytes 884740
  31.3 3.3 %collective-permute-start.8 = (f32[4,144,128]{2,1,0:T(8,128)S(1)}, f32[4,144,128]{2,1,0:T(8,128)S(1)}, u32[]{:S(2)}, u32[]{:S(2)}) collective-permute-start(f32[4,144,128]{2,1,0:T(8,128)S(1)} %collective-permute-done.4.p2), channel_id=1, source_target_pairs={{0,8},{8,0},{16,24},{24,16},{32,40},{40,32},{48,56},{56,48},{64,72... | collective-permute-start | bytes 884744 | tf_op jit(solution)/shard_map/ppermute | solution.py:614
  34.5 1.6 %copy-start.10 = (f32[4,144,128]{2,1,0:T(8,128)}, f32[4,144,128]{2,1,0:T(8,128)S(1)}, u32[]{:S(2)}) copy-start(f32[4,144,128]{2,1,0:T(8,128)S(1)} %collective-permute-done.3.p1) | copy-start | bytes 884740
  34.5 1.6 %collective-permute-start.7 = (f32[4,144,128]{2,1,0:T(8,128)S(1)}, f32[4,144,128]{2,1,0:T(8,128)S(1)}, u32[]{:S(2)}, u32[]{:S(2)}) collective-permute-start(f32[4,144,128]{2,1,0:T(8,128)S(1)} %collective-permute-done.3.p1), channel_id=1, source_target_pairs={{0,8},{8,0},{16,24},{24,16},{32,40},{40,32},{48,56},{56,48},{64,72... | collective-permute-start | bytes 884744 | tf_op jit(solution)/shard_map/ppermute | solution.py:614
  34.5 1.6 %copy-start.11 = (f32[4,144,128]{2,1,0:T(8,128)}, f32[4,144,128]{2,1,0:T(8,128)S(1)}, u32[]{:S(2)}) copy-start(f32[4,144,128]{2,1,0:T(8,128)S(1)} %collective-permute-done.6.p4) | copy-start | bytes 884740
  34.5 1.6 %copy-start.12 = (f32[4,144,128]{2,1,0:T(8,128)}, f32[4,144,128]{2,1,0:T(8,128)S(1)}, u32[]{:S(2)}) copy-start(f32[4,144,128]{2,1,0:T(8,128)S(1)} %collective-permute-done.9.p7) | copy-start | bytes 884740
  34.6 1.6 %copy-start.13 = (f32[4,144,128]{2,1,0:T(8,128)}, f32[4,144,128]{2,1,0:T(8,128)S(1)}, u32[]{:S(2)}) copy-start(f32[4,144,128]{2,1,0:T(8,128)S(1)} %collective-permute-done.8.p6) | copy-start | bytes 884740
  36.1 0.7 copy-start.14
  44.1 14.2 %all-to-all-start = ((f32[8,144,128]{2,1,0:T(8,128)}), f32[8,144,128]{2,1,0:T(8,128)S(1)}, u32[]{:S(2)}, u32[]{:S(2)}) async-start(f32[8,144,128]{2,1,0:T(8,128)} %bitcast.26), calls=%async_computation | async-start | bytes 1179648 | tf_op jit(solution)/shard_map/all_to_all | solution.py:642
  48.8 0.7 copy-start.4
  49.4 8.8 %copy-start.5 = (f32[8,128]{1,0:T(8,128)S(1)}, f32[8,128]{1,0:T(8,128)}, u32[]{:S(2)}) copy-start(f32[8,128]{1,0:T(8,128)} %get-tuple-element.31.stat_ref) | copy-start | bytes 12292
  73.7 11.0 %copy-start = (f32[8,144,128]{2,1,0:T(8,128)}, f32[8,144,128]{2,1,0:T(8,128)S(1)}, u32[]{:S(2)}) copy-start(f32[8,144,128]{2,1,0:T(8,128)S(1)} %all_to_all.15) | copy-start | bytes 1769476
  74.5 28.6 %all-to-all-start.2 = ((f32[32,32,128]{2,1,0:T(8,128)}), f32[32,32,128]{2,1,0:T(8,128)S(1)}, u32[]{:S(2)}, u32[]{:S(2)}) async-start(f32[32,32,128]{2,1,0:T(8,128)} %get-tuple-element.47), calls=%async_computation.2 | async-start | bytes 1048576 | tf_op jit(solution)/shard_map/all_to_all | solution.py:647
  92.6 2.9 %collective-permute-start.10 = (f32[8,128]{1,0:T(8,128)S(1)}, f32[8,128]{1,0:T(8,128)S(1)}, u32[]{:S(2)}, u32[]{:S(2)}) collective-permute-start(f32[8,128]{1,0:T(8,128)S(1)} %get-tuple-element.45), channel_id=1, source_target_pairs={{0,1},{1,0},{2,3},{3,2},{4,5},{5,4},{6,7},{7,6},{8,9},{9,8},{10,11... | collective-permute-start | bytes 12296 | tf_op jit(solution)/shard_map/ppermute | solution.py:614
  95.5 4.0 %collective-permute-start.13 = (f32[8,128]{1,0:T(8,128)S(1)}, f32[8,128]{1,0:T(8,128)S(1)}, u32[]{:S(2)}, u32[]{:S(2)}) collective-permute-start(f32[8,128]{1,0:T(8,128)S(1)} %add.3.n0), channel_id=1, source_target_pairs={{0,6},{1,7},{2,4},{3,5},{4,2},{5,3},{6,0},{7,1},{8,14},{9,15},{10,... | collective-permute-start | bytes 12296 | tf_op jit(solution)/shard_map/ppermute | solution.py:614
  96.4 4.3 %collective-permute-start.12 = (f32[8,128]{1,0:T(8,128)S(1)}, f32[8,128]{1,0:T(8,128)S(1)}, u32[]{:S(2)}, u32[]{:S(2)}) collective-permute-start(f32[8,128]{1,0:T(8,128)S(1)} %add.3.n0), channel_id=1, source_target_pairs={{0,4},{1,5},{2,6},{3,7},{4,0},{5,1},{6,2},{7,3},{8,12},{9,13},{10,... | collective-permute-start | bytes 12296 | tf_op jit(solution)/shard_map/ppermute | solution.py:614
  97.6 3.1 %collective-permute-start.11 = (f32[8,128]{1,0:T(8,128)S(1)}, f32[8,128]{1,0:T(8,128)S(1)}, u32[]{:S(2)}, u32[]{:S(2)}) collective-permute-start(f32[8,128]{1,0:T(8,128)S(1)} %add.3.n0), channel_id=1, source_target_pairs={{0,2},{1,3},{2,0},{3,1},{4,6},{5,7},{6,4},{7,5},{8,10},{9,11},{10,... | collective-permute-start | bytes 12296 | tf_op jit(solution)/shard_map/ppermute | solution.py:614
  103.1 0.8 copy-start.6

commit v5 on v4

--- a/solution.py
+++ b/solution.py
@@ -17,6 +17,7 @@
 groups = 8
 rows = points * planes
 chunk = rows // groups
+returned = 112
 spacing = 0.49
 prefactor = 0.5 * (2.0 * math.pi / (points * spacing)) ** 2
 f32 = jnp.float32
@@ -202,7 +203,12 @@
     corr = [jnp.zeros((36, 128), f32) for _ in range(trials)]
     for u in range(bands):
         d = u ^ me
-        along, across = (d >> 3, (d >> 1) & 3) if u & 1 else ((d >> 1) & 3, d >> 3)
+        z, y = d >> 3, (d >> 1) & 3
+        if u & 1:
+            z, y = (z >> 1) | ((y >> 1) << 1), ((z ^ (z >> 1)) & 1) | (((y ^ (y >> 1)) & 1) << 1)
+            along, across = z, y
+        else:
+            along, across = y, z
         slot = ((d & 1) << 4) | (along << 2) | across
         blocks = [t_ref[slot, q * 36 : q * 36 + 36, :] for q in range(4)]
         fields = [*blocks[:3], unpack_last(*blocks[:3]), blocks[3]]
@@ -328,6 +334,7 @@
     doubled = jnp.where(k == 0, 1.0, 2.0) * (prefactor / float(points**3))
     energy = jnp.zeros((1, 128), f32)
     own = [jnp.where(lane_of((1, 128)) == 0, 0.0, 0.0)]
+    tails, directs = [], []
     for pair in (2, 1, 0):
         parts = [
             jnp.concatenate([source_of(2 * (2 * pair + i) + c) for i in range(2)], axis=1)
@@ -344,28 +351,39 @@
         product = jnp.sum(u * t, axis=0, keepdims=True)
         energy = energy + product[:, :128] + product[:, 128:]
         e = left_table(g3, t)
-        if pair == 0:
-            l1 = lane_of((1, 128))
-            ride = jnp.zeros((1, 128), f32)
-            entries = []
-            for p in range(trials):
-                kinetic = jnp.sum(jnp.where((l1 >= p * half) & (l1 < (p + 1) * half), energy, 0.0), axis=1, keepdims=True)
-                off = alpha[p] - stat_ref[0:1, 1 + p : 2 + p]
-                at_p = sums_ref[0:1, 5 + p : 6 + p] - 2.0 * off * sums_ref[0:1, 1 + p : 2 + p] + off * off * sums_ref[0:1, 0:1]
-                ride = jnp.where(l1 == 96 + p, kinetic + at_p, ride)
-                entries += [(0, p, alpha[p]), (0, 4 + p, start[p])]
-            scal_ref[...] = tile_of((8, 128), entries)
-            e = e + jnp.concatenate([ride, jnp.zeros((1, 128), f32)], axis=1)
         for i in range(2):
             for c in range(2):
-                out_ref[pl.ds(2 * (2 * pair + i) + c, points, stride=planes), :] = (
-                    e[c * points : (c + 1) * points, i * 128 : i * 128 + 128]
-                )
+                r = 2 * (2 * pair + i) + c
+                value = e[c * points : (c + 1) * points, i * 128 : i * 128 + 128]
+                if r >= 9:
+                    tails.append((r - 9, value))
+                else:
+                    directs.append((r, value))
+        if pair == 2:
+            tails = [value for _, value in sorted(tails, key=lambda entry: entry[0])]
+        for r, value in directs:
+            spare = pltpu.roll(tails[r // 3], 96 - 32 * (r % 3), 1)
+            value = jnp.where(lane < 96, value, spare)
+            for g in range(groups):
+                out_ref[pl.ds(g * returned + r, planes, stride=9), :] = value[planes * g : planes * g + planes]
+        directs = []
+    l1 = lane_of((1, 128))
+    ride = jnp.zeros((1, 128), f32)
+    entries = []
+    for p in range(trials):
+        kinetic = jnp.sum(jnp.where((l1 >= p * half) & (l1 < (p + 1) * half), energy, 0.0), axis=1, keepdims=True)
+        off = alpha[p] - stat_ref[0:1, 1 + p : 2 + p]
+        at_p = sums_ref[0:1, 5 + p : 6 + p] - 2.0 * off * sums_ref[0:1, 1 + p : 2 + p] + off * off * sums_ref[0:1, 0:1]
+        ride = jnp.where(l1 == 96 + p, kinetic + at_p, ride)
+        entries += [(0, p, alpha[p]), (0, 4 + p, start[p])]
+    scal_ref[...] = tile_of((8, 128), entries)
+    for g in range(groups):
+        out_ref[g * returned + 108 : g * returned + 112, :] = jnp.broadcast_to(ride, (4, 128))
     fetch.wait()
 
 
 def step_kernel(in_ref, scal_ref, tail_ref, base_ref, step_ref, out_ref, tail, sems):
-    shares = jnp.sum(in_ref[pl.ds(0, groups, stride=chunk), :], axis=0, keepdims=True)
+    shares = jnp.sum(in_ref[pl.ds(108, groups, stride=returned), :], axis=0, keepdims=True)
     lane = lane_of((1, 128))
     start = jnp.where((lane >= 4) & (lane < 8), scal_ref[0:1, :], 0.0)
     curvature = pltpu.roll(jnp.where((lane >= 96) & (lane < 100), shares, 0.0), 36, 1)
@@ -385,16 +403,17 @@
     copies = [begin(field_far, field_ref, sems.at[0]), begin(o_far, o_ref, sems.at[1])]
     alpha = [step_ref[0:1, p : p + 1] for p in range(trials)]
     step = [step_ref[0:1, 8 + p : 9 + p] for p in range(trials)]
+    narrow = lane_of((groups, 128))
+
+    def waves_of(x):
+        r = [in_ref[pl.ds(x * 9 + n, groups, stride=returned), :] for n in range(9)]
+        for n in range(3):
+            r0, r1, r2 = (pltpu.roll(r[3 * n + t], 32 + 32 * t, 1) for t in range(3))
+            r.append(jnp.where(narrow < 32, r0, jnp.where(narrow < 64, r1, r2)))
+        return jnp.concatenate(r, axis=0)
+
     for x in range(0, planes, 2):
-        b = jnp.concatenate(
-            [
-                jnp.concatenate(
-                    [in_ref[pl.ds((x + i) * 12 + r, groups, stride=chunk), :] for r in range(12)], axis=0
-                )
-                for i in range(2)
-            ],
-            axis=1,
-        )
+        b = jnp.concatenate([waves_of(x), waves_of(x + 1)], axis=1)
         v = left_table(g4, b)
         for i in range(2):
             real[pl.ds(x + i, points, stride=planes), :] = v[:points, i * 128 : i * 128 + 128]
@@ -506,7 +525,7 @@
 
 
 BIG = 56000000
-HUGE = 60000000
+SOME = 54500000
 
 
 def shape(*dims, dtype=f32):
@@ -544,12 +563,12 @@
 
 def forward(pieces, o, tables):
     return call(
-        forward_kernel, [far] * 11,
+        forward_kernel, [hbm] * 8 + [far] * 3,
         (shape(5, rows, 128), shape(rows, 128), shape(8, 128)),
         [buffer(rows, 128), buffer(5, rows, 128), buffer(bands, 144, 128), buffer(2, 640, 256, dtype=bf16), buffer(2, 96, 192, dtype=bf16), buffer(rows, 128),
          buffer(rows, 640, dtype=bf16), buffer(rows, 640, dtype=bf16), buffer(rows, 128), buffer(rows, 128),
          pltpu.SemaphoreType.DMA((11,))],
-        name="forward", room=HUGE, places=(far, far, vmem),
+        name="forward", room=SOME, places=(far, far, vmem),
     )(*pieces, o, tables["w1"], tables["g1"])
 
 
@@ -571,7 +590,7 @@
 
 def waves(arrived, stat, sums, g2, g3, base):
     return call(
-        wave_kernel, [vmem] * 5 + [far], (shape(rows, 128), shape(8, 128), shape(bands, 8, 128)),
+        wave_kernel, [vmem] * 5 + [far], (shape(groups * returned, 128), shape(8, 128), shape(bands, 8, 128)),
         [pltpu.SemaphoreType.DMA((1,))], name="waves", room=8 * 2**20,
     )(arrived, stat, sums, g2, g3, base)
 
@@ -602,7 +621,7 @@
     return call(
         last_kernel, [vmem] * 5 + [far, hbm, far, far], (cells, shape(planes, trials, 288)),
         [buffer(144, 128), buffer(bands, 32, 128), part, part, part, pltpu.SemaphoreType.DMA((3, 6)), pltpu.SemaphoreType.DMA((6,))],
-        name="last", room=BIG, places=(far, vmem),
+        name="last", room=SOME, places=(far, vmem),
     )(step, *norms, packed, band, response, residual)
 
 
@@ -618,16 +637,17 @@
     return lax.ppermute(value, "band", [(s, s ^ (odd if s & 1 else even)) for s in range(bands)])
 
 
-along_z, along_y = (8, 16, 24), (2, 4, 6)
+first_masks = ((8, 8), (16, 2), (24, 10))
+second_masks = ((2, 24), (4, 6), (6, 30))
 
 
 def gather_first(packed):
     value = packed[None]
-    return jnp.concatenate([value] + [crossed(value, z, y) for z, y in zip(along_z, along_y)], axis=0)
+    return jnp.concatenate([value] + [crossed(value, *masks) for masks in first_masks], axis=0)
 
 
 def gather_second(quad):
-    quads = [quad] + [crossed(quad, y, z) for z, y in zip(along_z, along_y)]
+    quads = [quad] + [crossed(quad, *masks) for masks in second_masks]
     return quads + [swapped(q, "band", bands, 1) for q in quads]
 
 
@@ -642,7 +662,7 @@
     arrived = lax.all_to_all(sent.reshape(groups, chunk, 128), "grid", 0, 0, tiled=True).reshape(rows, 128)
     sums, g2, g3, g4, w2 = local_sums(energies, fields, o_far, stat, tables)
     back, scal, tail = waves(arrived, stat, sums, g2, g3, base)
-    back = lax.all_to_all(back.reshape(groups, chunk, 128), "grid", 0, 0, tiled=True).reshape(rows, 128)
+    back = lax.all_to_all(back.reshape(groups, returned, 128), "grid", 0, 0, tiled=True).reshape(groups * returned, 128)
     step, payload = steps(back, scal, tail, base)
     band = lax.all_to_all(payload, "band", 0, 0, tiled=True)
     response, residual, norm = image(energies, back, step, fields, o_far, g4, w2)

time: 108 us -> 103 us (0.954)
  waiting for transfers between devices: 22.3 us -> 19.2 us
  starting transfers between devices: 34.2 us -> 36.8 us
  local copies, waits for them, and re-layouts: 5.03 us -> 3.12 us
  blocking collectives: 13.4 us -> 11.6 us
    ppermute x8, starting transfers between devices: 7.46 us -> 11.6 us  [swapped(): return lax.ppermute(value, axis, [(s, s ^ mask) for s in range(size)])]
    ppermute x6, waiting for transfers between devices: 10.6 us -> 7.37 us  [crossed(): lax.ppermute(value, 'band', [(s, s ^ (odd if s & 1 else even)) for s in r...]
    all_to_all x1, starting transfers between devices: 10.1 us -> 7.78 us  [on_device(): band = lax.all_to_all(payload, 'band', 0, 0, tiled=True)]
    unnamed x31 -> x15, local copies, waits for them, and re-layouts: 5.03 us -> 3.12 us
    all_to_all x1, blocking collectives: 13.4 us -> 11.6 us  [on_device(): lax.all_to_all(back.reshape(groups, returned, 128), 'grid', 0, 0, tiled=T...]
    all_to_all x1, waiting for transfers between devices: 2.46 us -> 1.2 us  [on_device(): band = lax.all_to_all(payload, 'band', 0, 0, tiled=True)]
  transfers between devices with their start and end apart: 16 -> 16, of which waited for: 8 -> 9; matrix products, arithmetic and copies ran while one was open for 2% -> 2% of each run, Pallas kernels for 14% -> 15%
where the time goes in v5:
time: 103 us; the launch traced here: 102 us
  starting transfers between devices  36.8 us (36%)
  Pallas kernels  30.2 us (29%)
  waiting for transfers between devices  19.2 us (19%)
  blocking collectives  11.6 us (11%)
  local copies, waits for them, and re-layouts  3.12 us (3%)
  between operations  1.45 us (1%)
    ppermute x6, starting transfers between devices, crossed(): lax.ppermute(value, 'band', [(s, s ^ (odd if s & 1 else even)) for s in r...  13.4 us
    ppermute x8, starting transfers between devices, swapped(): return lax.ppermute(value, axis, [(s, s ^ mask) for s in range(size)])  11.6 us
    all_to_all x1, blocking collectives, on_device(): lax.all_to_all(back.reshape(groups, returned, 128), 'grid', 0, 0, tiled=T...  11.6 us
    pallas_call x1, Pallas kernels, image(): call(image_kernel, [smem, vmem, vmem, far, far, vmem, vmem], (cells, cell...  7.87 us
    all_to_all x1, starting transfers between devices, on_device(): band = lax.all_to_all(payload, 'band', 0, 0, tiled=True)  7.78 us
    ppermute x6, waiting for transfers between devices, crossed(): lax.ppermute(value, 'band', [(s, s ^ (odd if s & 1 else even)) for s in r...  7.37 us
    ppermute x8, waiting for transfers between devices, swapped(): return lax.ppermute(value, axis, [(s, s ^ mask) for s in range(size)])  6.8 us
    pallas_call x1, Pallas kernels, forward(): call(forward_kernel, [hbm] * 8 + [far] * 3, (shape(5, rows, 128), shape(r...  6.44 us
  transfers between devices with their start and end apart: 16, of which 9 were waited for; matrix products, arithmetic and copies ran while one was open for 2% of the time, Pallas kernels for 15%

profile of v5, /device:TPU:1, one launch (start us, length us, event | category | flops | bytes accessed | tf_op | source)
XLA Modules:
  0.0 102.5 jit_solution(12909852780921065763)
XLA Ops:
  0.6 0.0 copy-start.4
  0.6 1.7 %pack.1.packed_ref = f32[144,128]{1,0:T(8,128)} custom-call(f32[12,4,288]{2,1,0:T(4,128)} %bitcast.27, f32[12,288]{1,0:T(8,128)} %local_far.1), custom_call_target="tpu_custom_call" | custom-call | flops 1000000 | bytes 1000000 | tf_op jit(solution)/shard_map/pack/pallas_call | solution.py:545
  2.4 4.9 %collective-permute-start.2 = (f32[1,144,128]{2,1,0:T(8,128)}, f32[1,144,128]{2,1,0:T(8,128)S(1)}, u32[]{:S(2)}, u32[]{:S(2)}) collective-permute-start(f32[1,144,128]{2,1,0:T(8,128)} %bitcast.19), channel_id=1, source_target_pairs={{0,192},{8,88},{16,208},{24,72},{32,224},{40,120},{48,240},{56,104... | collective-permute-start | bytes 221192 | tf_op jit(solution)/shard_map/ppermute | solution.py:637
  7.3 0.2 collective-permute-start.1
  7.5 0.2 collective-permute-start
  7.7 1.9 %copy.15.o_ref = f32[1,12,9216]{2,1,0:T(8,128)} copy(f32[1,12,9216]{2,0,1:T(1,128)} %param.10) | data formatting | bytes 884736 | tf_op args[0]
  9.6 0.0 copy-start.1
  9.6 0.9 copy-done.1
  10.5 2.4 %orbital_rows.1 = (f32[1152,128]{1,0:T(8,128)}, f32[32,32,128]{2,1,0:T(8,128)}, f32[144,128]{1,0:T(8,128)S(1)}) custom-call(f32[1,12,9216]{2,1,0:T(8,128)} %copy.15.o_ref, f32[144,128]{1,0:T(8,128)S(1)} %copy-done.1), custom_call_target="tpu_custom_call" | custom-call | flops 1000000 | bytes 1000000 | tf_op jit(solution)/shard_map/orbital_rows/pallas_call | solution.py:552
  12.9 0.0 collective-permute-done.2
  12.9 0.0 collective-permute-done.1
  12.9 0.0 collective-permute-done
  12.9 0.0 copy-start.2
  12.9 0.0 copy-start.3
  13.0 7.7 %collective-permute-start.5 = (f32[4,144,128]{2,1,0:T(8,128)S(1)}, f32[4,144,128]{2,1,0:T(8,128)S(1)}, u32[]{:S(2)}, u32[]{:S(2)}) collective-permute-start(f32[4,144,128]{2,1,0:T(8,128)S(1)} %pad_maximum_fusion.p0), channel_id=1, source_target_pairs={{0,48},{8,248},{16,32},{24,232},{32,16},{40,216},{48,0},{56,200},{... | collective-permute-start | bytes 884744 | tf_op jit(solution)/shard_map/ppermute | solution.py:637
  20.7 0.0 collective-permute-start.4
  20.7 0.4 collective-permute-start.3
  21.1 2.2 %collective-permute-start.6 = (f32[4,144,128]{2,1,0:T(8,128)S(1)}, f32[4,144,128]{2,1,0:T(8,128)S(1)}, u32[]{:S(2)}, u32[]{:S(2)}) collective-permute-start(f32[4,144,128]{2,1,0:T(8,128)S(1)} %pad_maximum_fusion.p0), channel_id=1, source_target_pairs={{0,8},{8,0},{16,24},{24,16},{32,40},{40,32},{48,56},{56,48},{64,72... | collective-permute-start | bytes 884744 | tf_op jit(solution)/shard_map/ppermute | solution.py:633
  23.3 7.4 %collective-permute-done.5.p3 = f32[4,144,128]{2,1,0:T(8,128)S(1)} collective-permute-done((f32[4,144,128]{2,1,0:T(8,128)S(1)}, f32[4,144,128]{2,1,0:T(8,128)S(1)}, u32[]{:S(2)}, u32[]{:S(2)}) %collective-permute-start.5) | collective-permute-done | bytes 294944 | tf_op jit(solution)/shard_map/ppermute | solution.py:637
  30.7 4.8 %collective-permute-start.9 = (f32[4,144,128]{2,1,0:T(8,128)S(1)}, f32[4,144,128]{2,1,0:T(8,128)S(1)}, u32[]{:S(2)}, u32[]{:S(2)}) collective-permute-start(f32[4,144,128]{2,1,0:T(8,128)S(1)} %collective-permute-done.5.p3), channel_id=1, source_target_pairs={{0,8},{8,0},{16,24},{24,16},{32,40},{40,32},{48,56},{56,48},{64,72... | collective-permute-start | bytes 884744 | tf_op jit(solution)/shard_map/ppermute | solution.py:633
  35.4 0.0 collective-permute-done.4.p2
  35.4 0.0 collective-permute-start.8
  35.4 0.0 collective-permute-done.3.p1
  35.4 0.5 collective-permute-start.7
  35.9 0.0 collective-permute-done.6.p4
  35.9 0.7 collective-permute-done.9.p7
  36.6 0.0 copy-start.5
  36.6 0.4 collective-permute-done.8.p6
  37.1 0.0 copy-start.6
  37.1 0.4 collective-permute-done.7.p5
  37.5 0.0 copy-done.5
  37.5 0.3 copy-done.6
  37.8 0.0 copy-done.4
  37.8 6.4 %forward.1 = (f32[5,1152,128]{2,1,0:T(8,128)}, f32[1152,128]{1,0:T(8,128)}, f32[8,128]{1,0:T(8,128)S(1)}) custom-call(f32[4,144,128]{2,1,0:T(8,128)S(1)} %pad_maximum_fusion.p0, f32[4,144,128]{2,1,0:T(8,128)S(1)} %collective-permute-done.3.p1, f32[4,144,128]{2,1,0:T(8,128)S(1)} %collective-permute-done.4.p2, f32[4,144,128]{2,1,0:T(8,128)S(1)} %collective-permute-done.5.p3, ...), custom_call_target="tpu_custom_call" | custom-call | flops 1000000 | bytes 1000000 | tf_op jit(solution)/shard_map/forward/pallas_call | solution.py:565
  44.2 4.0 %all-to-all-start = ((f32[8,144,128]{2,1,0:T(8,128)}), f32[8,144,128]{2,1,0:T(8,128)S(1)}, u32[]{:S(2)}, u32[]{:S(2)}) async-start(f32[8,144,128]{2,1,0:T(8,128)} %bitcast.26), calls=%async_computation | async-start | bytes 1179648 | tf_op jit(solution)/shard_map/all_to_all | solution.py:662
  48.9 0.0 copy-done.2
  48.9 0.0 copy-done.3
  48.9 5.4 %local_sums.1 = (f32[8,128]{1,0:T(8,128)S(1)}, bf16[2,96,192]{2,1,0:T(8,128)(2,1)S(1)}, bf16[2,192,96]{2,1,0:T(8,128)(2,1)S(1)}, bf16[2,192,96]{2,1,0:T(8,128)(2,1)S(1)}, bf16[2,256,512]{2,1,0:T(8,128)(2,1)}) custom-call(f32[1]{0:T(128)S(6)} %copy.17.energy_ref, f32[5,1152,128]{2,1,0:T(8,128)} %get-tuple-element.32.field_ref.field_far, ...), custom_call_target="tpu_custom_call" | custom-call | flops 10000000 | bytes 10000000 | tf_op jit(solution)/shard_map/local_sums/pallas_call | solution.py:579
  54.3 3.9 %all-to-all-done = f32[8,144,128]{2,1,0:T(8,128)S(1)} async-done(((f32[8,144,128]{2,1,0:T(8,128)}), f32[8,144,128]{2,1,0:T(8,128)S(1)}, u32[]{:S(2)}, u32[]{:S(2)}) %all-to-all-start) | async-done | bytes 589856 | tf_op jit(solution)/shard_map/all_to_all | solution.py:662
  58.1 1.9 %waves.1 = (f32[896,128]{1,0:T(8,128)S(1)}, f32[8,128]{1,0:T(8,128)S(1)}, f32[32,8,128]{2,1,0:T(8,128)S(1)}) custom-call(f32[1152,128]{1,0:T(8,128)S(1)} %bitcast.16, f32[8,128]{1,0:T(8,128)S(1)} %get-tuple-element.31.stat_ref, f32[8,128]{1,0:T(8,128)S(1)} %get-tuple-element.33.sums_ref, bf16[2,96,192]{2,1,0:T(8,128)(2,1)S(1)} %get-tuple-element.34.g2, ...), custom_call_target="tpu_custom_call" | custom-call | flops 1000000 | bytes 1000000 | tf_op jit(solution)/shard_map/waves/pallas_call | solution.py:592
  60.0 11.6 %all_to_all.15 = f32[8,112,128]{2,1,0:T(8,128)S(1)} all-to-all(f32[8,112,128]{2,1,0:T(8,128)S(1)} %bitcast.23), channel_id=1, replica_groups=mesh['band'=32,'grid'=8] {'grid'}, dimensions={0} | all-to-all | bytes 917504 | tf_op jit(solution)/shard_map/all_to_all | solution.py:665
  71.6 0.0 copy-start
  71.6 0.8 steps.1
  72.5 7.8 %all-to-all-start.2 = ((f32[32,32,128]{2,1,0:T(8,128)}), f32[32,32,128]{2,1,0:T(8,128)S(1)}, u32[]{:S(2)}, u32[]{:S(2)}) async-start(f32[32,32,128]{2,1,0:T(8,128)} %get-tuple-element.47), calls=%async_computation.2 | async-start | bytes 1048576 | tf_op jit(solution)/shard_map/all_to_all | solution.py:667
  80.3 0.0 copy-done
  80.3 7.9 %image.1 = (f32[12,4,9216]{2,1,0:T(4,128)}, f32[12,4,9216]{2,1,0:T(4,128)}, f32[8,128]{1,0:T(8,128)S(1)}) custom-call(f32[1]{0:T(128)S(6)} %copy.17.energy_ref, f32[896,128]{1,0:T(8,128)} %bitcast.18, f32[8,128]{1,0:T(8,128)S(1)} %get-tuple-element.40.step_ref, f32[5,1152,128]{2,1,0:T(8,128)} %get-tuple-element.32.field_ref.field_far, ...), custom_call_target="tpu_custom_call" | custom-call | flops 20000000000 | bytes 1000000 | tf_op jit(solution)/shard_map/image/pallas_call | solution.py:608
  88.1 0.6 collective-permute-start.10
  88.8 2.4 %collective-permute-done.10 = f32[8,128]{1,0:T(8,128)S(1)} collective-permute-done((f32[8,128]{1,0:T(8,128)S(1)}, f32[8,128]{1,0:T(8,128)S(1)}, u32[]{:S(2)}, u32[]{:S(2)}) %collective-permute-start.10) | collective-permute-done | bytes 4128 | tf_op jit(solution)/shard_map/ppermute | solution.py:633
  91.2 2.3 %collective-permute-start.13 = (f32[8,128]{1,0:T(8,128)S(1)}, f32[8,128]{1,0:T(8,128)S(1)}, u32[]{:S(2)}, u32[]{:S(2)}) collective-permute-start(f32[8,128]{1,0:T(8,128)S(1)} %add.3.n0), channel_id=1, source_target_pairs={{0,6},{1,7},{2,4},{3,5},{4,2},{5,3},{6,0},{7,1},{8,14},{9,15},{10,... | collective-permute-start | bytes 12296 | tf_op jit(solution)/shard_map/ppermute | solution.py:633
  93.4 1.2 %collective-permute-start.12 = (f32[8,128]{1,0:T(8,128)S(1)}, f32[8,128]{1,0:T(8,128)S(1)}, u32[]{:S(2)}, u32[]{:S(2)}) collective-permute-start(f32[8,128]{1,0:T(8,128)S(1)} %add.3.n0), channel_id=1, source_target_pairs={{0,4},{1,5},{2,6},{3,7},{4,0},{5,1},{6,2},{7,3},{8,12},{9,13},{10,... | collective-permute-start | bytes 12296 | tf_op jit(solution)/shard_map/ppermute | solution.py:633
  94.6 0.0 collective-permute-start.11
  94.6 0.5 collective-permute-done.13.n3
  95.1 2.4 %collective-permute-done.12.n2 = f32[8,128]{1,0:T(8,128)S(1)} collective-permute-done((f32[8,128]{1,0:T(8,128)S(1)}, f32[8,128]{1,0:T(8,128)S(1)}, u32[]{:S(2)}, u32[]{:S(2)}) %collective-permute-start.12) | collective-permute-done | bytes 4128 | tf_op jit(solution)/shard_map/ppermute | solution.py:633
  97.5 0.0 collective-permute-done.11.n1
  97.5 1.2 %all-to-all-done.2.band_ref = f32[32,32,128]{2,1,0:T(8,128)S(1)} async-done(((f32[32,32,128]{2,1,0:T(8,128)}), f32[32,32,128]{2,1,0:T(8,128)S(1)}, u32[]{:S(2)}, u32[]{:S(2)}) %all-to-all-start.2) | async-done | bytes 524320 | tf_op jit(solution)/shard_map/all_to_all | solution.py:667
  98.7 3.7 %last.1 = (f32[12,4,9216]{2,1,0:T(4,128)}, f32[12,4,288]{2,1,0:T(4,128)}) custom-call(f32[8,128]{1,0:T(8,128)S(1)} %get-tuple-element.40.step_ref, f32[8,128]{1,0:T(8,128)S(1)} %add.3.n0, f32[8,128]{1,0:T(8,128)S(1)} %collective-permute-done.11.n1, f32[8,128]{1,0:T(8,128)S(1)} %collective-permute-done.12.n2, f32[8,128]{1,0:T(8,128)S(1)} %collective-permute-done.13.n3, ...), custom_call_target="tpu_custom_call" | custom-call | flops 1000000 | bytes 1000000 | tf_op jit(solution)/shard_map/last/pallas_call | solution.py:621
  (2 shorter events, 0.0 us)
Async XLA Ops:
  0.6 37.1 %copy-start.4 = (bf16[2,96,192]{2,1,0:T(8,128)(2,1)S(1)}, bf16[2,96,192]{2,1,0:T(8,128)(2,1)}, u32[]{:S(2)}) copy-start(bf16[2,96,192]{2,1,0:T(8,128)(2,1)} %constant.13.clone.g1_ref) | copy-start | bytes 221188
  2.4 10.5 %collective-permute-start.2 = (f32[1,144,128]{2,1,0:T(8,128)}, f32[1,144,128]{2,1,0:T(8,128)S(1)}, u32[]{:S(2)}, u32[]{:S(2)}) collective-permute-start(f32[1,144,128]{2,1,0:T(8,128)} %bitcast.19), channel_id=1, source_target_pairs={{0,192},{8,88},{16,208},{24,72},{32,224},{40,120},{48,240},{56,104... | collective-permute-start | bytes 221192 | tf_op jit(solution)/shard_map/ppermute | solution.py:637
  7.3 5.6 %collective-permute-start.1 = (f32[1,144,128]{2,1,0:T(8,128)}, f32[1,144,128]{2,1,0:T(8,128)S(1)}, u32[]{:S(2)}, u32[]{:S(2)}) collective-permute-start(f32[1,144,128]{2,1,0:T(8,128)} %bitcast.20), channel_id=1, source_target_pairs={{0,128},{8,24},{16,144},{24,8},{32,160},{40,56},{48,176},{56,40},{... | collective-permute-start | bytes 221192 | tf_op jit(solution)/shard_map/ppermute | solution.py:637
  7.5 5.4 %collective-permute-start = (f32[1,144,128]{2,1,0:T(8,128)}, f32[1,144,128]{2,1,0:T(8,128)S(1)}, u32[]{:S(2)}, u32[]{:S(2)}) collective-permute-start(f32[1,144,128]{2,1,0:T(8,128)} %bitcast.21), channel_id=1, source_target_pairs={{0,64},{8,72},{16,80},{24,88},{32,96},{40,104},{48,112},{56,120},{... | collective-permute-start | bytes 221192 | tf_op jit(solution)/shard_map/ppermute | solution.py:637
  9.6 0.9 copy-start.1
  12.9 36.0 %copy-start.2 = (bf16[2,192,96]{2,1,0:T(8,128)(2,1)S(1)}, bf16[2,192,96]{2,1,0:T(8,128)(2,1)}, u32[]{:S(2)}) copy-start(bf16[2,192,96]{2,1,0:T(8,128)(2,1)} %constant.15.clone.g3_ref) | copy-start | bytes 221188
  12.9 36.0 %copy-start.3 = (bf16[2,96,192]{2,1,0:T(8,128)(2,1)S(1)}, bf16[2,96,192]{2,1,0:T(8,128)(2,1)}, u32[]{:S(2)}) copy-start(bf16[2,96,192]{2,1,0:T(8,128)(2,1)} %constant.14.clone.g2_ref) | copy-start | bytes 221188
  13.0 17.7 %collective-permute-start.5 = (f32[4,144,128]{2,1,0:T(8,128)S(1)}, f32[4,144,128]{2,1,0:T(8,128)S(1)}, u32[]{:S(2)}, u32[]{:S(2)}) collective-permute-start(f32[4,144,128]{2,1,0:T(8,128)S(1)} %pad_maximum_fusion.p0), channel_id=1, source_target_pairs={{0,48},{8,248},{16,32},{24,232},{32,16},{40,216},{48,0},{56,200},{... | collective-permute-start | bytes 884744 | tf_op jit(solution)/shard_map/ppermute | solution.py:637
  20.7 14.7 %collective-permute-start.4 = (f32[4,144,128]{2,1,0:T(8,128)S(1)}, f32[4,144,128]{2,1,0:T(8,128)S(1)}, u32[]{:S(2)}, u32[]{:S(2)}) collective-permute-start(f32[4,144,128]{2,1,0:T(8,128)S(1)} %pad_maximum_fusion.p0), channel_id=1, source_target_pairs={{0,32},{8,56},{16,48},{24,40},{32,0},{40,24},{48,16},{56,8},{64,96... | collective-permute-start | bytes 884744 | tf_op jit(solution)/shard_map/ppermute | solution.py:637
  20.7 14.8 %collective-permute-start.3 = (f32[4,144,128]{2,1,0:T(8,128)S(1)}, f32[4,144,128]{2,1,0:T(8,128)S(1)}, u32[]{:S(2)}, u32[]{:S(2)}) collective-permute-start(f32[4,144,128]{2,1,0:T(8,128)S(1)} %pad_maximum_fusion.p0), channel_id=1, source_target_pairs={{0,16},{8,200},{16,0},{24,216},{32,48},{40,232},{48,32},{56,248},{... | collective-permute-start | bytes 884744 | tf_op jit(solution)/shard_map/ppermute | solution.py:637
  21.1 14.9 %collective-permute-start.6 = (f32[4,144,128]{2,1,0:T(8,128)S(1)}, f32[4,144,128]{2,1,0:T(8,128)S(1)}, u32[]{:S(2)}, u32[]{:S(2)}) collective-permute-start(f32[4,144,128]{2,1,0:T(8,128)S(1)} %pad_maximum_fusion.p0), channel_id=1, source_target_pairs={{0,8},{8,0},{16,24},{24,16},{32,40},{40,32},{48,56},{56,48},{64,72... | collective-permute-start | bytes 884744 | tf_op jit(solution)/shard_map/ppermute | solution.py:633
  30.7 6.0 %collective-permute-start.9 = (f32[4,144,128]{2,1,0:T(8,128)S(1)}, f32[4,144,128]{2,1,0:T(8,128)S(1)}, u32[]{:S(2)}, u32[]{:S(2)}) collective-permute-start(f32[4,144,128]{2,1,0:T(8,128)S(1)} %collective-permute-done.5.p3), channel_id=1, source_target_pairs={{0,8},{8,0},{16,24},{24,16},{32,40},{40,32},{48,56},{56,48},{64,72... | collective-permute-start | bytes 884744 | tf_op jit(solution)/shard_map/ppermute | solution.py:633
  35.4 1.6 %collective-permute-start.8 = (f32[4,144,128]{2,1,0:T(8,128)S(1)}, f32[4,144,128]{2,1,0:T(8,128)S(1)}, u32[]{:S(2)}, u32[]{:S(2)}) collective-permute-start(f32[4,144,128]{2,1,0:T(8,128)S(1)} %collective-permute-done.4.p2), channel_id=1, source_target_pairs={{0,8},{8,0},{16,24},{24,16},{32,40},{40,32},{48,56},{56,48},{64,72... | collective-permute-start | bytes 884744 | tf_op jit(solution)/shard_map/ppermute | solution.py:633
  35.4 2.0 %collective-permute-start.7 = (f32[4,144,128]{2,1,0:T(8,128)S(1)}, f32[4,144,128]{2,1,0:T(8,128)S(1)}, u32[]{:S(2)}, u32[]{:S(2)}) collective-permute-start(f32[4,144,128]{2,1,0:T(8,128)S(1)} %collective-permute-done.3.p1), channel_id=1, source_target_pairs={{0,8},{8,0},{16,24},{24,16},{32,40},{40,32},{48,56},{56,48},{64,72... | collective-permute-start | bytes 884744 | tf_op jit(solution)/shard_map/ppermute | solution.py:633
  36.6 0.8 copy-start.5
  37.1 0.7 copy-start.6
  44.2 13.9 %all-to-all-start = ((f32[8,144,128]{2,1,0:T(8,128)}), f32[8,144,128]{2,1,0:T(8,128)S(1)}, u32[]{:S(2)}, u32[]{:S(2)}) async-start(f32[8,144,128]{2,1,0:T(8,128)} %bitcast.26), calls=%async_computation | async-start | bytes 1179648 | tf_op jit(solution)/shard_map/all_to_all | solution.py:662
  71.6 8.6 %copy-start = (f32[8,112,128]{2,1,0:T(8,128)}, f32[8,112,128]{2,1,0:T(8,128)S(1)}, u32[]{:S(2)}) copy-start(f32[8,112,128]{2,1,0:T(8,128)S(1)} %all_to_all.15) | copy-start | bytes 1376260
  72.5 26.3 %all-to-all-start.2 = ((f32[32,32,128]{2,1,0:T(8,128)}), f32[32,32,128]{2,1,0:T(8,128)S(1)}, u32[]{:S(2)}, u32[]{:S(2)}) async-start(f32[32,32,128]{2,1,0:T(8,128)} %get-tuple-element.47), calls=%async_computation.2 | async-start | bytes 1048576 | tf_op jit(solution)/shard_map/all_to_all | solution.py:667
  88.1 3.0 %collective-permute-start.10 = (f32[8,128]{1,0:T(8,128)S(1)}, f32[8,128]{1,0:T(8,128)S(1)}, u32[]{:S(2)}, u32[]{:S(2)}) collective-permute-start(f32[8,128]{1,0:T(8,128)S(1)} %get-tuple-element.45), channel_id=1, source_target_pairs={{0,1},{1,0},{2,3},{3,2},{4,5},{5,4},{6,7},{7,6},{8,9},{9,8},{10,11... | collective-permute-start | bytes 12296 | tf_op jit(solution)/shard_map/ppermute | solution.py:633
  91.2 4.0 %collective-permute-start.13 = (f32[8,128]{1,0:T(8,128)S(1)}, f32[8,128]{1,0:T(8,128)S(1)}, u32[]{:S(2)}, u32[]{:S(2)}) collective-permute-start(f32[8,128]{1,0:T(8,128)S(1)} %add.3.n0), channel_id=1, source_target_pairs={{0,6},{1,7},{2,4},{3,5},{4,2},{5,3},{6,0},{7,1},{8,14},{9,15},{10,... | collective-permute-start | bytes 12296 | tf_op jit(solution)/shard_map/ppermute | solution.py:633
  93.4 4.1 %collective-permute-start.12 = (f32[8,128]{1,0:T(8,128)S(1)}, f32[8,128]{1,0:T(8,128)S(1)}, u32[]{:S(2)}, u32[]{:S(2)}) collective-permute-start(f32[8,128]{1,0:T(8,128)S(1)} %add.3.n0), channel_id=1, source_target_pairs={{0,4},{1,5},{2,6},{3,7},{4,0},{5,1},{6,2},{7,3},{8,12},{9,13},{10,... | collective-permute-start | bytes 12296 | tf_op jit(solution)/shard_map/ppermute | solution.py:633
  94.6 2.9 %collective-permute-start.11 = (f32[8,128]{1,0:T(8,128)S(1)}, f32[8,128]{1,0:T(8,128)S(1)}, u32[]{:S(2)}, u32[]{:S(2)}) collective-permute-start(f32[8,128]{1,0:T(8,128)S(1)} %add.3.n0), channel_id=1, source_target_pairs={{0,2},{1,3},{2,0},{3,1},{4,6},{5,7},{6,4},{7,5},{8,10},{9,11},{10,... | collective-permute-start | bytes 12296 | tf_op jit(solution)/shard_map/ppermute | solution.py:633

commit v6 on v5

--- a/solution.py
+++ b/solution.py
@@ -273,10 +273,10 @@
     kept.wait()
 
 
-def local_kernel(energy_ref, field_ref, o_ref, stat_ref, g2_ref, g3_ref, g4_ref, w2_ref,
-                 out_ref, g2, g3, g4, w2, sums, sems):
+def local_kernel(energy_ref, field_ref, o_ref, stat_ref, g2_ref, g3_ref, g4_ref, w2_ref, base_ref,
+                 out_ref, g2, g3, g4, w2, tail_ref, sums, sems):
     step = pl.program_id(0)
-    pairs = ((g2_ref, g2), (g3_ref, g3), (g4_ref, g4), (w2_ref, w2))
+    pairs = ((g2_ref, g2), (g3_ref, g3), (g4_ref, g4), (w2_ref, w2), (base_ref.at[:, pl.ds(24, 8), :], tail_ref))
 
     @pl.when(step == 0)
     def _():
@@ -300,9 +300,8 @@
             pltpu.make_async_copy(source, target, sems.at[n]).wait()
 
 
-def wave_kernel(in_ref, stat_ref, sums_ref, g2, g3, base_ref, out_ref, scal_ref, tail_ref, sems):
+def wave_kernel(in_ref, stat_ref, sums_ref, g2, g3, out_ref, scal_ref):
     owner = lax.axis_index("grid")
-    fetch = begin(base_ref.at[:, pl.ds(24, 8), :], tail_ref, sems.at[0])
     s0 = in_ref[pl.ds(0, points, stride=planes), :]
     s1 = in_ref[pl.ds(1, points, stride=planes), :]
     weight = s0[:, 120:121]
@@ -379,7 +378,6 @@
     scal_ref[...] = tile_of((8, 128), entries)
     for g in range(groups):
         out_ref[g * returned + 108 : g * returned + 112, :] = jnp.broadcast_to(ride, (4, 128))
-    fetch.wait()
 
 
 def step_kernel(in_ref, scal_ref, tail_ref, base_ref, step_ref, out_ref, tail, sems):
@@ -400,7 +398,12 @@
                  response_ref, residual_ref, norm_ref,
                  field_ref, o_ref, real, imag, kinetic, mixed_s, mixed_r, flat_s, flat_r, sems, out_sems):
     energy = energy_ref[0]
-    copies = [begin(field_far, field_ref, sems.at[0]), begin(o_far, o_ref, sems.at[1])]
+    third = rows // 3
+    copies = []
+    for n in range(3):
+        at = pl.ds(n * third, third)
+        copies.append((begin(field_far.at[:, at, :], field_ref.at[:, at, :], sems.at[n]),
+                       begin(o_far.at[at], o_ref.at[at], sems.at[3 + n])))
     alpha = [step_ref[0:1, p : p + 1] for p in range(trials)]
     step = [step_ref[0:1, 8 + p : 9 + p] for p in range(trials)]
     narrow = lane_of((groups, 128))
@@ -436,8 +439,6 @@
         return 0
 
     lax.fori_loop(0, rows // big, along_z, 0)
-    for copy in copies:
-        copy.wait()
 
     def back(i, sums):
         at = pl.ds(pl.multiple_of(i * size, size), size)
@@ -461,7 +462,11 @@
         begin(flat_r.at[i], residual_ref.at[:, :, cells], out_sems.at[1, i])
         return tuple(out)
 
-    sums = lax.fori_loop(0, rows // size, back, tuple(jnp.zeros((8, 128), f32) for _ in range(trials)))
+    sums = tuple(jnp.zeros((8, 128), f32) for _ in range(trials))
+    for n in range(3):
+        for copy in copies[n]:
+            copy.wait()
+        sums = lax.fori_loop(n * (third // size), (n + 1) * (third // size), back, sums)
     norm_ref[...] = tile_of((8, 128), [(0, p, total(s)) for p, s in enumerate(sums)])
     for i in range(rows // size):
         cells = pl.ds(i * 768, 768)
@@ -572,27 +577,26 @@
     )(*pieces, o, tables["w1"], tables["g1"])
 
 
-def local_sums(energies, fields, o, stat, tables):
+def local_sums(energies, fields, o, stat, tables, base):
     size, count = 192, rows // 192
     tile = pl.BlockSpec((8, 128), lambda i: (0, 0))
     kinds = [tables[name] for name in ("g2", "g3", "g4", "w2")]
     return pl.pallas_call(
         local_kernel, grid=(count,),
         in_specs=[smem, pl.BlockSpec((5, size, 128), lambda i: (0, i, 0)), pl.BlockSpec((size, 128), lambda i: (i, 0)),
-                  tile] + [far] * 4,
-        out_specs=(tile, *[vmem] * 4),
-        out_shape=(shape(8, 128), *[shape(*t.shape, dtype=bf16) for t in kinds]),
-        scratch_shapes=[buffer(9, 8, 128), pltpu.SemaphoreType.DMA((4,))],
+                  tile] + [far] * 5,
+        out_specs=(tile, *[vmem] * 5),
+        out_shape=(shape(8, 128), *[shape(*t.shape, dtype=bf16) for t in kinds], shape(bands, 8, 128)),
+        scratch_shapes=[buffer(9, 8, 128), pltpu.SemaphoreType.DMA((5,))],
         compiler_params=pltpu.CompilerParams(vmem_limit_bytes=BIG), name="local_sums",
         cost_estimate=pl.CostEstimate(flops=10**7, bytes_accessed=10**7, transcendentals=0),
-    )(energies, fields, o, stat, *kinds)
-
-
-def waves(arrived, stat, sums, g2, g3, base):
+    )(energies, fields, o, stat, *kinds, base)
+
+
+def waves(arrived, stat, sums, g2, g3):
     return call(
-        wave_kernel, [vmem] * 5 + [far], (shape(groups * returned, 128), shape(8, 128), shape(bands, 8, 128)),
-        [pltpu.SemaphoreType.DMA((1,))], name="waves", room=8 * 2**20,
-    )(arrived, stat, sums, g2, g3, base)
+        wave_kernel, [vmem] * 5, (shape(groups * returned, 128), shape(8, 128)), name="waves", room=8 * 2**20,
+    )(arrived, stat, sums, g2, g3)
 
 
 def steps(arrived, scal, tail, base):
@@ -610,7 +614,7 @@
         [buffer(5, rows, 128), buffer(rows, 128), buffer(rows, 128), buffer(rows, 128), buffer(rows, 512),
          buffer(384, 128), buffer(384, 128),
          buffer(12, planes, trials, 768), buffer(12, planes, trials, 768),
-         pltpu.SemaphoreType.DMA((2,)), pltpu.SemaphoreType.DMA((2, 12))],
+         pltpu.SemaphoreType.DMA((6,)), pltpu.SemaphoreType.DMA((2, 12))],
         name="image", room=BIG, places=(far, far, vmem), flops=2 * 10**10,
     )(energies, arrived, step, fields, o, g4, w2)
 
@@ -660,8 +664,8 @@
     pieces = gather_second(quad)
     fields, sent, stat = forward(pieces, o_far, tables)
     arrived = lax.all_to_all(sent.reshape(groups, chunk, 128), "grid", 0, 0, tiled=True).reshape(rows, 128)
-    sums, g2, g3, g4, w2 = local_sums(energies, fields, o_far, stat, tables)
-    back, scal, tail = waves(arrived, stat, sums, g2, g3, base)
+    sums, g2, g3, g4, w2, tail = local_sums(energies, fields, o_far, stat, tables, base)
+    back, scal = waves(arrived, stat, sums, g2, g3)
     back = lax.all_to_all(back.reshape(groups, returned, 128), "grid", 0, 0, tiled=True).reshape(groups * returned, 128)
     step, payload = steps(back, scal, tail, base)
     band = lax.all_to_all(payload, "band", 0, 0, tiled=True)

time: 103 us -> 103 us (level)
    unnamed x15 -> x17, local copies, waits for them, and re-layouts: 3.12 us -> 3.13 us
where the time goes in v6:
time: 103 us; the launch traced here: 102 us
  starting transfers between devices  37.2 us (36%)
  Pallas kernels  29.3 us (28%)
  waiting for transfers between devices  19.2 us (19%)
  blocking collectives  11.6 us (11%)
  local copies, waits for them, and re-layouts  3.13 us (3%)
  between operations  1.61 us (2%)
    ppermute x6, starting transfers between devices, crossed(): lax.ppermute(value, 'band', [(s, s ^ (odd if s & 1 else even)) for s in r...  13.4 us
    ppermute x8, starting transfers between devices, swapped(): return lax.ppermute(value, axis, [(s, s ^ mask) for s in range(size)])  12 us
    all_to_all x1, blocking collectives, on_device(): lax.all_to_all(back.reshape(groups, returned, 128), 'grid', 0, 0, tiled=T...  11.6 us
    all_to_all x1, starting transfers between devices, on_device(): band = lax.all_to_all(payload, 'band', 0, 0, tiled=True)  7.76 us
    pallas_call x1, Pallas kernels, image(): call(image_kernel, [smem, vmem, vmem, far, far, vmem, vmem], (cells, cell...  7.58 us
    ppermute x6, waiting for transfers between devices, crossed(): lax.ppermute(value, 'band', [(s, s ^ (odd if s & 1 else even)) for s in r...  7.37 us
    ppermute x8, waiting for transfers between devices, swapped(): return lax.ppermute(value, axis, [(s, s ^ mask) for s in range(size)])  6.76 us
    pallas_call x1, Pallas kernels, forward(): call(forward_kernel, [hbm] * 8 + [far] * 3, (shape(5, rows, 128), shape(r...  6.43 us
  transfers between devices with their start and end apart: 16, of which 9 were waited for; matrix products, arithmetic and copies ran while one was open for 2% of the time, Pallas kernels for 15%

profile of v6, /device:TPU:1, one launch (start us, length us, event | category | flops | bytes accessed | tf_op | source)
XLA Modules:
  0.0 102.0 jit_solution(18079700991013880933)
XLA Ops:
  0.6 0.0 copy-start.5
  0.6 1.7 %pack.1.packed_ref = f32[144,128]{1,0:T(8,128)} custom-call(f32[12,4,288]{2,1,0:T(4,128)} %bitcast.27, f32[12,288]{1,0:T(8,128)} %local_far.1), custom_call_target="tpu_custom_call" | custom-call | flops 1000000 | bytes 1000000 | tf_op jit(solution)/shard_map/pack/pallas_call | solution.py:550
  2.4 4.9 %collective-permute-start.2 = (f32[1,144,128]{2,1,0:T(8,128)}, f32[1,144,128]{2,1,0:T(8,128)S(1)}, u32[]{:S(2)}, u32[]{:S(2)}) collective-permute-start(f32[1,144,128]{2,1,0:T(8,128)} %bitcast.19), channel_id=1, source_target_pairs={{0,192},{8,88},{16,208},{24,72},{32,224},{40,120},{48,240},{56,104... | collective-permute-start | bytes 221192 | tf_op jit(solution)/shard_map/ppermute | solution.py:641
  7.3 0.2 collective-permute-start.1
  7.5 0.2 collective-permute-start
  7.7 1.9 %copy.15.o_ref = f32[1,12,9216]{2,1,0:T(8,128)} copy(f32[1,12,9216]{2,0,1:T(1,128)} %param.10) | data formatting | bytes 884736 | tf_op args[0]
  9.6 0.0 copy-start.1
  9.6 0.9 copy-done.1
  10.5 2.4 %orbital_rows.1 = (f32[1152,128]{1,0:T(8,128)}, f32[32,32,128]{2,1,0:T(8,128)}, f32[144,128]{1,0:T(8,128)S(1)}) custom-call(f32[1,12,9216]{2,1,0:T(8,128)} %copy.15.o_ref, f32[144,128]{1,0:T(8,128)S(1)} %copy-done.1), custom_call_target="tpu_custom_call" | custom-call | flops 1000000 | bytes 1000000 | tf_op jit(solution)/shard_map/orbital_rows/pallas_call | solution.py:557
  12.9 0.0 collective-permute-done.2
  12.9 0.0 collective-permute-done.1
  12.9 0.0 collective-permute-done
  12.9 0.0 copy-start.3
  13.0 0.0 copy-start.4
  13.0 7.7 %collective-permute-start.5 = (f32[4,144,128]{2,1,0:T(8,128)S(1)}, f32[4,144,128]{2,1,0:T(8,128)S(1)}, u32[]{:S(2)}, u32[]{:S(2)}) collective-permute-start(f32[4,144,128]{2,1,0:T(8,128)S(1)} %pad_maximum_fusion.p0), channel_id=1, source_target_pairs={{0,48},{8,248},{16,32},{24,232},{32,16},{40,216},{48,0},{56,200},{... | collective-permute-start | bytes 884744 | tf_op jit(solution)/shard_map/ppermute | solution.py:641
  20.7 0.0 collective-permute-start.4
  20.7 0.4 collective-permute-start.3
  21.1 2.2 %collective-permute-start.6 = (f32[4,144,128]{2,1,0:T(8,128)S(1)}, f32[4,144,128]{2,1,0:T(8,128)S(1)}, u32[]{:S(2)}, u32[]{:S(2)}) collective-permute-start(f32[4,144,128]{2,1,0:T(8,128)S(1)} %pad_maximum_fusion.p0), channel_id=1, source_target_pairs={{0,8},{8,0},{16,24},{24,16},{32,40},{40,32},{48,56},{56,48},{64,72... | collective-permute-start | bytes 884744 | tf_op jit(solution)/shard_map/ppermute | solution.py:637
  23.3 7.4 %collective-permute-done.5.p3 = f32[4,144,128]{2,1,0:T(8,128)S(1)} collective-permute-done((f32[4,144,128]{2,1,0:T(8,128)S(1)}, f32[4,144,128]{2,1,0:T(8,128)S(1)}, u32[]{:S(2)}, u32[]{:S(2)}) %collective-permute-start.5) | collective-permute-done | bytes 294944 | tf_op jit(solution)/shard_map/ppermute | solution.py:641
  30.7 4.8 %collective-permute-start.9 = (f32[4,144,128]{2,1,0:T(8,128)S(1)}, f32[4,144,128]{2,1,0:T(8,128)S(1)}, u32[]{:S(2)}, u32[]{:S(2)}) collective-permute-start(f32[4,144,128]{2,1,0:T(8,128)S(1)} %collective-permute-done.5.p3), channel_id=1, source_target_pairs={{0,8},{8,0},{16,24},{24,16},{32,40},{40,32},{48,56},{56,48},{64,72... | collective-permute-start | bytes 884744 | tf_op jit(solution)/shard_map/ppermute | solution.py:637
  35.4 0.0 collective-permute-done.4.p2
  35.4 0.0 collective-permute-start.8
  35.4 0.0 collective-permute-done.3.p1
  35.4 0.5 collective-permute-start.7
  35.9 0.0 collective-permute-done.6.p4
  36.0 0.7 collective-permute-done.9.p7
  36.6 0.0 copy-start.6
  36.6 0.4 collective-permute-done.8.p6
  37.1 0.0 copy-start.7
  37.1 0.4 collective-permute-done.7.p5
  37.5 0.0 copy-done.6
  37.5 0.3 copy-done.7
  37.8 0.0 copy-done.5
  37.8 6.4 %forward.1 = (f32[5,1152,128]{2,1,0:T(8,128)}, f32[1152,128]{1,0:T(8,128)}, f32[8,128]{1,0:T(8,128)S(1)}) custom-call(f32[4,144,128]{2,1,0:T(8,128)S(1)} %pad_maximum_fusion.p0, f32[4,144,128]{2,1,0:T(8,128)S(1)} %collective-permute-done.3.p1, f32[4,144,128]{2,1,0:T(8,128)S(1)} %collective-permute-done.4.p2, f32[4,144,128]{2,1,0:T(8,128)S(1)} %collective-permute-done.5.p3, ...), custom_call_target="tpu_custom_call" | custom-call | flops 1000000 | bytes 1000000 | tf_op jit(solution)/shard_map/forward/pallas_call | solution.py:570
  44.2 4.0 %all-to-all-start = ((f32[8,144,128]{2,1,0:T(8,128)}), f32[8,144,128]{2,1,0:T(8,128)S(1)}, u32[]{:S(2)}, u32[]{:S(2)}) async-start(f32[8,144,128]{2,1,0:T(8,128)} %bitcast.26), calls=%async_computation | async-start | bytes 1179648 | tf_op jit(solution)/shard_map/all_to_all | solution.py:666
  48.9 0.0 copy-done.3
  48.9 0.0 copy-done.4
  48.9 5.4 %local_sums.1 = (f32[8,128]{1,0:T(8,128)S(1)}, bf16[2,96,192]{2,1,0:T(8,128)(2,1)S(1)}, bf16[2,192,96]{2,1,0:T(8,128)(2,1)S(1)}, bf16[2,192,96]{2,1,0:T(8,128)(2...) custom-call(f32[1]{0:T(128)S(6)} %copy.17.energy_ref, ...), custom_call_target="tpu_custom_call" | custom-call | flops 10000000 | bytes 10000000 | tf_op jit(solution)/shard_map/local_sums/pallas_call | solution.py:584
  54.4 0.0 copy-start.2
  54.4 3.8 %all-to-all-done = f32[8,144,128]{2,1,0:T(8,128)S(1)} async-done(((f32[8,144,128]{2,1,0:T(8,128)}), f32[8,144,128]{2,1,0:T(8,128)S(1)}, u32[]{:S(2)}, u32[]{:S(2)}) %all-to-all-start) | async-done | bytes 589856 | tf_op jit(solution)/shard_map/all_to_all | solution.py:666
  58.2 1.2 %waves.1 = (f32[896,128]{1,0:T(8,128)S(1)}, f32[8,128]{1,0:T(8,128)S(1)}) custom-call(f32[1152,128]{1,0:T(8,128)S(1)} %bitcast.16, f32[8,128]{1,0:T(8,128)S(1)} %get-tuple-element.31.stat_ref, f32[8,128]{1,0:T(8,128)S(1)} %get-tuple-element.34.sums_ref, bf16[2,96,192]{2,1,0:T(8,128)(2,1)S(1)} %get-tuple-element.35.g2, ...), custom_call_target="tpu_custom_call" | custom-call | flops 1000000 | bytes 1000000 | tf_op jit(solution)/shard_map/waves/pallas_call | solution.py:597
  59.4 11.6 %all_to_all.15 = f32[8,112,128]{2,1,0:T(8,128)S(1)} all-to-all(f32[8,112,128]{2,1,0:T(8,128)S(1)} %bitcast.23), channel_id=1, replica_groups=mesh['band'=32,'grid'=8] {'grid'}, dimensions={0} | all-to-all | bytes 917504 | tf_op jit(solution)/shard_map/all_to_all | solution.py:669
  71.0 0.0 copy-start
  71.0 0.0 copy-done.2
  71.0 0.8 steps.1
  71.9 7.8 %all-to-all-start.2 = ((f32[32,32,128]{2,1,0:T(8,128)}), f32[32,32,128]{2,1,0:T(8,128)S(1)}, u32[]{:S(2)}, u32[]{:S(2)}) async-start(f32[32,32,128]{2,1,0:T(8,128)} %get-tuple-element.47), calls=%async_computation.2 | async-start | bytes 1048576 | tf_op jit(solution)/shard_map/all_to_all | solution.py:671
  79.6 0.0 copy-done
  79.6 7.6 %image.1 = (f32[12,4,9216]{2,1,0:T(4,128)}, f32[12,4,9216]{2,1,0:T(4,128)}, f32[8,128]{1,0:T(8,128)S(1)}) custom-call(f32[1]{0:T(128)S(6)} %copy.17.energy_ref, f32[896,128]{1,0:T(8,128)} %bitcast.18, f32[8,128]{1,0:T(8,128)S(1)} %get-tuple-element.40.step_ref, f32[5,1152,128]{2,1,0:T(8,128)} %get-tuple-element.32.field_ref.field_far, ...), custom_call_target="tpu_custom_call" | custom-call | flops 20000000000 | bytes 1000000 | tf_op jit(solution)/shard_map/image/pallas_call | solution.py:612
  87.2 0.8 collective-permute-start.10
  88.0 2.3 %collective-permute-done.10 = f32[8,128]{1,0:T(8,128)S(1)} collective-permute-done((f32[8,128]{1,0:T(8,128)S(1)}, f32[8,128]{1,0:T(8,128)S(1)}, u32[]{:S(2)}, u32[]{:S(2)}) %collective-permute-start.10) | collective-permute-done | bytes 4128 | tf_op jit(solution)/shard_map/ppermute | solution.py:637
  90.4 2.4 %collective-permute-start.13 = (f32[8,128]{1,0:T(8,128)S(1)}, f32[8,128]{1,0:T(8,128)S(1)}, u32[]{:S(2)}, u32[]{:S(2)}) collective-permute-start(f32[8,128]{1,0:T(8,128)S(1)} %add.3.n0), channel_id=1, source_target_pairs={{0,6},{1,7},{2,4},{3,5},{4,2},{5,3},{6,0},{7,1},{8,14},{9,15},{10,... | collective-permute-start | bytes 12296 | tf_op jit(solution)/shard_map/ppermute | solution.py:637
  92.8 1.2 %collective-permute-start.12 = (f32[8,128]{1,0:T(8,128)S(1)}, f32[8,128]{1,0:T(8,128)S(1)}, u32[]{:S(2)}, u32[]{:S(2)}) collective-permute-start(f32[8,128]{1,0:T(8,128)S(1)} %add.3.n0), channel_id=1, source_target_pairs={{0,4},{1,5},{2,6},{3,7},{4,0},{5,1},{6,2},{7,3},{8,12},{9,13},{10,... | collective-permute-start | bytes 12296 | tf_op jit(solution)/shard_map/ppermute | solution.py:637
  94.0 0.0 collective-permute-start.11
  94.0 0.3 collective-permute-done.13.n3
  94.3 2.6 %collective-permute-done.12.n2 = f32[8,128]{1,0:T(8,128)S(1)} collective-permute-done((f32[8,128]{1,0:T(8,128)S(1)}, f32[8,128]{1,0:T(8,128)S(1)}, u32[]{:S(2)}, u32[]{:S(2)}) %collective-permute-start.12) | collective-permute-done | bytes 4128 | tf_op jit(solution)/shard_map/ppermute | solution.py:637
  96.9 0.0 collective-permute-done.11.n1
  96.9 1.2 %all-to-all-done.2.band_ref = f32[32,32,128]{2,1,0:T(8,128)S(1)} async-done(((f32[32,32,128]{2,1,0:T(8,128)}), f32[32,32,128]{2,1,0:T(8,128)S(1)}, u32[]{:S(2)}, u32[]{:S(2)}) %all-to-all-start.2) | async-done | bytes 524320 | tf_op jit(solution)/shard_map/all_to_all | solution.py:671
  98.1 3.7 %last.1 = (f32[12,4,9216]{2,1,0:T(4,128)}, f32[12,4,288]{2,1,0:T(4,128)}) custom-call(f32[8,128]{1,0:T(8,128)S(1)} %get-tuple-element.40.step_ref, f32[8,128]{1,0:T(8,128)S(1)} %add.3.n0, f32[8,128]{1,0:T(8,128)S(1)} %collective-permute-done.11.n1, f32[8,128]{1,0:T(8,128)S(1)} %collective-permute-done.12.n2, f32[8,128]{1,0:T(8,128)S(1)} %collective-permute-done.13.n3, ...), custom_call_target="tpu_custom_call" | custom-call | flops 1000000 | bytes 1000000 | tf_op jit(solution)/shard_map/last/pallas_call | solution.py:625
  (2 shorter events, 0.0 us)
Async XLA Ops:
  0.6 37.1 %copy-start.5 = (bf16[2,96,192]{2,1,0:T(8,128)(2,1)S(1)}, bf16[2,96,192]{2,1,0:T(8,128)(2,1)}, u32[]{:S(2)}) copy-start(bf16[2,96,192]{2,1,0:T(8,128)(2,1)} %constant.13.clone.g1_ref) | copy-start | bytes 221188
  2.4 10.5 %collective-permute-start.2 = (f32[1,144,128]{2,1,0:T(8,128)}, f32[1,144,128]{2,1,0:T(8,128)S(1)}, u32[]{:S(2)}, u32[]{:S(2)}) collective-permute-start(f32[1,144,128]{2,1,0:T(8,128)} %bitcast.19), channel_id=1, source_target_pairs={{0,192},{8,88},{16,208},{24,72},{32,224},{40,120},{48,240},{56,104... | collective-permute-start | bytes 221192 | tf_op jit(solution)/shard_map/ppermute | solution.py:641
  7.3 5.6 %collective-permute-start.1 = (f32[1,144,128]{2,1,0:T(8,128)}, f32[1,144,128]{2,1,0:T(8,128)S(1)}, u32[]{:S(2)}, u32[]{:S(2)}) collective-permute-start(f32[1,144,128]{2,1,0:T(8,128)} %bitcast.20), channel_id=1, source_target_pairs={{0,128},{8,24},{16,144},{24,8},{32,160},{40,56},{48,176},{56,40},{... | collective-permute-start | bytes 221192 | tf_op jit(solution)/shard_map/ppermute | solution.py:641
  7.5 5.4 %collective-permute-start = (f32[1,144,128]{2,1,0:T(8,128)}, f32[1,144,128]{2,1,0:T(8,128)S(1)}, u32[]{:S(2)}, u32[]{:S(2)}) collective-permute-start(f32[1,144,128]{2,1,0:T(8,128)} %bitcast.21), channel_id=1, source_target_pairs={{0,64},{8,72},{16,80},{24,88},{32,96},{40,104},{48,112},{56,120},{... | collective-permute-start | bytes 221192 | tf_op jit(solution)/shard_map/ppermute | solution.py:641
  9.6 0.9 copy-start.1
  12.9 36.0 %copy-start.3 = (bf16[2,192,96]{2,1,0:T(8,128)(2,1)S(1)}, bf16[2,192,96]{2,1,0:T(8,128)(2,1)}, u32[]{:S(2)}) copy-start(bf16[2,192,96]{2,1,0:T(8,128)(2,1)} %constant.15.clone.g3_ref) | copy-start | bytes 221188
  13.0 36.0 %copy-start.4 = (bf16[2,96,192]{2,1,0:T(8,128)(2,1)S(1)}, bf16[2,96,192]{2,1,0:T(8,128)(2,1)}, u32[]{:S(2)}) copy-start(bf16[2,96,192]{2,1,0:T(8,128)(2,1)} %constant.14.clone.g2_ref) | copy-start | bytes 221188
  13.0 17.7 %collective-permute-start.5 = (f32[4,144,128]{2,1,0:T(8,128)S(1)}, f32[4,144,128]{2,1,0:T(8,128)S(1)}, u32[]{:S(2)}, u32[]{:S(2)}) collective-permute-start(f32[4,144,128]{2,1,0:T(8,128)S(1)} %pad_maximum_fusion.p0), channel_id=1, source_target_pairs={{0,48},{8,248},{16,32},{24,232},{32,16},{40,216},{48,0},{56,200},{... | collective-permute-start | bytes 884744 | tf_op jit(solution)/shard_map/ppermute | solution.py:641
  20.7 14.7 %collective-permute-start.4 = (f32[4,144,128]{2,1,0:T(8,128)S(1)}, f32[4,144,128]{2,1,0:T(8,128)S(1)}, u32[]{:S(2)}, u32[]{:S(2)}) collective-permute-start(f32[4,144,128]{2,1,0:T(8,128)S(1)} %pad_maximum_fusion.p0), channel_id=1, source_target_pairs={{0,32},{8,56},{16,48},{24,40},{32,0},{40,24},{48,16},{56,8},{64,96... | collective-permute-start | bytes 884744 | tf_op jit(solution)/shard_map/ppermute | solution.py:641
  20.7 14.8 %collective-permute-start.3 = (f32[4,144,128]{2,1,0:T(8,128)S(1)}, f32[4,144,128]{2,1,0:T(8,128)S(1)}, u32[]{:S(2)}, u32[]{:S(2)}) collective-permute-start(f32[4,144,128]{2,1,0:T(8,128)S(1)} %pad_maximum_fusion.p0), channel_id=1, source_target_pairs={{0,16},{8,200},{16,0},{24,216},{32,48},{40,232},{48,32},{56,248},{... | collective-permute-start | bytes 884744 | tf_op jit(solution)/shard_map/ppermute | solution.py:641
  21.1 14.9 %collective-permute-start.6 = (f32[4,144,128]{2,1,0:T(8,128)S(1)}, f32[4,144,128]{2,1,0:T(8,128)S(1)}, u32[]{:S(2)}, u32[]{:S(2)}) collective-permute-start(f32[4,144,128]{2,1,0:T(8,128)S(1)} %pad_maximum_fusion.p0), channel_id=1, source_target_pairs={{0,8},{8,0},{16,24},{24,16},{32,40},{40,32},{48,56},{56,48},{64,72... | collective-permute-start | bytes 884744 | tf_op jit(solution)/shard_map/ppermute | solution.py:637
  30.7 6.0 %collective-permute-start.9 = (f32[4,144,128]{2,1,0:T(8,128)S(1)}, f32[4,144,128]{2,1,0:T(8,128)S(1)}, u32[]{:S(2)}, u32[]{:S(2)}) collective-permute-start(f32[4,144,128]{2,1,0:T(8,128)S(1)} %collective-permute-done.5.p3), channel_id=1, source_target_pairs={{0,8},{8,0},{16,24},{24,16},{32,40},{40,32},{48,56},{56,48},{64,72... | collective-permute-start | bytes 884744 | tf_op jit(solution)/shard_map/ppermute | solution.py:637
  35.4 1.6 %collective-permute-start.8 = (f32[4,144,128]{2,1,0:T(8,128)S(1)}, f32[4,144,128]{2,1,0:T(8,128)S(1)}, u32[]{:S(2)}, u32[]{:S(2)}) collective-permute-start(f32[4,144,128]{2,1,0:T(8,128)S(1)} %collective-permute-done.4.p2), channel_id=1, source_target_pairs={{0,8},{8,0},{16,24},{24,16},{32,40},{40,32},{48,56},{56,48},{64,72... | collective-permute-start | bytes 884744 | tf_op jit(solution)/shard_map/ppermute | solution.py:637
  35.4 2.0 %collective-permute-start.7 = (f32[4,144,128]{2,1,0:T(8,128)S(1)}, f32[4,144,128]{2,1,0:T(8,128)S(1)}, u32[]{:S(2)}, u32[]{:S(2)}) collective-permute-start(f32[4,144,128]{2,1,0:T(8,128)S(1)} %collective-permute-done.3.p1), channel_id=1, source_target_pairs={{0,8},{8,0},{16,24},{24,16},{32,40},{40,32},{48,56},{56,48},{64,72... | collective-permute-start | bytes 884744 | tf_op jit(solution)/shard_map/ppermute | solution.py:637
  36.6 0.8 copy-start.6
  37.1 0.7 copy-start.7
  44.2 14.0 %all-to-all-start = ((f32[8,144,128]{2,1,0:T(8,128)}), f32[8,144,128]{2,1,0:T(8,128)S(1)}, u32[]{:S(2)}, u32[]{:S(2)}) async-start(f32[8,144,128]{2,1,0:T(8,128)} %bitcast.26), calls=%async_computation | async-start | bytes 1179648 | tf_op jit(solution)/shard_map/all_to_all | solution.py:666
  54.4 16.7 %copy-start.2 = (f32[32,8,128]{2,1,0:T(8,128)S(1)}, f32[32,8,128]{2,1,0:T(8,128)}, u32[]{:S(2)}) copy-start(f32[32,8,128]{2,1,0:T(8,128)} %get-tuple-element.39.tail_ref) | copy-start | bytes 393220
  71.0 8.6 %copy-start = (f32[8,112,128]{2,1,0:T(8,128)}, f32[8,112,128]{2,1,0:T(8,128)S(1)}, u32[]{:S(2)}) copy-start(f32[8,112,128]{2,1,0:T(8,128)S(1)} %all_to_all.15) | copy-start | bytes 1376260
  71.9 26.3 %all-to-all-start.2 = ((f32[32,32,128]{2,1,0:T(8,128)}), f32[32,32,128]{2,1,0:T(8,128)S(1)}, u32[]{:S(2)}, u32[]{:S(2)}) async-start(f32[32,32,128]{2,1,0:T(8,128)} %get-tuple-element.47), calls=%async_computation.2 | async-start | bytes 1048576 | tf_op jit(solution)/shard_map/all_to_all | solution.py:671
  87.2 3.2 %collective-permute-start.10 = (f32[8,128]{1,0:T(8,128)S(1)}, f32[8,128]{1,0:T(8,128)S(1)}, u32[]{:S(2)}, u32[]{:S(2)}) collective-permute-start(f32[8,128]{1,0:T(8,128)S(1)} %get-tuple-element.45), channel_id=1, source_target_pairs={{0,1},{1,0},{2,3},{3,2},{4,5},{5,4},{6,7},{7,6},{8,9},{9,8},{10,11... | collective-permute-start | bytes 12296 | tf_op jit(solution)/shard_map/ppermute | solution.py:637
  90.4 4.0 %collective-permute-start.13 = (f32[8,128]{1,0:T(8,128)S(1)}, f32[8,128]{1,0:T(8,128)S(1)}, u32[]{:S(2)}, u32[]{:S(2)}) collective-permute-start(f32[8,128]{1,0:T(8,128)S(1)} %add.3.n0), channel_id=1, source_target_pairs={{0,6},{1,7},{2,4},{3,5},{4,2},{5,3},{6,0},{7,1},{8,14},{9,15},{10,... | collective-permute-start | bytes 12296 | tf_op jit(solution)/shard_map/ppermute | solution.py:637
  92.8 4.1 %collective-permute-start.12 = (f32[8,128]{1,0:T(8,128)S(1)}, f32[8,128]{1,0:T(8,128)S(1)}, u32[]{:S(2)}, u32[]{:S(2)}) collective-permute-start(f32[8,128]{1,0:T(8,128)S(1)} %add.3.n0), channel_id=1, source_target_pairs={{0,4},{1,5},{2,6},{3,7},{4,0},{5,1},{6,2},{7,3},{8,12},{9,13},{10,... | collective-permute-start | bytes 12296 | tf_op jit(solution)/shard_map/ppermute | solution.py:637
  94.0 2.9 %collective-permute-start.11 = (f32[8,128]{1,0:T(8,128)S(1)}, f32[8,128]{1,0:T(8,128)S(1)}, u32[]{:S(2)}, u32[]{:S(2)}) collective-permute-start(f32[8,128]{1,0:T(8,128)S(1)} %add.3.n0), channel_id=1, source_target_pairs={{0,2},{1,3},{2,0},{3,1},{4,6},{5,7},{6,4},{7,5},{8,10},{9,11},{10,... | collective-permute-start | bytes 12296 | tf_op jit(solution)/shard_map/ppermute | solution.py:637

commit v7 on v6

--- a/solution.py
+++ b/solution.py
@@ -474,20 +474,15 @@
         pltpu.make_async_copy(flat_r.at[i], residual_ref.at[:, :, cells], out_sems.at[1, i]).wait()
 
 
-def last_kernel(step_ref, n0, n1, n2, n3, packed_far, band_ref, response_ref, residual_ref,
-                direction_ref, density_ref, packed_ref, bands_in, first, second, result, sems, out_sems):
+def direction_kernel(step_ref, n0, n1, response_ref, residual_ref, direction_ref, first, second, result, sems, out_sems):
     parts = 6
     width = points * points // parts
-    arrival = begin(band_ref, bands_in, sems.at[2, 0])
-    kept = begin(packed_far, packed_ref, sems.at[2, 1])
     loads = []
     for i in range(parts):
         cells = pl.ds(i * width, width)
         loads.append((begin(response_ref.at[:, :, cells], first.at[i], sems.at[0, i]),
                       begin(residual_ref.at[:, :, cells], second.at[i], sems.at[1, i])))
-    new = n0[0:1, :]
-    for part in (n1, n2, n3):
-        new = new + part[0:1, :]
+    new = n0[0:1, :] + n1[0:1, :]
     ratio = [new[:, p : p + 1] / step_ref[0:1, 4 + p : 5 + p] / step_ref[0:1, 8 + p : 9 + p] for p in range(trials)]
     r = row_of((trials, 128))
     ratios = jnp.zeros((trials, 128), f32)
@@ -500,11 +495,18 @@
             copy.wait()
         result[i, :, :, :] = second[i] + ratios * first[i]
         stores.append(begin(result.at[i], direction_ref.at[:, :, pl.ds(i * width, width)], out_sems.at[i]))
-    arrival.wait()
+    for copy in stores:
+        copy.wait()
+
+
+def density_kernel(packed_far, band_ref, density_ref, packed_ref, bands_in, sems):
+    arrival = begin(band_ref, bands_in, sems.at[0])
+    kept = begin(packed_far, packed_ref, sems.at[1])
     kept.wait()
     blocks = [packed_ref[q * 36 : q * 36 + 36, :] for q in range(3)]
     fields = [tighten(field) for field in (*blocks, unpack_last(*blocks))]
     sums = [jnp.zeros((27, 128), f32) for _ in range(trials)]
+    arrival.wait()
     for v in range(bands):
         square = bands_in[v, 0:27, :]
         square = square * square
@@ -519,8 +521,6 @@
         density_ref[:, p, 0:128] = jnp.where(lane < 96, c[0], r1)
         density_ref[:, p, 128:256] = jnp.where(lane < 64, r1, r2)
         density_ref[:, p, 256:288] = r2[:, 0:32]
-    for copy in stores:
-        copy.wait()
 
 
 vmem = pl.BlockSpec(memory_space=pltpu.VMEM)
@@ -619,14 +619,20 @@
     )(energies, arrived, step, fields, o, g4, w2)
 
 
-def last(step, norms, packed, band, response, residual):
-    cells = shape(planes, trials, points * points)
+def direct(step, norms, response, residual):
     part = buffer(6, planes, trials, points * points // 6)
     return call(
-        last_kernel, [vmem] * 5 + [far, hbm, far, far], (cells, shape(planes, trials, 288)),
-        [buffer(144, 128), buffer(bands, 32, 128), part, part, part, pltpu.SemaphoreType.DMA((3, 6)), pltpu.SemaphoreType.DMA((6,))],
-        name="last", room=SOME, places=(far, vmem),
-    )(step, *norms, packed, band, response, residual)
+        direction_kernel, [vmem] * 3 + [far] * 2, shape(planes, trials, points * points),
+        [part, part, part, pltpu.SemaphoreType.DMA((2, 6)), pltpu.SemaphoreType.DMA((6,))],
+        name="direction", room=BIG, places=far, flops=10**7,
+    )(step, *norms, response, residual)
+
+
+def density_of(packed, band):
+    return call(
+        density_kernel, [far, hbm], shape(planes, trials, 288),
+        [buffer(144, 128), buffer(bands, 32, 128), pltpu.SemaphoreType.DMA((2,))], name="density",
+    )(packed, band)
 
 
 def outward(value):
@@ -670,9 +676,10 @@
     step, payload = steps(back, scal, tail, base)
     band = lax.all_to_all(payload, "band", 0, 0, tiled=True)
     response, residual, norm = image(energies, back, step, fields, o_far, g4, w2)
-    norm = norm + swapped(norm, "grid", groups, 1)
-    norms = [norm] + [swapped(norm, "grid", groups, m) for m in (2, 4, 6)]
-    direction, density = last(step, norms, packed_far, band, response, residual)
+    norm = norm + swapped(norm, "grid", groups, 2) + swapped(norm, "grid", groups, 4) + swapped(norm, "grid", groups, 6)
+    norms = [norm, swapped(norm, "grid", groups, 1)]
+    direction = direct(step, norms, response, residual)
+    density = density_of(packed_far, band)
     return outward(response)[None], outward(residual)[None], outward(direction)[None], outward(density)
 
 

time: 103 us -> 101 us (0.981)
  waiting for transfers between devices: 19.2 us -> 16.4 us
    ppermute x8, waiting for transfers between devices: 6.76 us -> 5.1 us  [swapped(): return lax.ppermute(value, axis, [(s, s ^ mask) for s in range(size)])]
    all_to_all x1, waiting for transfers between devices: 1.2 us -> 0.09 us  [on_device(): band = lax.all_to_all(payload, 'band', 0, 0, tiled=True)]
    pallas_call x1 -> x2, Pallas kernels: 3.72 us -> 4.46 us  [the longest x1 2.91 us: direct(): call(direction_kernel, [vmem] * 3 + [far] * 2, shape(planes, trials, poin...]
  transfers between devices with their start and end apart: 16 -> 16, of which waited for: 9 -> 9; matrix products, arithmetic and copies ran while one was open for 2% -> 2% of each run, Pallas kernels for 15% -> 18%
where the time goes in v7:
time: 101 us; the launch traced here: 99.8 us
  starting transfers between devices  37 us (37%)
  Pallas kernels  30.1 us (30%)
  waiting for transfers between devices  16.4 us (16%)
  blocking collectives  11.6 us (11%)
  local copies, waits for them, and re-layouts  3.13 us (3%)
  between operations  1.62 us (2%)
    ppermute x6, starting transfers between devices, crossed(): lax.ppermute(value, 'band', [(s, s ^ (odd if s & 1 else even)) for s in r...  13.4 us
    ppermute x8, starting transfers between devices, swapped(): return lax.ppermute(value, axis, [(s, s ^ mask) for s in range(size)])  11.8 us
    all_to_all x1, blocking collectives, on_device(): lax.all_to_all(back.reshape(groups, returned, 128), 'grid', 0, 0, tiled=T...  11.6 us
    all_to_all x1, starting transfers between devices, on_device(): band = lax.all_to_all(payload, 'band', 0, 0, tiled=True)  7.78 us
    pallas_call x1, Pallas kernels, image(): call(image_kernel, [smem, vmem, vmem, far, far, vmem, vmem], (cells, cell...  7.6 us
    ppermute x6, waiting for transfers between devices, crossed(): lax.ppermute(value, 'band', [(s, s ^ (odd if s & 1 else even)) for s in r...  7.36 us
    pallas_call x1, Pallas kernels, forward(): call(forward_kernel, [hbm] * 8 + [far] * 3, (shape(5, rows, 128), shape(r...  6.46 us
    pallas_call x1, Pallas kernels, local_sums(): pl.pallas_call(local_kernel, grid=(count,), in_specs=[smem, pl.BlockSpec(...  5.42 us
  transfers between devices with their start and end apart: 16, of which 9 were waited for; matrix products, arithmetic and copies ran while one was open for 2% of the time, Pallas kernels for 18%

profile of v7, /device:TPU:1, one launch (start us, length us, event | category | flops | bytes accessed | tf_op | source)
XLA Modules:
  0.0 99.8 jit_solution(3782265247678005172)
XLA Ops:
  0.6 0.0 copy-start.5
  0.6 1.7 %pack.1.packed_ref = f32[144,128]{1,0:T(8,128)} custom-call(f32[12,4,288]{2,1,0:T(4,128)} %bitcast.28, f32[12,288]{1,0:T(8,128)} %local_far.1), custom_call_target="tpu_custom_call" | custom-call | flops 1000000 | bytes 1000000 | tf_op jit(solution)/shard_map/pack/pallas_call | solution.py:550
  2.4 4.9 %collective-permute-start.2 = (f32[1,144,128]{2,1,0:T(8,128)}, f32[1,144,128]{2,1,0:T(8,128)S(1)}, u32[]{:S(2)}, u32[]{:S(2)}) collective-permute-start(f32[1,144,128]{2,1,0:T(8,128)} %bitcast.19), channel_id=1, source_target_pairs={{0,192},{8,88},{16,208},{24,72},{32,224},{40,120},{48,240},{56,104... | collective-permute-start | bytes 221192 | tf_op jit(solution)/shard_map/ppermute | solution.py:647
  7.3 0.2 collective-permute-start.1
  7.5 0.2 collective-permute-start
  7.7 1.9 %copy.15.o_ref = f32[1,12,9216]{2,1,0:T(8,128)} copy(f32[1,12,9216]{2,0,1:T(1,128)} %param.10) | data formatting | bytes 884736 | tf_op args[0]
  9.6 0.0 copy-start.1
  9.6 0.9 copy-done.1
  10.5 2.4 %orbital_rows.1 = (f32[1152,128]{1,0:T(8,128)}, f32[32,32,128]{2,1,0:T(8,128)}, f32[144,128]{1,0:T(8,128)S(1)}) custom-call(f32[1,12,9216]{2,1,0:T(8,128)} %copy.15.o_ref, f32[144,128]{1,0:T(8,128)S(1)} %copy-done.1), custom_call_target="tpu_custom_call" | custom-call | flops 1000000 | bytes 1000000 | tf_op jit(solution)/shard_map/orbital_rows/pallas_call | solution.py:557
  12.9 0.0 collective-permute-done.2
  12.9 0.0 collective-permute-done.1
  12.9 0.0 collective-permute-done
  12.9 0.0 copy-start.3
  12.9 0.0 copy-start.4
  13.0 7.7 %collective-permute-start.5 = (f32[4,144,128]{2,1,0:T(8,128)S(1)}, f32[4,144,128]{2,1,0:T(8,128)S(1)}, u32[]{:S(2)}, u32[]{:S(2)}) collective-permute-start(f32[4,144,128]{2,1,0:T(8,128)S(1)} %pad_maximum_fusion.p0), channel_id=1, source_target_pairs={{0,48},{8,248},{16,32},{24,232},{32,16},{40,216},{48,0},{56,200},{... | collective-permute-start | bytes 884744 | tf_op jit(solution)/shard_map/ppermute | solution.py:647
  20.7 0.0 collective-permute-start.4
  20.7 0.4 collective-permute-start.3
  21.1 2.3 %collective-permute-start.6 = (f32[4,144,128]{2,1,0:T(8,128)S(1)}, f32[4,144,128]{2,1,0:T(8,128)S(1)}, u32[]{:S(2)}, u32[]{:S(2)}) collective-permute-start(f32[4,144,128]{2,1,0:T(8,128)S(1)} %pad_maximum_fusion.p0), channel_id=1, source_target_pairs={{0,8},{8,0},{16,24},{24,16},{32,40},{40,32},{48,56},{56,48},{64,72... | collective-permute-start | bytes 884744 | tf_op jit(solution)/shard_map/ppermute | solution.py:643
  23.3 7.4 %collective-permute-done.5.p3 = f32[4,144,128]{2,1,0:T(8,128)S(1)} collective-permute-done((f32[4,144,128]{2,1,0:T(8,128)S(1)}, f32[4,144,128]{2,1,0:T(8,128)S(1)}, u32[]{:S(2)}, u32[]{:S(2)}) %collective-permute-start.5) | collective-permute-done | bytes 294944 | tf_op jit(solution)/shard_map/ppermute | solution.py:647
  30.7 4.8 %collective-permute-start.9 = (f32[4,144,128]{2,1,0:T(8,128)S(1)}, f32[4,144,128]{2,1,0:T(8,128)S(1)}, u32[]{:S(2)}, u32[]{:S(2)}) collective-permute-start(f32[4,144,128]{2,1,0:T(8,128)S(1)} %collective-permute-done.5.p3), channel_id=1, source_target_pairs={{0,8},{8,0},{16,24},{24,16},{32,40},{40,32},{48,56},{56,48},{64,72... | collective-permute-start | bytes 884744 | tf_op jit(solution)/shard_map/ppermute | solution.py:643
  35.4 0.0 collective-permute-done.4.p2
  35.4 0.0 collective-permute-start.8
  35.4 0.0 collective-permute-done.3.p1
  35.4 0.5 collective-permute-start.7
  35.9 0.0 collective-permute-done.6.p4
  35.9 0.7 collective-permute-done.9.p7
  36.6 0.0 copy-start.6
  36.6 0.4 collective-permute-done.8.p6
  37.1 0.0 copy-start.7
  37.1 0.4 collective-permute-done.7.p5
  37.5 0.0 copy-done.6
  37.5 0.3 copy-done.7
  37.8 0.0 copy-done.5
  37.8 6.5 %forward.1 = (f32[5,1152,128]{2,1,0:T(8,128)}, f32[1152,128]{1,0:T(8,128)}, f32[8,128]{1,0:T(8,128)S(1)}) custom-call(f32[4,144,128]{2,1,0:T(8,128)S(1)} %pad_maximum_fusion.p0, f32[4,144,128]{2,1,0:T(8,128)S(1)} %collective-permute-done.3.p1, f32[4,144,128]{2,1,0:T(8,128)S(1)} %collective-permute-done.4.p2, f32[4,144,128]{2,1,0:T(8,128)S(1)} %collective-permute-done.5.p3, ...), custom_call_target="tpu_custom_call" | custom-call | flops 1000000 | bytes 1000000 | tf_op jit(solution)/shard_map/forward/pallas_call | solution.py:570
  44.2 4.0 %all-to-all-start = ((f32[8,144,128]{2,1,0:T(8,128)}), f32[8,144,128]{2,1,0:T(8,128)S(1)}, u32[]{:S(2)}, u32[]{:S(2)}) async-start(f32[8,144,128]{2,1,0:T(8,128)} %bitcast.27), calls=%async_computation | async-start | bytes 1179648 | tf_op jit(solution)/shard_map/all_to_all | solution.py:672
  48.9 0.0 copy-done.3
  48.9 0.0 copy-done.4
  48.9 5.4 %local_sums.1 = (f32[8,128]{1,0:T(8,128)S(1)}, bf16[2,96,192]{2,1,0:T(8,128)(2,1)S(1)}, bf16[2,192,96]{2,1,0:T(8,128)(2,1)S(1)}, bf16[2,192,96]{2,1,0:T(8,128)(2...) custom-call(f32[1]{0:T(128)S(6)} %copy.17.energy_ref, ...), custom_call_target="tpu_custom_call" | custom-call | flops 10000000 | bytes 10000000 | tf_op jit(solution)/shard_map/local_sums/pallas_call | solution.py:584
  54.4 0.0 copy-start.2
  54.4 3.8 %all-to-all-done = f32[8,144,128]{2,1,0:T(8,128)S(1)} async-done(((f32[8,144,128]{2,1,0:T(8,128)}), f32[8,144,128]{2,1,0:T(8,128)S(1)}, u32[]{:S(2)}, u32[]{:S(2)}) %all-to-all-start) | async-done | bytes 589856 | tf_op jit(solution)/shard_map/all_to_all | solution.py:672
  58.2 1.2 %waves.1 = (f32[896,128]{1,0:T(8,128)S(1)}, f32[8,128]{1,0:T(8,128)S(1)}) custom-call(f32[1152,128]{1,0:T(8,128)S(1)} %bitcast.16, f32[8,128]{1,0:T(8,128)S(1)} %get-tuple-element.29.stat_ref, f32[8,128]{1,0:T(8,128)S(1)} %get-tuple-element.32.sums_ref, bf16[2,96,192]{2,1,0:T(8,128)(2,1)S(1)} %get-tuple-element.33.g2, ...), custom_call_target="tpu_custom_call" | custom-call | flops 1000000 | bytes 1000000 | tf_op jit(solution)/shard_map/waves/pallas_call | solution.py:597
  59.4 11.6 %all_to_all.15 = f32[8,112,128]{2,1,0:T(8,128)S(1)} all-to-all(f32[8,112,128]{2,1,0:T(8,128)S(1)} %bitcast.23), channel_id=1, replica_groups=mesh['band'=32,'grid'=8] {'grid'}, dimensions={0} | all-to-all | bytes 917504 | tf_op jit(solution)/shard_map/all_to_all | solution.py:675
  71.0 0.0 copy-start
  71.0 0.0 copy-done.2
  71.0 0.8 steps.1
  71.9 7.8 %all-to-all-start.2 = ((f32[32,32,128]{2,1,0:T(8,128)}), f32[32,32,128]{2,1,0:T(8,128)S(1)}, u32[]{:S(2)}, u32[]{:S(2)}) async-start(f32[32,32,128]{2,1,0:T(8,128)} %get-tuple-element.45), calls=%async_computation.2 | async-start | bytes 1048576 | tf_op jit(solution)/shard_map/all_to_all | solution.py:677
  79.7 0.0 copy-done
  79.7 7.6 %image.1 = (f32[12,4,9216]{2,1,0:T(4,128)}, f32[12,4,9216]{2,1,0:T(4,128)}, f32[8,128]{1,0:T(8,128)S(1)}) custom-call(f32[1]{0:T(128)S(6)} %copy.17.energy_ref, f32[896,128]{1,0:T(8,128)} %bitcast.18, f32[8,128]{1,0:T(8,128)S(1)} %get-tuple-element.38.step_ref, f32[5,1152,128]{2,1,0:T(8,128)} %get-tuple-element.30.field_ref.field_far, ...), custom_call_target="tpu_custom_call" | custom-call | flops 20000000000 | bytes 1000000 | tf_op jit(solution)/shard_map/image/pallas_call | solution.py:612
  87.3 0.7 collective-permute-start.12
  88.0 1.2 %collective-permute-start.11 = (f32[8,128]{1,0:T(8,128)S(1)}, f32[8,128]{1,0:T(8,128)S(1)}, u32[]{:S(2)}, u32[]{:S(2)}) collective-permute-start(f32[8,128]{1,0:T(8,128)S(1)} %get-tuple-element.43), channel_id=1, source_target_pairs={{0,4},{1,5},{2,6},{3,7},{4,0},{5,1},{6,2},{7,3},{8,12},{9,13},{10,... | collective-permute-start | bytes 12296 | tf_op jit(solution)/shard_map/ppermute | solution.py:643
  89.2 1.4 %collective-permute-start.10 = (f32[8,128]{1,0:T(8,128)S(1)}, f32[8,128]{1,0:T(8,128)S(1)}, u32[]{:S(2)}, u32[]{:S(2)}) collective-permute-start(f32[8,128]{1,0:T(8,128)S(1)} %get-tuple-element.43), channel_id=1, source_target_pairs={{0,2},{1,3},{2,0},{3,1},{4,6},{5,7},{6,4},{7,5},{8,10},{9,11},{10,... | collective-permute-start | bytes 12296 | tf_op jit(solution)/shard_map/ppermute | solution.py:643
  90.6 0.7 collective-permute-done.12
  91.3 0.9 collective-permute-done.11
  92.2 0.0 collective-permute-done.10
  92.3 0.9 collective-permute-start.13
  93.1 1.9 %collective-permute-done.13.n1 = f32[8,128]{1,0:T(8,128)S(1)} collective-permute-done((f32[8,128]{1,0:T(8,128)S(1)}, f32[8,128]{1,0:T(8,128)S(1)}, u32[]{:S(2)}, u32[]{:S(2)}) %collective-permute-start.13) | collective-permute-done | bytes 4128 | tf_op jit(solution)/shard_map/ppermute | solution.py:643
  95.1 2.9 %direction.1 = f32[12,4,9216]{2,1,0:T(4,128)} custom-call(f32[8,128]{1,0:T(8,128)S(1)} %get-tuple-element.38.step_ref, f32[8,128]{1,0:T(8,128)S(1)} %add_add_fusion.n0, f32[8,128]{1,0:T(8,128)S(1)} %collective-permute-done.13.n1, f32[12,4,9216]{2,1,0:T(4,128)} %get-tuple-element.41.response_ref, f32[12,4,9216]{2,1,0:T(4,128)} %get-tuple-element.42.residual_ref), custom_call_target="tpu_custom_call" | custom-call | flops 10000000 | bytes 1000000 | tf_op jit(solution)/shard_map/direction/pallas_call | solution.py:624
  98.0 0.1 all-to-all-done.2.band_ref
  98.1 1.5 %density.1 = f32[12,4,288]{2,1,0:T(4,128)} custom-call(f32[144,128]{1,0:T(8,128)S(1)} %get-tuple-element.44.packed_far, f32[32,32,128]{2,1,0:T(8,128)S(1)} %all-to-all-done.2.band_ref), custom_call_target="tpu_custom_call" | custom-call | flops 1000000 | bytes 1000000 | tf_op jit(solution)/shard_map/density/pallas_call | solution.py:632
  (2 shorter events, 0.0 us)
Async XLA Ops:
  0.6 37.1 %copy-start.5 = (bf16[2,96,192]{2,1,0:T(8,128)(2,1)S(1)}, bf16[2,96,192]{2,1,0:T(8,128)(2,1)}, u32[]{:S(2)}) copy-start(bf16[2,96,192]{2,1,0:T(8,128)(2,1)} %constant.13.clone.g1_ref) | copy-start | bytes 221188
  2.4 10.5 %collective-permute-start.2 = (f32[1,144,128]{2,1,0:T(8,128)}, f32[1,144,128]{2,1,0:T(8,128)S(1)}, u32[]{:S(2)}, u32[]{:S(2)}) collective-permute-start(f32[1,144,128]{2,1,0:T(8,128)} %bitcast.19), channel_id=1, source_target_pairs={{0,192},{8,88},{16,208},{24,72},{32,224},{40,120},{48,240},{56,104... | collective-permute-start | bytes 221192 | tf_op jit(solution)/shard_map/ppermute | solution.py:647
  7.3 5.6 %collective-permute-start.1 = (f32[1,144,128]{2,1,0:T(8,128)}, f32[1,144,128]{2,1,0:T(8,128)S(1)}, u32[]{:S(2)}, u32[]{:S(2)}) collective-permute-start(f32[1,144,128]{2,1,0:T(8,128)} %bitcast.20), channel_id=1, source_target_pairs={{0,128},{8,24},{16,144},{24,8},{32,160},{40,56},{48,176},{56,40},{... | collective-permute-start | bytes 221192 | tf_op jit(solution)/shard_map/ppermute | solution.py:647
  7.5 5.4 %collective-permute-start = (f32[1,144,128]{2,1,0:T(8,128)}, f32[1,144,128]{2,1,0:T(8,128)S(1)}, u32[]{:S(2)}, u32[]{:S(2)}) collective-permute-start(f32[1,144,128]{2,1,0:T(8,128)} %bitcast.21), channel_id=1, source_target_pairs={{0,64},{8,72},{16,80},{24,88},{32,96},{40,104},{48,112},{56,120},{... | collective-permute-start | bytes 221192 | tf_op jit(solution)/shard_map/ppermute | solution.py:647
  9.6 0.9 copy-start.1
  12.9 36.0 %copy-start.3 = (bf16[2,192,96]{2,1,0:T(8,128)(2,1)S(1)}, bf16[2,192,96]{2,1,0:T(8,128)(2,1)}, u32[]{:S(2)}) copy-start(bf16[2,192,96]{2,1,0:T(8,128)(2,1)} %constant.15.clone.g3_ref) | copy-start | bytes 221188
  12.9 36.0 %copy-start.4 = (bf16[2,96,192]{2,1,0:T(8,128)(2,1)S(1)}, bf16[2,96,192]{2,1,0:T(8,128)(2,1)}, u32[]{:S(2)}) copy-start(bf16[2,96,192]{2,1,0:T(8,128)(2,1)} %constant.14.clone.g2_ref) | copy-start | bytes 221188
  13.0 17.7 %collective-permute-start.5 = (f32[4,144,128]{2,1,0:T(8,128)S(1)}, f32[4,144,128]{2,1,0:T(8,128)S(1)}, u32[]{:S(2)}, u32[]{:S(2)}) collective-permute-start(f32[4,144,128]{2,1,0:T(8,128)S(1)} %pad_maximum_fusion.p0), channel_id=1, source_target_pairs={{0,48},{8,248},{16,32},{24,232},{32,16},{40,216},{48,0},{56,200},{... | collective-permute-start | bytes 884744 | tf_op jit(solution)/shard_map/ppermute | solution.py:647
  20.7 14.7 %collective-permute-start.4 = (f32[4,144,128]{2,1,0:T(8,128)S(1)}, f32[4,144,128]{2,1,0:T(8,128)S(1)}, u32[]{:S(2)}, u32[]{:S(2)}) collective-permute-start(f32[4,144,128]{2,1,0:T(8,128)S(1)} %pad_maximum_fusion.p0), channel_id=1, source_target_pairs={{0,32},{8,56},{16,48},{24,40},{32,0},{40,24},{48,16},{56,8},{64,96... | collective-permute-start | bytes 884744 | tf_op jit(solution)/shard_map/ppermute | solution.py:647
  20.7 14.8 %collective-permute-start.3 = (f32[4,144,128]{2,1,0:T(8,128)S(1)}, f32[4,144,128]{2,1,0:T(8,128)S(1)}, u32[]{:S(2)}, u32[]{:S(2)}) collective-permute-start(f32[4,144,128]{2,1,0:T(8,128)S(1)} %pad_maximum_fusion.p0), channel_id=1, source_target_pairs={{0,16},{8,200},{16,0},{24,216},{32,48},{40,232},{48,32},{56,248},{... | collective-permute-start | bytes 884744 | tf_op jit(solution)/shard_map/ppermute | solution.py:647
  21.1 14.9 %collective-permute-start.6 = (f32[4,144,128]{2,1,0:T(8,128)S(1)}, f32[4,144,128]{2,1,0:T(8,128)S(1)}, u32[]{:S(2)}, u32[]{:S(2)}) collective-permute-start(f32[4,144,128]{2,1,0:T(8,128)S(1)} %pad_maximum_fusion.p0), channel_id=1, source_target_pairs={{0,8},{8,0},{16,24},{24,16},{32,40},{40,32},{48,56},{56,48},{64,72... | collective-permute-start | bytes 884744 | tf_op jit(solution)/shard_map/ppermute | solution.py:643
  30.7 6.0 %collective-permute-start.9 = (f32[4,144,128]{2,1,0:T(8,128)S(1)}, f32[4,144,128]{2,1,0:T(8,128)S(1)}, u32[]{:S(2)}, u32[]{:S(2)}) collective-permute-start(f32[4,144,128]{2,1,0:T(8,128)S(1)} %collective-permute-done.5.p3), channel_id=1, source_target_pairs={{0,8},{8,0},{16,24},{24,16},{32,40},{40,32},{48,56},{56,48},{64,72... | collective-permute-start | bytes 884744 | tf_op jit(solution)/shard_map/ppermute | solution.py:643
  35.4 1.6 %collective-permute-start.8 = (f32[4,144,128]{2,1,0:T(8,128)S(1)}, f32[4,144,128]{2,1,0:T(8,128)S(1)}, u32[]{:S(2)}, u32[]{:S(2)}) collective-permute-start(f32[4,144,128]{2,1,0:T(8,128)S(1)} %collective-permute-done.4.p2), channel_id=1, source_target_pairs={{0,8},{8,0},{16,24},{24,16},{32,40},{40,32},{48,56},{56,48},{64,72... | collective-permute-start | bytes 884744 | tf_op jit(solution)/shard_map/ppermute | solution.py:643
  35.4 2.0 %collective-permute-start.7 = (f32[4,144,128]{2,1,0:T(8,128)S(1)}, f32[4,144,128]{2,1,0:T(8,128)S(1)}, u32[]{:S(2)}, u32[]{:S(2)}) collective-permute-start(f32[4,144,128]{2,1,0:T(8,128)S(1)} %collective-permute-done.3.p1), channel_id=1, source_target_pairs={{0,8},{8,0},{16,24},{24,16},{32,40},{40,32},{48,56},{56,48},{64,72... | collective-permute-start | bytes 884744 | tf_op jit(solution)/shard_map/ppermute | solution.py:643
  36.6 0.8 copy-start.6
  37.1 0.7 copy-start.7
  44.2 13.9 %all-to-all-start = ((f32[8,144,128]{2,1,0:T(8,128)}), f32[8,144,128]{2,1,0:T(8,128)S(1)}, u32[]{:S(2)}, u32[]{:S(2)}) async-start(f32[8,144,128]{2,1,0:T(8,128)} %bitcast.27), calls=%async_computation | async-start | bytes 1179648 | tf_op jit(solution)/shard_map/all_to_all | solution.py:672
  54.4 16.7 %copy-start.2 = (f32[32,8,128]{2,1,0:T(8,128)S(1)}, f32[32,8,128]{2,1,0:T(8,128)}, u32[]{:S(2)}) copy-start(f32[32,8,128]{2,1,0:T(8,128)} %get-tuple-element.37.tail_ref) | copy-start | bytes 393220
  71.0 8.6 %copy-start = (f32[8,112,128]{2,1,0:T(8,128)}, f32[8,112,128]{2,1,0:T(8,128)S(1)}, u32[]{:S(2)}) copy-start(f32[8,112,128]{2,1,0:T(8,128)S(1)} %all_to_all.15) | copy-start | bytes 1376260
  71.9 26.2 %all-to-all-start.2 = ((f32[32,32,128]{2,1,0:T(8,128)}), f32[32,32,128]{2,1,0:T(8,128)S(1)}, u32[]{:S(2)}, u32[]{:S(2)}) async-start(f32[32,32,128]{2,1,0:T(8,128)} %get-tuple-element.45), calls=%async_computation.2 | async-start | bytes 1048576 | tf_op jit(solution)/shard_map/all_to_all | solution.py:677
  87.3 4.0 %collective-permute-start.12 = (f32[8,128]{1,0:T(8,128)S(1)}, f32[8,128]{1,0:T(8,128)S(1)}, u32[]{:S(2)}, u32[]{:S(2)}) collective-permute-start(f32[8,128]{1,0:T(8,128)S(1)} %get-tuple-element.43), channel_id=1, source_target_pairs={{0,6},{1,7},{2,4},{3,5},{4,2},{5,3},{6,0},{7,1},{8,14},{9,15},{10,... | collective-permute-start | bytes 12296 | tf_op jit(solution)/shard_map/ppermute | solution.py:643
  88.0 4.3 %collective-permute-start.11 = (f32[8,128]{1,0:T(8,128)S(1)}, f32[8,128]{1,0:T(8,128)S(1)}, u32[]{:S(2)}, u32[]{:S(2)}) collective-permute-start(f32[8,128]{1,0:T(8,128)S(1)} %get-tuple-element.43), channel_id=1, source_target_pairs={{0,4},{1,5},{2,6},{3,7},{4,0},{5,1},{6,2},{7,3},{8,12},{9,13},{10,... | collective-permute-start | bytes 12296 | tf_op jit(solution)/shard_map/ppermute | solution.py:643
  89.2 3.1 %collective-permute-start.10 = (f32[8,128]{1,0:T(8,128)S(1)}, f32[8,128]{1,0:T(8,128)S(1)}, u32[]{:S(2)}, u32[]{:S(2)}) collective-permute-start(f32[8,128]{1,0:T(8,128)S(1)} %get-tuple-element.43), channel_id=1, source_target_pairs={{0,2},{1,3},{2,0},{3,1},{4,6},{5,7},{6,4},{7,5},{8,10},{9,11},{10,... | collective-permute-start | bytes 12296 | tf_op jit(solution)/shard_map/ppermute | solution.py:643
  92.3 2.8 %collective-permute-start.13 = (f32[8,128]{1,0:T(8,128)S(1)}, f32[8,128]{1,0:T(8,128)S(1)}, u32[]{:S(2)}, u32[]{:S(2)}) collective-permute-start(f32[8,128]{1,0:T(8,128)S(1)} %add_add_fusion.n0), channel_id=1, source_target_pairs={{0,1},{1,0},{2,3},{3,2},{4,5},{5,4},{6,7},{7,6},{8,9},{9,8},{10,11... | collective-permute-start | bytes 12296 | tf_op jit(solution)/shard_map/ppermute | solution.py:643

commit v8 on v7

--- a/solution.py
+++ b/solution.py
@@ -243,7 +243,7 @@
 
     for copy in tables:
         copy.wait()
-    big = 384
+    big = 576
 
     def along_z(i, _):
         at = pl.ds(pl.multiple_of(i * big, big), big)
@@ -421,7 +421,7 @@
         for i in range(2):
             real[pl.ds(x + i, points, stride=planes), :] = v[:points, i * 128 : i * 128 + 128]
             imag[pl.ds(x + i, points, stride=planes), :] = v[points:, i * 128 : i * 128 + 128]
-    size = 96
+    size = 384
     mixed = planes * trials
     lane = lane_of((mixed, 128))
 
@@ -454,10 +454,10 @@
             mixed_r[there, :] = residual
             out.append(sums[p] + fold(residual * residual))
         for flat, ref in ((flat_s, mixed_s), (flat_r, mixed_r)):
-            for q in range(2):
+            for q in range(size // 48):
                 for n, tile in enumerate(tiles(ref, q)):
                     flat[i, :, :, 384 * q + 128 * n : 384 * q + 128 * n + 128] = tile.reshape(planes, trials, 128)
-        cells = pl.ds(pl.multiple_of(i * 768, 768), 768)
+        cells = pl.ds(pl.multiple_of(i * 3072, 3072), 3072)
         begin(flat_s.at[i], response_ref.at[:, :, cells], out_sems.at[0, i])
         begin(flat_r.at[i], residual_ref.at[:, :, cells], out_sems.at[1, i])
         return tuple(out)
@@ -469,7 +469,7 @@
         sums = lax.fori_loop(n * (third // size), (n + 1) * (third // size), back, sums)
     norm_ref[...] = tile_of((8, 128), [(0, p, total(s)) for p, s in enumerate(sums)])
     for i in range(rows // size):
-        cells = pl.ds(i * 768, 768)
+        cells = pl.ds(i * 3072, 3072)
         pltpu.make_async_copy(flat_s.at[i], response_ref.at[:, :, cells], out_sems.at[0, i]).wait()
         pltpu.make_async_copy(flat_r.at[i], residual_ref.at[:, :, cells], out_sems.at[1, i]).wait()
 
@@ -612,9 +612,9 @@
     return call(
         image_kernel, [smem, vmem, vmem, far, far, vmem, vmem], (cells, cells, shape(8, 128)),
         [buffer(5, rows, 128), buffer(rows, 128), buffer(rows, 128), buffer(rows, 128), buffer(rows, 512),
-         buffer(384, 128), buffer(384, 128),
-         buffer(12, planes, trials, 768), buffer(12, planes, trials, 768),
-         pltpu.SemaphoreType.DMA((6,)), pltpu.SemaphoreType.DMA((2, 12))],
+         buffer(1536, 128), buffer(1536, 128),
+         buffer(3, planes, trials, 3072), buffer(3, planes, trials, 3072),
+         pltpu.SemaphoreType.DMA((6,)), pltpu.SemaphoreType.DMA((2, 6))],
         name="image", room=BIG, places=(far, far, vmem), flops=2 * 10**10,
     )(energies, arrived, step, fields, o, g4, w2)
 

time: 101 us -> 100 us (0.990)
  Pallas kernels: 30.1 us -> 28.3 us
  waiting for transfers between devices: 16.4 us -> 18 us
    pallas_call x1, Pallas kernels: 7.6 us -> 5.93 us  [image(): call(image_kernel, [smem, vmem, vmem, far, far, vmem, vmem], (cells, cell...]
    all_to_all x1, waiting for transfers between devices: 0.09 us -> 1.52 us  [on_device(): band = lax.all_to_all(payload, 'band', 0, 0, tiled=True)]
  transfers between devices with their start and end apart: 16 -> 16, of which waited for: 9 -> 9; matrix products, arithmetic and copies ran while one was open for 2% -> 2% of each run, Pallas kernels for 18% -> 17%
where the time goes in v8:
time: 100 us; the launch traced here: 99.6 us
  starting transfers between devices  37 us (37%)
  Pallas kernels  28.3 us (28%)
  waiting for transfers between devices  18 us (18%)
  blocking collectives  11.6 us (12%)
  local copies, waits for them, and re-layouts  3.13 us (3%)
  between operations  1.62 us (2%)
    ppermute x6, starting transfers between devices, crossed(): lax.ppermute(value, 'band', [(s, s ^ (odd if s & 1 else even)) for s in r...  13.4 us
    ppermute x8, starting transfers between devices, swapped(): return lax.ppermute(value, axis, [(s, s ^ mask) for s in range(size)])  11.8 us
    all_to_all x1, blocking collectives, on_device(): lax.all_to_all(back.reshape(groups, returned, 128), 'grid', 0, 0, tiled=T...  11.6 us
    all_to_all x1, starting transfers between devices, on_device(): band = lax.all_to_all(payload, 'band', 0, 0, tiled=True)  7.78 us
    ppermute x6, waiting for transfers between devices, crossed(): lax.ppermute(value, 'band', [(s, s ^ (odd if s & 1 else even)) for s in r...  7.36 us
    pallas_call x1, Pallas kernels, forward(): call(forward_kernel, [hbm] * 8 + [far] * 3, (shape(5, rows, 128), shape(r...  6.31 us
    pallas_call x1, Pallas kernels, image(): call(image_kernel, [smem, vmem, vmem, far, far, vmem, vmem], (cells, cell...  5.93 us
    pallas_call x1, Pallas kernels, local_sums(): pl.pallas_call(local_kernel, grid=(count,), in_specs=[smem, pl.BlockSpec(...  5.42 us
  transfers between devices with their start and end apart: 16, of which 9 were waited for; matrix products, arithmetic and copies ran while one was open for 2% of the time, Pallas kernels for 17%

profile of v8, /device:TPU:1, one launch (start us, length us, event | category | flops | bytes accessed | tf_op | source)
XLA Modules:
  0.0 99.6 jit_solution(6273519532497917728)
XLA Ops:
  0.6 0.0 copy-start.5
  0.6 1.7 %pack.1.packed_ref = f32[144,128]{1,0:T(8,128)} custom-call(f32[12,4,288]{2,1,0:T(4,128)} %bitcast.28, f32[12,288]{1,0:T(8,128)} %local_far.1), custom_call_target="tpu_custom_call" | custom-call | flops 1000000 | bytes 1000000 | tf_op jit(solution)/shard_map/pack/pallas_call | solution.py:550
  2.4 4.9 %collective-permute-start.2 = (f32[1,144,128]{2,1,0:T(8,128)}, f32[1,144,128]{2,1,0:T(8,128)S(1)}, u32[]{:S(2)}, u32[]{:S(2)}) collective-permute-start(f32[1,144,128]{2,1,0:T(8,128)} %bitcast.19), channel_id=1, source_target_pairs={{0,192},{8,88},{16,208},{24,72},{32,224},{40,120},{48,240},{56,104... | collective-permute-start | bytes 221192 | tf_op jit(solution)/shard_map/ppermute | solution.py:647
  7.3 0.2 collective-permute-start.1
  7.5 0.2 collective-permute-start
  7.7 1.9 %copy.15.o_ref = f32[1,12,9216]{2,1,0:T(8,128)} copy(f32[1,12,9216]{2,0,1:T(1,128)} %param.10) | data formatting | bytes 884736 | tf_op args[0]
  9.6 0.0 copy-start.1
  9.6 0.9 copy-done.1
  10.5 2.4 %orbital_rows.1 = (f32[1152,128]{1,0:T(8,128)}, f32[32,32,128]{2,1,0:T(8,128)}, f32[144,128]{1,0:T(8,128)S(1)}) custom-call(f32[1,12,9216]{2,1,0:T(8,128)} %copy.15.o_ref, f32[144,128]{1,0:T(8,128)S(1)} %copy-done.1), custom_call_target="tpu_custom_call" | custom-call | flops 1000000 | bytes 1000000 | tf_op jit(solution)/shard_map/orbital_rows/pallas_call | solution.py:557
  12.9 0.0 collective-permute-done.2
  12.9 0.0 collective-permute-done.1
  12.9 0.0 collective-permute-done
  12.9 0.0 copy-start.3
  12.9 0.0 copy-start.4
  13.0 7.7 %collective-permute-start.5 = (f32[4,144,128]{2,1,0:T(8,128)S(1)}, f32[4,144,128]{2,1,0:T(8,128)S(1)}, u32[]{:S(2)}, u32[]{:S(2)}) collective-permute-start(f32[4,144,128]{2,1,0:T(8,128)S(1)} %pad_maximum_fusion.p0), channel_id=1, source_target_pairs={{0,48},{8,248},{16,32},{24,232},{32,16},{40,216},{48,0},{56,200},{... | collective-permute-start | bytes 884744 | tf_op jit(solution)/shard_map/ppermute | solution.py:647
  20.7 0.0 collective-permute-start.4
  20.7 0.4 collective-permute-start.3
  21.1 2.3 %collective-permute-start.6 = (f32[4,144,128]{2,1,0:T(8,128)S(1)}, f32[4,144,128]{2,1,0:T(8,128)S(1)}, u32[]{:S(2)}, u32[]{:S(2)}) collective-permute-start(f32[4,144,128]{2,1,0:T(8,128)S(1)} %pad_maximum_fusion.p0), channel_id=1, source_target_pairs={{0,8},{8,0},{16,24},{24,16},{32,40},{40,32},{48,56},{56,48},{64,72... | collective-permute-start | bytes 884744 | tf_op jit(solution)/shard_map/ppermute | solution.py:643
  23.3 7.4 %collective-permute-done.5.p3 = f32[4,144,128]{2,1,0:T(8,128)S(1)} collective-permute-done((f32[4,144,128]{2,1,0:T(8,128)S(1)}, f32[4,144,128]{2,1,0:T(8,128)S(1)}, u32[]{:S(2)}, u32[]{:S(2)}) %collective-permute-start.5) | collective-permute-done | bytes 294944 | tf_op jit(solution)/shard_map/ppermute | solution.py:647
  30.7 4.8 %collective-permute-start.9 = (f32[4,144,128]{2,1,0:T(8,128)S(1)}, f32[4,144,128]{2,1,0:T(8,128)S(1)}, u32[]{:S(2)}, u32[]{:S(2)}) collective-permute-start(f32[4,144,128]{2,1,0:T(8,128)S(1)} %collective-permute-done.5.p3), channel_id=1, source_target_pairs={{0,8},{8,0},{16,24},{24,16},{32,40},{40,32},{48,56},{56,48},{64,72... | collective-permute-start | bytes 884744 | tf_op jit(solution)/shard_map/ppermute | solution.py:643
  35.4 0.0 collective-permute-done.4.p2
  35.4 0.0 collective-permute-start.8
  35.4 0.0 collective-permute-done.3.p1
  35.4 0.5 collective-permute-start.7
  35.9 0.0 collective-permute-done.6.p4
  35.9 0.7 collective-permute-done.9.p7
  36.6 0.0 copy-start.6
  36.6 0.4 collective-permute-done.8.p6
  37.1 0.0 copy-start.7
  37.1 0.4 collective-permute-done.7.p5
  37.5 0.0 copy-done.6
  37.5 0.3 copy-done.7
  37.8 0.0 copy-done.5
  37.8 6.3 %forward.1 = (f32[5,1152,128]{2,1,0:T(8,128)}, f32[1152,128]{1,0:T(8,128)}, f32[8,128]{1,0:T(8,128)S(1)}) custom-call(f32[4,144,128]{2,1,0:T(8,128)S(1)} %pad_maximum_fusion.p0, f32[4,144,128]{2,1,0:T(8,128)S(1)} %collective-permute-done.3.p1, f32[4,144,128]{2,1,0:T(8,128)S(1)} %collective-permute-done.4.p2, f32[4,144,128]{2,1,0:T(8,128)S(1)} %collective-permute-done.5.p3, ...), custom_call_target="tpu_custom_call" | custom-call | flops 1000000 | bytes 1000000 | tf_op jit(solution)/shard_map/forward/pallas_call | solution.py:570
  44.1 4.0 %all-to-all-start = ((f32[8,144,128]{2,1,0:T(8,128)}), f32[8,144,128]{2,1,0:T(8,128)S(1)}, u32[]{:S(2)}, u32[]{:S(2)}) async-start(f32[8,144,128]{2,1,0:T(8,128)} %bitcast.27), calls=%async_computation | async-start | bytes 1179648 | tf_op jit(solution)/shard_map/all_to_all | solution.py:672
  48.8 0.0 copy-done.3
  48.8 0.0 copy-done.4
  48.8 5.4 %local_sums.1 = (f32[8,128]{1,0:T(8,128)S(1)}, bf16[2,96,192]{2,1,0:T(8,128)(2,1)S(1)}, bf16[2,192,96]{2,1,0:T(8,128)(2,1)S(1)}, bf16[2,192,96]{2,1,0:T(8,128)(2...) custom-call(f32[1]{0:T(128)S(6)} %copy.17.energy_ref, ...), custom_call_target="tpu_custom_call" | custom-call | flops 10000000 | bytes 10000000 | tf_op jit(solution)/shard_map/local_sums/pallas_call | solution.py:584
  54.2 0.0 copy-start.2
  54.2 3.8 %all-to-all-done = f32[8,144,128]{2,1,0:T(8,128)S(1)} async-done(((f32[8,144,128]{2,1,0:T(8,128)}), f32[8,144,128]{2,1,0:T(8,128)S(1)}, u32[]{:S(2)}, u32[]{:S(2)}) %all-to-all-start) | async-done | bytes 589856 | tf_op jit(solution)/shard_map/all_to_all | solution.py:672
  58.0 1.2 %waves.1 = (f32[896,128]{1,0:T(8,128)S(1)}, f32[8,128]{1,0:T(8,128)S(1)}) custom-call(f32[1152,128]{1,0:T(8,128)S(1)} %bitcast.16, f32[8,128]{1,0:T(8,128)S(1)} %get-tuple-element.29.stat_ref, f32[8,128]{1,0:T(8,128)S(1)} %get-tuple-element.32.sums_ref, bf16[2,96,192]{2,1,0:T(8,128)(2,1)S(1)} %get-tuple-element.33.g2, ...), custom_call_target="tpu_custom_call" | custom-call | flops 1000000 | bytes 1000000 | tf_op jit(solution)/shard_map/waves/pallas_call | solution.py:597
  59.3 11.6 %all_to_all.15 = f32[8,112,128]{2,1,0:T(8,128)S(1)} all-to-all(f32[8,112,128]{2,1,0:T(8,128)S(1)} %bitcast.23), channel_id=1, replica_groups=mesh['band'=32,'grid'=8] {'grid'}, dimensions={0} | all-to-all | bytes 917504 | tf_op jit(solution)/shard_map/all_to_all | solution.py:675
  70.9 0.0 copy-start
  70.9 0.0 copy-done.2
  70.9 0.8 steps.1
  71.7 7.8 %all-to-all-start.2 = ((f32[32,32,128]{2,1,0:T(8,128)}), f32[32,32,128]{2,1,0:T(8,128)S(1)}, u32[]{:S(2)}, u32[]{:S(2)}) async-start(f32[32,32,128]{2,1,0:T(8,128)} %get-tuple-element.45), calls=%async_computation.2 | async-start | bytes 1048576 | tf_op jit(solution)/shard_map/all_to_all | solution.py:677
  79.5 0.0 copy-done
  79.5 5.9 %image.1 = (f32[12,4,9216]{2,1,0:T(4,128)}, f32[12,4,9216]{2,1,0:T(4,128)}, f32[8,128]{1,0:T(8,128)S(1)}) custom-call(f32[1]{0:T(128)S(6)} %copy.17.energy_ref, f32[896,128]{1,0:T(8,128)} %bitcast.18, f32[8,128]{1,0:T(8,128)S(1)} %get-tuple-element.38.step_ref, f32[5,1152,128]{2,1,0:T(8,128)} %get-tuple-element.30.field_ref.field_far, ...), custom_call_target="tpu_custom_call" | custom-call | flops 20000000000 | bytes 1000000 | tf_op jit(solution)/shard_map/image/pallas_call | solution.py:612
  85.5 0.7 collective-permute-start.12
  86.2 1.2 %collective-permute-start.11 = (f32[8,128]{1,0:T(8,128)S(1)}, f32[8,128]{1,0:T(8,128)S(1)}, u32[]{:S(2)}, u32[]{:S(2)}) collective-permute-start(f32[8,128]{1,0:T(8,128)S(1)} %get-tuple-element.43), channel_id=1, source_target_pairs={{0,4},{1,5},{2,6},{3,7},{4,0},{5,1},{6,2},{7,3},{8,12},{9,13},{10,... | collective-permute-start | bytes 12296 | tf_op jit(solution)/shard_map/ppermute | solution.py:643
  87.4 1.4 %collective-permute-start.10 = (f32[8,128]{1,0:T(8,128)S(1)}, f32[8,128]{1,0:T(8,128)S(1)}, u32[]{:S(2)}, u32[]{:S(2)}) collective-permute-start(f32[8,128]{1,0:T(8,128)S(1)} %get-tuple-element.43), channel_id=1, source_target_pairs={{0,2},{1,3},{2,0},{3,1},{4,6},{5,7},{6,4},{7,5},{8,10},{9,11},{10,... | collective-permute-start | bytes 12296 | tf_op jit(solution)/shard_map/ppermute | solution.py:643
  88.8 0.7 collective-permute-done.12
  89.5 0.9 collective-permute-done.11
  90.4 0.0 collective-permute-done.10
  90.4 0.9 collective-permute-start.13
  91.3 2.2 %collective-permute-done.13.n1 = f32[8,128]{1,0:T(8,128)S(1)} collective-permute-done((f32[8,128]{1,0:T(8,128)S(1)}, f32[8,128]{1,0:T(8,128)S(1)}, u32[]{:S(2)}, u32[]{:S(2)}) %collective-permute-start.13) | collective-permute-done | bytes 4128 | tf_op jit(solution)/shard_map/ppermute | solution.py:643
  93.5 2.9 %direction.1 = f32[12,4,9216]{2,1,0:T(4,128)} custom-call(f32[8,128]{1,0:T(8,128)S(1)} %get-tuple-element.38.step_ref, f32[8,128]{1,0:T(8,128)S(1)} %add_add_fusion.n0, f32[8,128]{1,0:T(8,128)S(1)} %collective-permute-done.13.n1, f32[12,4,9216]{2,1,0:T(4,128)} %get-tuple-element.41.response_ref, f32[12,4,9216]{2,1,0:T(4,128)} %get-tuple-element.42.residual_ref), custom_call_target="tpu_custom_call" | custom-call | flops 10000000 | bytes 1000000 | tf_op jit(solution)/shard_map/direction/pallas_call | solution.py:624
  96.4 1.5 %all-to-all-done.2.band_ref = f32[32,32,128]{2,1,0:T(8,128)S(1)} async-done(((f32[32,32,128]{2,1,0:T(8,128)}), f32[32,32,128]{2,1,0:T(8,128)S(1)}, u32[]{:S(2)}, u32[]{:S(2)}) %all-to-all-start.2) | async-done | bytes 524320 | tf_op jit(solution)/shard_map/all_to_all | solution.py:677
  97.9 1.5 %density.1 = f32[12,4,288]{2,1,0:T(4,128)} custom-call(f32[144,128]{1,0:T(8,128)S(1)} %get-tuple-element.44.packed_far, f32[32,32,128]{2,1,0:T(8,128)S(1)} %all-to-all-done.2.band_ref), custom_call_target="tpu_custom_call" | custom-call | flops 1000000 | bytes 1000000 | tf_op jit(solution)/shard_map/density/pallas_call | solution.py:632
  (2 shorter events, 0.0 us)
Async XLA Ops:
  0.6 37.1 %copy-start.5 = (bf16[2,96,192]{2,1,0:T(8,128)(2,1)S(1)}, bf16[2,96,192]{2,1,0:T(8,128)(2,1)}, u32[]{:S(2)}) copy-start(bf16[2,96,192]{2,1,0:T(8,128)(2,1)} %constant.13.clone.g1_ref) | copy-start | bytes 221188
  2.4 10.5 %collective-permute-start.2 = (f32[1,144,128]{2,1,0:T(8,128)}, f32[1,144,128]{2,1,0:T(8,128)S(1)}, u32[]{:S(2)}, u32[]{:S(2)}) collective-permute-start(f32[1,144,128]{2,1,0:T(8,128)} %bitcast.19), channel_id=1, source_target_pairs={{0,192},{8,88},{16,208},{24,72},{32,224},{40,120},{48,240},{56,104... | collective-permute-start | bytes 221192 | tf_op jit(solution)/shard_map/ppermute | solution.py:647
  7.3 5.6 %collective-permute-start.1 = (f32[1,144,128]{2,1,0:T(8,128)}, f32[1,144,128]{2,1,0:T(8,128)S(1)}, u32[]{:S(2)}, u32[]{:S(2)}) collective-permute-start(f32[1,144,128]{2,1,0:T(8,128)} %bitcast.20), channel_id=1, source_target_pairs={{0,128},{8,24},{16,144},{24,8},{32,160},{40,56},{48,176},{56,40},{... | collective-permute-start | bytes 221192 | tf_op jit(solution)/shard_map/ppermute | solution.py:647
  7.5 5.4 %collective-permute-start = (f32[1,144,128]{2,1,0:T(8,128)}, f32[1,144,128]{2,1,0:T(8,128)S(1)}, u32[]{:S(2)}, u32[]{:S(2)}) collective-permute-start(f32[1,144,128]{2,1,0:T(8,128)} %bitcast.21), channel_id=1, source_target_pairs={{0,64},{8,72},{16,80},{24,88},{32,96},{40,104},{48,112},{56,120},{... | collective-permute-start | bytes 221192 | tf_op jit(solution)/shard_map/ppermute | solution.py:647
  9.6 0.9 copy-start.1
  12.9 35.8 %copy-start.3 = (bf16[2,192,96]{2,1,0:T(8,128)(2,1)S(1)}, bf16[2,192,96]{2,1,0:T(8,128)(2,1)}, u32[]{:S(2)}) copy-start(bf16[2,192,96]{2,1,0:T(8,128)(2,1)} %constant.15.clone.g3_ref) | copy-start | bytes 221188
  12.9 35.8 %copy-start.4 = (bf16[2,96,192]{2,1,0:T(8,128)(2,1)S(1)}, bf16[2,96,192]{2,1,0:T(8,128)(2,1)}, u32[]{:S(2)}) copy-start(bf16[2,96,192]{2,1,0:T(8,128)(2,1)} %constant.14.clone.g2_ref) | copy-start | bytes 221188
  13.0 17.7 %collective-permute-start.5 = (f32[4,144,128]{2,1,0:T(8,128)S(1)}, f32[4,144,128]{2,1,0:T(8,128)S(1)}, u32[]{:S(2)}, u32[]{:S(2)}) collective-permute-start(f32[4,144,128]{2,1,0:T(8,128)S(1)} %pad_maximum_fusion.p0), channel_id=1, source_target_pairs={{0,48},{8,248},{16,32},{24,232},{32,16},{40,216},{48,0},{56,200},{... | collective-permute-start | bytes 884744 | tf_op jit(solution)/shard_map/ppermute | solution.py:647
  20.7 14.7 %collective-permute-start.4 = (f32[4,144,128]{2,1,0:T(8,128)S(1)}, f32[4,144,128]{2,1,0:T(8,128)S(1)}, u32[]{:S(2)}, u32[]{:S(2)}) collective-permute-start(f32[4,144,128]{2,1,0:T(8,128)S(1)} %pad_maximum_fusion.p0), channel_id=1, source_target_pairs={{0,32},{8,56},{16,48},{24,40},{32,0},{40,24},{48,16},{56,8},{64,96... | collective-permute-start | bytes 884744 | tf_op jit(solution)/shard_map/ppermute | solution.py:647
  20.7 14.8 %collective-permute-start.3 = (f32[4,144,128]{2,1,0:T(8,128)S(1)}, f32[4,144,128]{2,1,0:T(8,128)S(1)}, u32[]{:S(2)}, u32[]{:S(2)}) collective-permute-start(f32[4,144,128]{2,1,0:T(8,128)S(1)} %pad_maximum_fusion.p0), channel_id=1, source_target_pairs={{0,16},{8,200},{16,0},{24,216},{32,48},{40,232},{48,32},{56,248},{... | collective-permute-start | bytes 884744 | tf_op jit(solution)/shard_map/ppermute | solution.py:647
  21.1 14.9 %collective-permute-start.6 = (f32[4,144,128]{2,1,0:T(8,128)S(1)}, f32[4,144,128]{2,1,0:T(8,128)S(1)}, u32[]{:S(2)}, u32[]{:S(2)}) collective-permute-start(f32[4,144,128]{2,1,0:T(8,128)S(1)} %pad_maximum_fusion.p0), channel_id=1, source_target_pairs={{0,8},{8,0},{16,24},{24,16},{32,40},{40,32},{48,56},{56,48},{64,72... | collective-permute-start | bytes 884744 | tf_op jit(solution)/shard_map/ppermute | solution.py:643
  30.7 6.0 %collective-permute-start.9 = (f32[4,144,128]{2,1,0:T(8,128)S(1)}, f32[4,144,128]{2,1,0:T(8,128)S(1)}, u32[]{:S(2)}, u32[]{:S(2)}) collective-permute-start(f32[4,144,128]{2,1,0:T(8,128)S(1)} %collective-permute-done.5.p3), channel_id=1, source_target_pairs={{0,8},{8,0},{16,24},{24,16},{32,40},{40,32},{48,56},{56,48},{64,72... | collective-permute-start | bytes 884744 | tf_op jit(solution)/shard_map/ppermute | solution.py:643
  35.4 1.6 %collective-permute-start.8 = (f32[4,144,128]{2,1,0:T(8,128)S(1)}, f32[4,144,128]{2,1,0:T(8,128)S(1)}, u32[]{:S(2)}, u32[]{:S(2)}) collective-permute-start(f32[4,144,128]{2,1,0:T(8,128)S(1)} %collective-permute-done.4.p2), channel_id=1, source_target_pairs={{0,8},{8,0},{16,24},{24,16},{32,40},{40,32},{48,56},{56,48},{64,72... | collective-permute-start | bytes 884744 | tf_op jit(solution)/shard_map/ppermute | solution.py:643
  35.4 2.0 %collective-permute-start.7 = (f32[4,144,128]{2,1,0:T(8,128)S(1)}, f32[4,144,128]{2,1,0:T(8,128)S(1)}, u32[]{:S(2)}, u32[]{:S(2)}) collective-permute-start(f32[4,144,128]{2,1,0:T(8,128)S(1)} %collective-permute-done.3.p1), channel_id=1, source_target_pairs={{0,8},{8,0},{16,24},{24,16},{32,40},{40,32},{48,56},{56,48},{64,72... | collective-permute-start | bytes 884744 | tf_op jit(solution)/shard_map/ppermute | solution.py:643
  36.6 0.8 copy-start.6
  37.1 0.7 copy-start.7
  44.1 13.9 %all-to-all-start = ((f32[8,144,128]{2,1,0:T(8,128)}), f32[8,144,128]{2,1,0:T(8,128)S(1)}, u32[]{:S(2)}, u32[]{:S(2)}) async-start(f32[8,144,128]{2,1,0:T(8,128)} %bitcast.27), calls=%async_computation | async-start | bytes 1179648 | tf_op jit(solution)/shard_map/all_to_all | solution.py:672
  54.2 16.7 %copy-start.2 = (f32[32,8,128]{2,1,0:T(8,128)S(1)}, f32[32,8,128]{2,1,0:T(8,128)}, u32[]{:S(2)}) copy-start(f32[32,8,128]{2,1,0:T(8,128)} %get-tuple-element.37.tail_ref) | copy-start | bytes 393220
  70.9 8.6 %copy-start = (f32[8,112,128]{2,1,0:T(8,128)}, f32[8,112,128]{2,1,0:T(8,128)S(1)}, u32[]{:S(2)}) copy-start(f32[8,112,128]{2,1,0:T(8,128)S(1)} %all_to_all.15) | copy-start | bytes 1376260
  71.7 26.2 %all-to-all-start.2 = ((f32[32,32,128]{2,1,0:T(8,128)}), f32[32,32,128]{2,1,0:T(8,128)S(1)}, u32[]{:S(2)}, u32[]{:S(2)}) async-start(f32[32,32,128]{2,1,0:T(8,128)} %get-tuple-element.45), calls=%async_computation.2 | async-start | bytes 1048576 | tf_op jit(solution)/shard_map/all_to_all | solution.py:677
  85.5 4.0 %collective-permute-start.12 = (f32[8,128]{1,0:T(8,128)S(1)}, f32[8,128]{1,0:T(8,128)S(1)}, u32[]{:S(2)}, u32[]{:S(2)}) collective-permute-start(f32[8,128]{1,0:T(8,128)S(1)} %get-tuple-element.43), channel_id=1, source_target_pairs={{0,6},{1,7},{2,4},{3,5},{4,2},{5,3},{6,0},{7,1},{8,14},{9,15},{10,... | collective-permute-start | bytes 12296 | tf_op jit(solution)/shard_map/ppermute | solution.py:643
  86.2 4.3 %collective-permute-start.11 = (f32[8,128]{1,0:T(8,128)S(1)}, f32[8,128]{1,0:T(8,128)S(1)}, u32[]{:S(2)}, u32[]{:S(2)}) collective-permute-start(f32[8,128]{1,0:T(8,128)S(1)} %get-tuple-element.43), channel_id=1, source_target_pairs={{0,4},{1,5},{2,6},{3,7},{4,0},{5,1},{6,2},{7,3},{8,12},{9,13},{10,... | collective-permute-start | bytes 12296 | tf_op jit(solution)/shard_map/ppermute | solution.py:643
  87.4 3.1 %collective-permute-start.10 = (f32[8,128]{1,0:T(8,128)S(1)}, f32[8,128]{1,0:T(8,128)S(1)}, u32[]{:S(2)}, u32[]{:S(2)}) collective-permute-start(f32[8,128]{1,0:T(8,128)S(1)} %get-tuple-element.43), channel_id=1, source_target_pairs={{0,2},{1,3},{2,0},{3,1},{4,6},{5,7},{6,4},{7,5},{8,10},{9,11},{10,... | collective-permute-start | bytes 12296 | tf_op jit(solution)/shard_map/ppermute | solution.py:643
  90.4 3.1 %collective-permute-start.13 = (f32[8,128]{1,0:T(8,128)S(1)}, f32[8,128]{1,0:T(8,128)S(1)}, u32[]{:S(2)}, u32[]{:S(2)}) collective-permute-start(f32[8,128]{1,0:T(8,128)S(1)} %add_add_fusion.n0), channel_id=1, source_target_pairs={{0,1},{1,0},{2,3},{3,2},{4,5},{5,4},{6,7},{7,6},{8,9},{9,8},{10,11... | collective-permute-start | bytes 12296 | tf_op jit(solution)/shard_map/ppermute | solution.py:643

commit v9 on v8

--- a/solution.py
+++ b/solution.py
@@ -475,7 +475,7 @@
 
 
 def direction_kernel(step_ref, n0, n1, response_ref, residual_ref, direction_ref, first, second, result, sems, out_sems):
-    parts = 6
+    parts = 3
     width = points * points // parts
     loads = []
     for i in range(parts):
@@ -578,7 +578,7 @@
 
 
 def local_sums(energies, fields, o, stat, tables, base):
-    size, count = 192, rows // 192
+    size, count = 384, rows // 384
     tile = pl.BlockSpec((8, 128), lambda i: (0, 0))
     kinds = [tables[name] for name in ("g2", "g3", "g4", "w2")]
     return pl.pallas_call(
@@ -620,7 +620,7 @@
 
 
 def direct(step, norms, response, residual):
-    part = buffer(6, planes, trials, points * points // 6)
+    part = buffer(3, planes, trials, points * points // 3)
     return call(
         direction_kernel, [vmem] * 3 + [far] * 2, shape(planes, trials, points * points),
         [part, part, part, pltpu.SemaphoreType.DMA((2, 6)), pltpu.SemaphoreType.DMA((6,))],

time: 100 us -> 100 us (level)
    all_to_all x1, waiting for transfers between devices: 3.81 us -> 4.84 us  [on_device(): lax.all_to_all(sent.reshape(groups, chunk, 128), 'grid', 0, 0, tiled=True)]
    pallas_call x1, Pallas kernels: 5.42 us -> 4.38 us  [local_sums(): pl.pallas_call(local_kernel, grid=(count,), in_specs=[smem, pl.BlockSpec(...]
  transfers between devices with their start and end apart: 16 -> 16, of which waited for: 9 -> 9; matrix products, arithmetic and copies ran while one was open for 2% -> 2% of each run, Pallas kernels for 17% -> 16%
where the time goes in v9:
time: 100 us; the launch traced here: 99.6 us
  starting transfers between devices  37 us (37%)
  Pallas kernels  27.4 us (27%)
  waiting for transfers between devices  18.9 us (19%)
  blocking collectives  11.6 us (12%)
  local copies, waits for them, and re-layouts  3.13 us (3%)
  between operations  1.62 us (2%)
    ppermute x6, starting transfers between devices, crossed(): lax.ppermute(value, 'band', [(s, s ^ (odd if s & 1 else even)) for s in r...  13.4 us
    ppermute x8, starting transfers between devices, swapped(): return lax.ppermute(value, axis, [(s, s ^ mask) for s in range(size)])  11.8 us
    all_to_all x1, blocking collectives, on_device(): lax.all_to_all(back.reshape(groups, returned, 128), 'grid', 0, 0, tiled=T...  11.6 us
    all_to_all x1, starting transfers between devices, on_device(): band = lax.all_to_all(payload, 'band', 0, 0, tiled=True)  7.78 us
    ppermute x6, waiting for transfers between devices, crossed(): lax.ppermute(value, 'band', [(s, s ^ (odd if s & 1 else even)) for s in r...  7.36 us
    pallas_call x1, Pallas kernels, forward(): call(forward_kernel, [hbm] * 8 + [far] * 3, (shape(5, rows, 128), shape(r...  6.31 us
    pallas_call x1, Pallas kernels, image(): call(image_kernel, [smem, vmem, vmem, far, far, vmem, vmem], (cells, cell...  5.93 us
    ppermute x8, waiting for transfers between devices, swapped(): return lax.ppermute(value, axis, [(s, s ^ mask) for s in range(size)])  5.33 us
  transfers between devices with their start and end apart: 16, of which 9 were waited for; matrix products, arithmetic and copies ran while one was open for 2% of the time, Pallas kernels for 16%

profile of v9, /device:TPU:1, one launch (start us, length us, event | category | flops | bytes accessed | tf_op | source)
XLA Modules:
  0.0 99.6 jit_solution(13972302042386795571)
XLA Ops:
  0.6 0.0 copy-start.5
  0.6 1.7 %pack.1.packed_ref = f32[144,128]{1,0:T(8,128)} custom-call(f32[12,4,288]{2,1,0:T(4,128)} %bitcast.28, f32[12,288]{1,0:T(8,128)} %local_far.1), custom_call_target="tpu_custom_call" | custom-call | flops 1000000 | bytes 1000000 | tf_op jit(solution)/shard_map/pack/pallas_call | solution.py:550
  2.4 4.9 %collective-permute-start.2 = (f32[1,144,128]{2,1,0:T(8,128)}, f32[1,144,128]{2,1,0:T(8,128)S(1)}, u32[]{:S(2)}, u32[]{:S(2)}) collective-permute-start(f32[1,144,128]{2,1,0:T(8,128)} %bitcast.19), channel_id=1, source_target_pairs={{0,192},{8,88},{16,208},{24,72},{32,224},{40,120},{48,240},{56,104... | collective-permute-start | bytes 221192 | tf_op jit(solution)/shard_map/ppermute | solution.py:647
  7.3 0.2 collective-permute-start.1
  7.5 0.2 collective-permute-start
  7.7 1.9 %copy.15.o_ref = f32[1,12,9216]{2,1,0:T(8,128)} copy(f32[1,12,9216]{2,0,1:T(1,128)} %param.10) | data formatting | bytes 884736 | tf_op args[0]
  9.6 0.0 copy-start.1
  9.6 0.9 copy-done.1
  10.5 2.4 %orbital_rows.1 = (f32[1152,128]{1,0:T(8,128)}, f32[32,32,128]{2,1,0:T(8,128)}, f32[144,128]{1,0:T(8,128)S(1)}) custom-call(f32[1,12,9216]{2,1,0:T(8,128)} %copy.15.o_ref, f32[144,128]{1,0:T(8,128)S(1)} %copy-done.1), custom_call_target="tpu_custom_call" | custom-call | flops 1000000 | bytes 1000000 | tf_op jit(solution)/shard_map/orbital_rows/pallas_call | solution.py:557
  12.9 0.0 collective-permute-done.2
  12.9 0.0 collective-permute-done.1
  12.9 0.0 collective-permute-done
  12.9 0.0 copy-start.3
  12.9 0.0 copy-start.4
  13.0 7.7 %collective-permute-start.5 = (f32[4,144,128]{2,1,0:T(8,128)S(1)}, f32[4,144,128]{2,1,0:T(8,128)S(1)}, u32[]{:S(2)}, u32[]{:S(2)}) collective-permute-start(f32[4,144,128]{2,1,0:T(8,128)S(1)} %pad_maximum_fusion.p0), channel_id=1, source_target_pairs={{0,48},{8,248},{16,32},{24,232},{32,16},{40,216},{48,0},{56,200},{... | collective-permute-start | bytes 884744 | tf_op jit(solution)/shard_map/ppermute | solution.py:647
  20.7 0.0 collective-permute-start.4
  20.7 0.4 collective-permute-start.3
  21.1 2.3 %collective-permute-start.6 = (f32[4,144,128]{2,1,0:T(8,128)S(1)}, f32[4,144,128]{2,1,0:T(8,128)S(1)}, u32[]{:S(2)}, u32[]{:S(2)}) collective-permute-start(f32[4,144,128]{2,1,0:T(8,128)S(1)} %pad_maximum_fusion.p0), channel_id=1, source_target_pairs={{0,8},{8,0},{16,24},{24,16},{32,40},{40,32},{48,56},{56,48},{64,72... | collective-permute-start | bytes 884744 | tf_op jit(solution)/shard_map/ppermute | solution.py:643
  23.3 7.4 %collective-permute-done.5.p3 = f32[4,144,128]{2,1,0:T(8,128)S(1)} collective-permute-done((f32[4,144,128]{2,1,0:T(8,128)S(1)}, f32[4,144,128]{2,1,0:T(8,128)S(1)}, u32[]{:S(2)}, u32[]{:S(2)}) %collective-permute-start.5) | collective-permute-done | bytes 294944 | tf_op jit(solution)/shard_map/ppermute | solution.py:647
  30.7 4.8 %collective-permute-start.9 = (f32[4,144,128]{2,1,0:T(8,128)S(1)}, f32[4,144,128]{2,1,0:T(8,128)S(1)}, u32[]{:S(2)}, u32[]{:S(2)}) collective-permute-start(f32[4,144,128]{2,1,0:T(8,128)S(1)} %collective-permute-done.5.p3), channel_id=1, source_target_pairs={{0,8},{8,0},{16,24},{24,16},{32,40},{40,32},{48,56},{56,48},{64,72... | collective-permute-start | bytes 884744 | tf_op jit(solution)/shard_map/ppermute | solution.py:643
  35.4 0.0 collective-permute-done.4.p2
  35.4 0.0 collective-permute-start.8
  35.4 0.0 collective-permute-done.3.p1
  35.4 0.5 collective-permute-start.7
  35.9 0.0 collective-permute-done.6.p4
  35.9 0.7 collective-permute-done.9.p7
  36.6 0.0 copy-start.6
  36.6 0.4 collective-permute-done.8.p6
  37.1 0.0 copy-start.7
  37.1 0.4 collective-permute-done.7.p5
  37.5 0.0 copy-done.6
  37.5 0.3 copy-done.7
  37.8 0.0 copy-done.5
  37.8 6.3 %forward.1 = (f32[5,1152,128]{2,1,0:T(8,128)}, f32[1152,128]{1,0:T(8,128)}, f32[8,128]{1,0:T(8,128)S(1)}) custom-call(f32[4,144,128]{2,1,0:T(8,128)S(1)} %pad_maximum_fusion.p0, f32[4,144,128]{2,1,0:T(8,128)S(1)} %collective-permute-done.3.p1, f32[4,144,128]{2,1,0:T(8,128)S(1)} %collective-permute-done.4.p2, f32[4,144,128]{2,1,0:T(8,128)S(1)} %collective-permute-done.5.p3, ...), custom_call_target="tpu_custom_call" | custom-call | flops 1000000 | bytes 1000000 | tf_op jit(solution)/shard_map/forward/pallas_call | solution.py:570
  44.1 4.0 %all-to-all-start = ((f32[8,144,128]{2,1,0:T(8,128)}), f32[8,144,128]{2,1,0:T(8,128)S(1)}, u32[]{:S(2)}, u32[]{:S(2)}) async-start(f32[8,144,128]{2,1,0:T(8,128)} %bitcast.27), calls=%async_computation | async-start | bytes 1179648 | tf_op jit(solution)/shard_map/all_to_all | solution.py:672
  48.8 0.0 copy-done.3
  48.8 0.0 copy-done.4
  48.8 4.4 %local_sums.1 = (f32[8,128]{1,0:T(8,128)S(1)}, bf16[2,96,192]{2,1,0:T(8,128)(2,1)S(1)}, bf16[2,192,96]{2,1,0:T(8,128)(2,1)S(1)}, bf16[2,192,96]{2,1,0:T(8,128)(2...) custom-call(f32[1]{0:T(128)S(6)} %copy.17.energy_ref, ...), custom_call_target="tpu_custom_call" | custom-call | flops 10000000 | bytes 10000000 | tf_op jit(solution)/shard_map/local_sums/pallas_call | solution.py:584
  53.2 0.0 copy-start.2
  53.2 4.8 %all-to-all-done = f32[8,144,128]{2,1,0:T(8,128)S(1)} async-done(((f32[8,144,128]{2,1,0:T(8,128)}), f32[8,144,128]{2,1,0:T(8,128)S(1)}, u32[]{:S(2)}, u32[]{:S(2)}) %all-to-all-start) | async-done | bytes 589856 | tf_op jit(solution)/shard_map/all_to_all | solution.py:672
  58.0 1.2 %waves.1 = (f32[896,128]{1,0:T(8,128)S(1)}, f32[8,128]{1,0:T(8,128)S(1)}) custom-call(f32[1152,128]{1,0:T(8,128)S(1)} %bitcast.16, f32[8,128]{1,0:T(8,128)S(1)} %get-tuple-element.29.stat_ref, f32[8,128]{1,0:T(8,128)S(1)} %get-tuple-element.32.sums_ref, bf16[2,96,192]{2,1,0:T(8,128)(2,1)S(1)} %get-tuple-element.33.g2, ...), custom_call_target="tpu_custom_call" | custom-call | flops 1000000 | bytes 1000000 | tf_op jit(solution)/shard_map/waves/pallas_call | solution.py:597
  59.3 11.6 %all_to_all.15 = f32[8,112,128]{2,1,0:T(8,128)S(1)} all-to-all(f32[8,112,128]{2,1,0:T(8,128)S(1)} %bitcast.23), channel_id=1, replica_groups=mesh['band'=32,'grid'=8] {'grid'}, dimensions={0} | all-to-all | bytes 917504 | tf_op jit(solution)/shard_map/all_to_all | solution.py:675
  70.9 0.0 copy-start
  70.9 0.0 copy-done.2
  70.9 0.8 steps.1
  71.7 7.8 %all-to-all-start.2 = ((f32[32,32,128]{2,1,0:T(8,128)}), f32[32,32,128]{2,1,0:T(8,128)S(1)}, u32[]{:S(2)}, u32[]{:S(2)}) async-start(f32[32,32,128]{2,1,0:T(8,128)} %get-tuple-element.45), calls=%async_computation.2 | async-start | bytes 1048576 | tf_op jit(solution)/shard_map/all_to_all | solution.py:677
  79.5 0.0 copy-done
  79.5 5.9 %image.1 = (f32[12,4,9216]{2,1,0:T(4,128)}, f32[12,4,9216]{2,1,0:T(4,128)}, f32[8,128]{1,0:T(8,128)S(1)}) custom-call(f32[1]{0:T(128)S(6)} %copy.17.energy_ref, f32[896,128]{1,0:T(8,128)} %bitcast.18, f32[8,128]{1,0:T(8,128)S(1)} %get-tuple-element.38.step_ref, f32[5,1152,128]{2,1,0:T(8,128)} %get-tuple-element.30.field_ref.field_far, ...), custom_call_target="tpu_custom_call" | custom-call | flops 20000000000 | bytes 1000000 | tf_op jit(solution)/shard_map/image/pallas_call | solution.py:612
  85.5 0.7 collective-permute-start.12
  86.2 1.2 %collective-permute-start.11 = (f32[8,128]{1,0:T(8,128)S(1)}, f32[8,128]{1,0:T(8,128)S(1)}, u32[]{:S(2)}, u32[]{:S(2)}) collective-permute-start(f32[8,128]{1,0:T(8,128)S(1)} %get-tuple-element.43), channel_id=1, source_target_pairs={{0,4},{1,5},{2,6},{3,7},{4,0},{5,1},{6,2},{7,3},{8,12},{9,13},{10,... | collective-permute-start | bytes 12296 | tf_op jit(solution)/shard_map/ppermute | solution.py:643
  87.4 1.4 %collective-permute-start.10 = (f32[8,128]{1,0:T(8,128)S(1)}, f32[8,128]{1,0:T(8,128)S(1)}, u32[]{:S(2)}, u32[]{:S(2)}) collective-permute-start(f32[8,128]{1,0:T(8,128)S(1)} %get-tuple-element.43), channel_id=1, source_target_pairs={{0,2},{1,3},{2,0},{3,1},{4,6},{5,7},{6,4},{7,5},{8,10},{9,11},{10,... | collective-permute-start | bytes 12296 | tf_op jit(solution)/shard_map/ppermute | solution.py:643
  88.8 0.7 collective-permute-done.12
  89.5 0.9 collective-permute-done.11
  90.4 0.0 collective-permute-done.10
  90.4 0.9 collective-permute-start.13
  91.3 2.2 %collective-permute-done.13.n1 = f32[8,128]{1,0:T(8,128)S(1)} collective-permute-done((f32[8,128]{1,0:T(8,128)S(1)}, f32[8,128]{1,0:T(8,128)S(1)}, u32[]{:S(2)}, u32[]{:S(2)}) %collective-permute-start.13) | collective-permute-done | bytes 4128 | tf_op jit(solution)/shard_map/ppermute | solution.py:643
  93.5 3.1 %direction.1 = f32[12,4,9216]{2,1,0:T(4,128)} custom-call(f32[8,128]{1,0:T(8,128)S(1)} %get-tuple-element.38.step_ref, f32[8,128]{1,0:T(8,128)S(1)} %add_add_fusion.n0, f32[8,128]{1,0:T(8,128)S(1)} %collective-permute-done.13.n1, f32[12,4,9216]{2,1,0:T(4,128)} %get-tuple-element.41.response_ref, f32[12,4,9216]{2,1,0:T(4,128)} %get-tuple-element.42.residual_ref), custom_call_target="tpu_custom_call" | custom-call | flops 10000000 | bytes 1000000 | tf_op jit(solution)/shard_map/direction/pallas_call | solution.py:624
  96.6 1.4 %all-to-all-done.2.band_ref = f32[32,32,128]{2,1,0:T(8,128)S(1)} async-done(((f32[32,32,128]{2,1,0:T(8,128)}), f32[32,32,128]{2,1,0:T(8,128)S(1)}, u32[]{:S(2)}, u32[]{:S(2)}) %all-to-all-start.2) | async-done | bytes 524320 | tf_op jit(solution)/shard_map/all_to_all | solution.py:677
  97.9 1.5 %density.1 = f32[12,4,288]{2,1,0:T(4,128)} custom-call(f32[144,128]{1,0:T(8,128)S(1)} %get-tuple-element.44.packed_far, f32[32,32,128]{2,1,0:T(8,128)S(1)} %all-to-all-done.2.band_ref), custom_call_target="tpu_custom_call" | custom-call | flops 1000000 | bytes 1000000 | tf_op jit(solution)/shard_map/density/pallas_call | solution.py:632
  (2 shorter events, 0.0 us)
Async XLA Ops:
  0.6 37.1 %copy-start.5 = (bf16[2,96,192]{2,1,0:T(8,128)(2,1)S(1)}, bf16[2,96,192]{2,1,0:T(8,128)(2,1)}, u32[]{:S(2)}) copy-start(bf16[2,96,192]{2,1,0:T(8,128)(2,1)} %constant.13.clone.g1_ref) | copy-start | bytes 221188
  2.4 10.5 %collective-permute-start.2 = (f32[1,144,128]{2,1,0:T(8,128)}, f32[1,144,128]{2,1,0:T(8,128)S(1)}, u32[]{:S(2)}, u32[]{:S(2)}) collective-permute-start(f32[1,144,128]{2,1,0:T(8,128)} %bitcast.19), channel_id=1, source_target_pairs={{0,192},{8,88},{16,208},{24,72},{32,224},{40,120},{48,240},{56,104... | collective-permute-start | bytes 221192 | tf_op jit(solution)/shard_map/ppermute | solution.py:647
  7.3 5.6 %collective-permute-start.1 = (f32[1,144,128]{2,1,0:T(8,128)}, f32[1,144,128]{2,1,0:T(8,128)S(1)}, u32[]{:S(2)}, u32[]{:S(2)}) collective-permute-start(f32[1,144,128]{2,1,0:T(8,128)} %bitcast.20), channel_id=1, source_target_pairs={{0,128},{8,24},{16,144},{24,8},{32,160},{40,56},{48,176},{56,40},{... | collective-permute-start | bytes 221192 | tf_op jit(solution)/shard_map/ppermute | solution.py:647
  7.5 5.4 %collective-permute-start = (f32[1,144,128]{2,1,0:T(8,128)}, f32[1,144,128]{2,1,0:T(8,128)S(1)}, u32[]{:S(2)}, u32[]{:S(2)}) collective-permute-start(f32[1,144,128]{2,1,0:T(8,128)} %bitcast.21), channel_id=1, source_target_pairs={{0,64},{8,72},{16,80},{24,88},{32,96},{40,104},{48,112},{56,120},{... | collective-permute-start | bytes 221192 | tf_op jit(solution)/shard_map/ppermute | solution.py:647
  9.6 0.9 copy-start.1
  12.9 35.8 %copy-start.3 = (bf16[2,192,96]{2,1,0:T(8,128)(2,1)S(1)}, bf16[2,192,96]{2,1,0:T(8,128)(2,1)}, u32[]{:S(2)}) copy-start(bf16[2,192,96]{2,1,0:T(8,128)(2,1)} %constant.15.clone.g3_ref) | copy-start | bytes 221188
  12.9 35.8 %copy-start.4 = (bf16[2,96,192]{2,1,0:T(8,128)(2,1)S(1)}, bf16[2,96,192]{2,1,0:T(8,128)(2,1)}, u32[]{:S(2)}) copy-start(bf16[2,96,192]{2,1,0:T(8,128)(2,1)} %constant.14.clone.g2_ref) | copy-start | bytes 221188
  13.0 17.7 %collective-permute-start.5 = (f32[4,144,128]{2,1,0:T(8,128)S(1)}, f32[4,144,128]{2,1,0:T(8,128)S(1)}, u32[]{:S(2)}, u32[]{:S(2)}) collective-permute-start(f32[4,144,128]{2,1,0:T(8,128)S(1)} %pad_maximum_fusion.p0), channel_id=1, source_target_pairs={{0,48},{8,248},{16,32},{24,232},{32,16},{40,216},{48,0},{56,200},{... | collective-permute-start | bytes 884744 | tf_op jit(solution)/shard_map/ppermute | solution.py:647
  20.7 14.7 %collective-permute-start.4 = (f32[4,144,128]{2,1,0:T(8,128)S(1)}, f32[4,144,128]{2,1,0:T(8,128)S(1)}, u32[]{:S(2)}, u32[]{:S(2)}) collective-permute-start(f32[4,144,128]{2,1,0:T(8,128)S(1)} %pad_maximum_fusion.p0), channel_id=1, source_target_pairs={{0,32},{8,56},{16,48},{24,40},{32,0},{40,24},{48,16},{56,8},{64,96... | collective-permute-start | bytes 884744 | tf_op jit(solution)/shard_map/ppermute | solution.py:647
  20.7 14.8 %collective-permute-start.3 = (f32[4,144,128]{2,1,0:T(8,128)S(1)}, f32[4,144,128]{2,1,0:T(8,128)S(1)}, u32[]{:S(2)}, u32[]{:S(2)}) collective-permute-start(f32[4,144,128]{2,1,0:T(8,128)S(1)} %pad_maximum_fusion.p0), channel_id=1, source_target_pairs={{0,16},{8,200},{16,0},{24,216},{32,48},{40,232},{48,32},{56,248},{... | collective-permute-start | bytes 884744 | tf_op jit(solution)/shard_map/ppermute | solution.py:647
  21.1 14.9 %collective-permute-start.6 = (f32[4,144,128]{2,1,0:T(8,128)S(1)}, f32[4,144,128]{2,1,0:T(8,128)S(1)}, u32[]{:S(2)}, u32[]{:S(2)}) collective-permute-start(f32[4,144,128]{2,1,0:T(8,128)S(1)} %pad_maximum_fusion.p0), channel_id=1, source_target_pairs={{0,8},{8,0},{16,24},{24,16},{32,40},{40,32},{48,56},{56,48},{64,72... | collective-permute-start | bytes 884744 | tf_op jit(solution)/shard_map/ppermute | solution.py:643
  30.7 6.0 %collective-permute-start.9 = (f32[4,144,128]{2,1,0:T(8,128)S(1)}, f32[4,144,128]{2,1,0:T(8,128)S(1)}, u32[]{:S(2)}, u32[]{:S(2)}) collective-permute-start(f32[4,144,128]{2,1,0:T(8,128)S(1)} %collective-permute-done.5.p3), channel_id=1, source_target_pairs={{0,8},{8,0},{16,24},{24,16},{32,40},{40,32},{48,56},{56,48},{64,72... | collective-permute-start | bytes 884744 | tf_op jit(solution)/shard_map/ppermute | solution.py:643
  35.4 1.6 %collective-permute-start.8 = (f32[4,144,128]{2,1,0:T(8,128)S(1)}, f32[4,144,128]{2,1,0:T(8,128)S(1)}, u32[]{:S(2)}, u32[]{:S(2)}) collective-permute-start(f32[4,144,128]{2,1,0:T(8,128)S(1)} %collective-permute-done.4.p2), channel_id=1, source_target_pairs={{0,8},{8,0},{16,24},{24,16},{32,40},{40,32},{48,56},{56,48},{64,72... | collective-permute-start | bytes 884744 | tf_op jit(solution)/shard_map/ppermute | solution.py:643
  35.4 2.0 %collective-permute-start.7 = (f32[4,144,128]{2,1,0:T(8,128)S(1)}, f32[4,144,128]{2,1,0:T(8,128)S(1)}, u32[]{:S(2)}, u32[]{:S(2)}) collective-permute-start(f32[4,144,128]{2,1,0:T(8,128)S(1)} %collective-permute-done.3.p1), channel_id=1, source_target_pairs={{0,8},{8,0},{16,24},{24,16},{32,40},{40,32},{48,56},{56,48},{64,72... | collective-permute-start | bytes 884744 | tf_op jit(solution)/shard_map/ppermute | solution.py:643
  36.6 0.8 copy-start.6
  37.1 0.7 copy-start.7
  44.1 13.9 %all-to-all-start = ((f32[8,144,128]{2,1,0:T(8,128)}), f32[8,144,128]{2,1,0:T(8,128)S(1)}, u32[]{:S(2)}, u32[]{:S(2)}) async-start(f32[8,144,128]{2,1,0:T(8,128)} %bitcast.27), calls=%async_computation | async-start | bytes 1179648 | tf_op jit(solution)/shard_map/all_to_all | solution.py:672
  53.2 17.7 %copy-start.2 = (f32[32,8,128]{2,1,0:T(8,128)S(1)}, f32[32,8,128]{2,1,0:T(8,128)}, u32[]{:S(2)}) copy-start(f32[32,8,128]{2,1,0:T(8,128)} %get-tuple-element.37.tail_ref) | copy-start | bytes 393220
  70.9 8.6 %copy-start = (f32[8,112,128]{2,1,0:T(8,128)}, f32[8,112,128]{2,1,0:T(8,128)S(1)}, u32[]{:S(2)}) copy-start(f32[8,112,128]{2,1,0:T(8,128)S(1)} %all_to_all.15) | copy-start | bytes 1376260
  71.7 26.2 %all-to-all-start.2 = ((f32[32,32,128]{2,1,0:T(8,128)}), f32[32,32,128]{2,1,0:T(8,128)S(1)}, u32[]{:S(2)}, u32[]{:S(2)}) async-start(f32[32,32,128]{2,1,0:T(8,128)} %get-tuple-element.45), calls=%async_computation.2 | async-start | bytes 1048576 | tf_op jit(solution)/shard_map/all_to_all | solution.py:677
  85.5 4.0 %collective-permute-start.12 = (f32[8,128]{1,0:T(8,128)S(1)}, f32[8,128]{1,0:T(8,128)S(1)}, u32[]{:S(2)}, u32[]{:S(2)}) collective-permute-start(f32[8,128]{1,0:T(8,128)S(1)} %get-tuple-element.43), channel_id=1, source_target_pairs={{0,6},{1,7},{2,4},{3,5},{4,2},{5,3},{6,0},{7,1},{8,14},{9,15},{10,... | collective-permute-start | bytes 12296 | tf_op jit(solution)/shard_map/ppermute | solution.py:643
  86.2 4.3 %collective-permute-start.11 = (f32[8,128]{1,0:T(8,128)S(1)}, f32[8,128]{1,0:T(8,128)S(1)}, u32[]{:S(2)}, u32[]{:S(2)}) collective-permute-start(f32[8,128]{1,0:T(8,128)S(1)} %get-tuple-element.43), channel_id=1, source_target_pairs={{0,4},{1,5},{2,6},{3,7},{4,0},{5,1},{6,2},{7,3},{8,12},{9,13},{10,... | collective-permute-start | bytes 12296 | tf_op jit(solution)/shard_map/ppermute | solution.py:643
  87.4 3.1 %collective-permute-start.10 = (f32[8,128]{1,0:T(8,128)S(1)}, f32[8,128]{1,0:T(8,128)S(1)}, u32[]{:S(2)}, u32[]{:S(2)}) collective-permute-start(f32[8,128]{1,0:T(8,128)S(1)} %get-tuple-element.43), channel_id=1, source_target_pairs={{0,2},{1,3},{2,0},{3,1},{4,6},{5,7},{6,4},{7,5},{8,10},{9,11},{10,... | collective-permute-start | bytes 12296 | tf_op jit(solution)/shard_map/ppermute | solution.py:643
  90.4 3.1 %collective-permute-start.13 = (f32[8,128]{1,0:T(8,128)S(1)}, f32[8,128]{1,0:T(8,128)S(1)}, u32[]{:S(2)}, u32[]{:S(2)}) collective-permute-start(f32[8,128]{1,0:T(8,128)S(1)} %add_add_fusion.n0), channel_id=1, source_target_pairs={{0,1},{1,0},{2,3},{3,2},{4,5},{5,4},{6,7},{7,6},{8,9},{9,8},{10,11... | collective-permute-start | bytes 12296 | tf_op jit(solution)/shard_map/ppermute | solution.py:643
